TPU v7x, 32 devices: a whole 2x2x4 slice. The times are simulated.
32 devices in a mesh: seq: 4 (over z), dp: 8 (over y, x, core).
Axes of the slice: x: 2, y: 2, z: 4, core: 2. Of those that a mesh axis runs over, the one named last changes fastest.
Arguments:
- layer_in: bfloat16 [2, 8, 1024, 768], P(None, 'dp', 'seq'), may hold values from -6 to 6
- cotangent: bfloat16 [2, 8, 1024, 768], P(None, 'dp', 'seq'), may hold values from -6 to 6
- valid_len: int32 [2, 8], P(None, 'dp'), may hold values from 512 to 1024, as said below
- sep_pos: int32 [2, 8], P(None, 'dp'), may hold values from 128 to 768, as said below
- w_query: bfloat16 [768, 384], P(('seq', 'dp')), may hold values from -0.21875 to 0.21875
- w_key: bfloat16 [768, 384], P(('seq', 'dp')), may hold values from -0.21875 to 0.21875
- w_value: bfloat16 [768, 384], P(('seq', 'dp')), may hold values from -0.21875 to 0.21875
- w_depth: bfloat16 [9, 768], P(None, ('seq', 'dp')), may hold values from -2 to 2
- w_point: bfloat16 [768, 384], P(('seq', 'dp')), may hold values from -0.21875 to 0.21875
- w_kernel: bfloat16 [20736], P(('seq', 'dp')), may hold values from -0.3125 to 0.3125
- w_convout: bfloat16 [768, 384], P(('seq', 'dp')), may hold values from -0.21875 to 0.21875
- w_output: bfloat16 [768, 768], P(('seq', 'dp')), may hold values from -0.875 to 0.875
- gain_attn: bfloat16 [768], P(('seq', 'dp')), may hold values from 0.3984375 to 1.59375
- shift_attn: bfloat16 [768], P(('seq', 'dp')), may hold values from -0.3984375 to 0.3984375
- w_up: bfloat16 [2, 384, 1536], P(None, None, ('seq', 'dp')), may hold values from -0.3125 to 0.3125
- w_down: bfloat16 [2, 1536, 384], P(None, ('seq', 'dp')), may hold values from -0.15625 to 0.15625
- gain_out: bfloat16 [768], P(('seq', 'dp')), may hold values from 0.3984375 to 1.59375
- shift_out: bfloat16 [768], P(('seq', 'dp')), may hold values from -0.3984375 to 0.3984375
Outputs:
- layer_out: bfloat16 [2, 8, 1024, 768], P(None, 'dp', 'seq')
- x_grad: float32 [2, 8, 1024, 768], P(None, 'dp', 'seq')
- grad_query: float32 [768, 384], P(('seq', 'dp'))
- grad_key: float32 [768, 384], P(('seq', 'dp'))
- grad_value: float32 [768, 384], P(('seq', 'dp'))
- grad_depth: float32 [9, 768], P(None, ('seq', 'dp'))
- grad_point: float32 [768, 384], P(('seq', 'dp'))
- grad_kernel: float32 [20736], P(('seq', 'dp'))
- grad_convout: float32 [768, 384], P(('seq', 'dp'))
- grad_output: float32 [768, 768], P(('seq', 'dp'))
- grad_gain_attn: float32 [768], P(('seq', 'dp'))
- grad_shift_attn: float32 [768], P(('seq', 'dp'))
- grad_up: float32 [2, 384, 1536], P(None, None, ('seq', 'dp'))
- grad_down: float32 [2, 1536, 384], P(None, ('seq', 'dp'))
- grad_gain_out: float32 [768], P(('seq', 'dp'))
- grad_shift_out: float32 [768], P(('seq', 'dp'))
Inputs may be any that keep to these rules, and one draw needn't show every extreme that they name: `valid_len`: for every index of dp, one of its rows over the 2 micro-batches, which one drawn from the seed, has all 1024 tokens. `sep_pos`: below the row's valid_len and at least valid_len // 4 (a quarter, rounded down).
All inputs are finite; a program needn't handle non-finite values.
Results may differ from a plain program's by a relative error of at most 0.015.
Values may be sent and summed in bfloat16 or wider, within the bound.
No kernel may reach another device: no remote copies, remote signals or barrier semaphores. Data moves between devices by JAX's collectives and lax.ppermute only.
A program may use at most 192 MiB of HBM per device.

v0:
```python
import jax
import jax.numpy as jnp
from jax import lax
from jax.sharding import PartitionSpec as P

HEADS = 6
HEAD_DIM = 64
KERNEL = 9
GROUPS = 2
LEN = 1024


inv_root_two = 0.7071067811865476
inv_root_tau = 0.3989422804014327


def extended(block, sides, width):
    for axis, dim in sides:
        count = lax.axis_size(axis)
        forward = [(i, i + 1) for i in range(count - 1)]
        backward = [(target, source) for source, target in forward]
        low = lax.ppermute(
            lax.slice_in_dim(block, block.shape[dim] - width, None, axis=dim), axis, forward
        )
        high = lax.ppermute(lax.slice_in_dim(block, 0, width, axis=dim), axis, backward)
        block = jnp.concatenate([low, block, high], axis=dim)
    return block


def erf_gelu(pre_act):
    return 0.5 * pre_act * (1.0 + lax.erf(pre_act * inv_root_two))


def gelu_slope(pre_act):
    return (
        0.5 * (1.0 + lax.erf(pre_act * inv_root_two))
        + pre_act * jnp.exp(-0.5 * pre_act * pre_act) * inv_root_tau
    )


def softmax_last(scores):
    row_peak = jnp.max(scores, -1, keepdims=True)
    exponent = jnp.exp(scores - row_peak)
    return exponent / jnp.sum(exponent, -1, keepdims=True)


def norm_forward(signal, gain_vec, shift_vec):
    centred = signal - jnp.mean(signal, -1, keepdims=True)
    inv_scale = lax.rsqrt(jnp.mean(centred * centred, -1, keepdims=True) + 1e-06)
    normed = centred * inv_scale
    return (normed * gain_vec + shift_vec, normed, inv_scale)


def norm_backward(grad_out, normed, inv_scale, gain_vec):
    d_gain = jnp.sum(grad_out * normed, axis=(0, 1))
    d_shift = jnp.sum(grad_out, axis=(0, 1))
    d_normed = grad_out * gain_vec
    d_signal = inv_scale * (
        d_normed
        - jnp.mean(d_normed, -1, keepdims=True)
        - normed * jnp.mean(d_normed * normed, -1, keepdims=True)
    )
    return (d_signal, d_gain, d_shift)


def run_batch(gathered, tokens, grad_rows, valid_rows, sep_rows, first_pos):
    (
        query_weight,
        key_weight,
        value_weight,
        depth_kernel,
        point_weight,
        kernel_flat,
        conv_weight,
        out_weight,
        attn_gain,
        attn_shift,
        up_weight,
        down_weight,
        out_gain,
        out_shift,
    ) = gathered
    row_count, local_len, width = tokens.shape
    half_span = (KERNEL - 1) // 2
    heads_width = HEADS * HEAD_DIM
    group_width = width // GROUPS
    score_scale = HEAD_DIM ** (-0.5)
    kernel_weight = kernel_flat.reshape(heads_width, HEADS * KERNEL)
    tokens_wide = tokens.astype(jnp.float32)
    query_low = jnp.dot(tokens, query_weight, preferred_element_type=jnp.float32).astype(
        jnp.bfloat16
    )
    keys_low = jnp.dot(tokens, key_weight, preferred_element_type=jnp.float32).astype(jnp.bfloat16)
    values_low = jnp.dot(tokens, value_weight, preferred_element_type=jnp.float32).astype(
        jnp.bfloat16
    )
    keys_all, values_all = (
        lax.all_gather(keys_low, "seq", axis=1, tiled=True),
        lax.all_gather(values_low, "seq", axis=1, tiled=True),
    )
    full_len = keys_all.shape[1]
    query_heads = query_low.reshape(row_count, local_len, HEADS, HEAD_DIM)
    keys_heads = keys_all.reshape(row_count, full_len, HEADS, HEAD_DIM)
    values_heads = values_all.reshape(row_count, full_len, HEADS, HEAD_DIM)
    scores = (
        jnp.einsum("rqhe,rkhe->rhqk", query_heads, keys_heads, preferred_element_type=jnp.float32)
        * score_scale
    )
    key_live = jnp.arange(full_len)[None, :] < valid_rows[:, None]
    scores = jnp.where(key_live[:, None, None, :], scores, -1e30)
    probs = softmax_last(scores)
    probs_low = probs.astype(jnp.bfloat16)
    attended = jnp.einsum(
        "rhqk,rkhe->rqhe", probs_low, values_heads, preferred_element_type=jnp.float32
    ).reshape(row_count, local_len, heads_width)
    padded = extended(tokens, (("seq", 1),), half_span)
    padded_wide = padded.astype(jnp.float32)
    depth_wide = depth_kernel.astype(jnp.float32)
    depth_out = jnp.zeros((row_count, local_len, width), jnp.float32)
    for tap_index in range(KERNEL):
        depth_out = (
            depth_out + depth_wide[tap_index] * padded_wide[:, tap_index : tap_index + local_len]
        )
    depth_low = depth_out.astype(jnp.bfloat16)
    key_conv = jnp.dot(depth_low, point_weight, preferred_element_type=jnp.float32)
    query_wide = query_low.astype(jnp.float32)
    conv_attn_low = (key_conv * query_wide).astype(jnp.bfloat16)
    kernel_logits = jnp.dot(conv_attn_low, kernel_weight, preferred_element_type=jnp.float32)
    kernel_probs = softmax_last(kernel_logits.reshape(row_count, local_len, HEADS, KERNEL))
    conv_values = jnp.dot(padded, conv_weight, preferred_element_type=jnp.float32)
    positions = first_pos - half_span + jnp.arange(local_len + 2 * half_span)
    inside = (positions >= 0) & (positions < LEN)
    segment = jnp.where(
        positions[None, :] < sep_rows[:, None],
        0,
        jnp.where(positions[None, :] < valid_rows[:, None], 1, 2),
    )
    segment = jnp.where(inside[None, :], segment, -1)
    own_segment = segment[:, half_span : half_span + local_len]
    tap_weights = []
    same_masks = []
    conv_heads = jnp.zeros((row_count, local_len, HEADS, HEAD_DIM), jnp.float32)
    for tap_index in range(KERNEL):
        same_seg = (segment[:, tap_index : tap_index + local_len] == own_segment).astype(
            jnp.float32
        )
        tap_weight = kernel_probs[..., tap_index] * same_seg[:, :, None]
        window = conv_values[:, tap_index : tap_index + local_len].reshape(
            row_count, local_len, HEADS, HEAD_DIM
        )
        conv_heads = conv_heads + tap_weight[..., None] * window
        tap_weights.append(tap_weight)
        same_masks.append(same_seg)
    context_low = jnp.concatenate(
        [attended, conv_heads.reshape(row_count, local_len, heads_width)], -1
    ).astype(jnp.bfloat16)
    branch = jnp.dot(context_low, out_weight, preferred_element_type=jnp.float32)
    attn_gain_wide = attn_gain.astype(jnp.float32)
    out_gain_wide = out_gain.astype(jnp.float32)
    attn_out, normed_one, inv_one = norm_forward(
        branch + tokens_wide, attn_gain_wide, attn_shift.astype(jnp.float32)
    )
    grouped = attn_out.astype(jnp.bfloat16).reshape(row_count, local_len, GROUPS, group_width)
    pre_act = jnp.einsum("rsgd,gdf->rsgf", grouped, up_weight, preferred_element_type=jnp.float32)
    act_low = erf_gelu(pre_act).astype(jnp.bfloat16)
    down_out = jnp.einsum(
        "rsgf,gfd->rsgd", act_low, down_weight, preferred_element_type=jnp.float32
    ).reshape(row_count, local_len, width)
    final_out, normed_two, inv_two = norm_forward(
        down_out + attn_out, out_gain_wide, out_shift.astype(jnp.float32)
    )
    grad_wide = grad_rows.astype(jnp.float32)
    d_second, d_out_gain, d_out_shift = norm_backward(grad_wide, normed_two, inv_two, out_gain_wide)
    d_down_low = d_second.astype(jnp.bfloat16).reshape(row_count, local_len, GROUPS, group_width)
    d_down_w = jnp.einsum("rsgf,rsgd->gfd", act_low, d_down_low, preferred_element_type=jnp.float32)
    d_act = jnp.einsum(
        "rsgd,gfd->rsgf", d_down_low, down_weight, preferred_element_type=jnp.float32
    )
    d_pre_low = (d_act * gelu_slope(pre_act)).astype(jnp.bfloat16)
    d_up_w = jnp.einsum("rsgd,rsgf->gdf", grouped, d_pre_low, preferred_element_type=jnp.float32)
    d_attn_out = d_second + jnp.einsum(
        "rsgf,gdf->rsgd", d_pre_low, up_weight, preferred_element_type=jnp.float32
    ).reshape(row_count, local_len, width)
    d_first, d_attn_gain, d_attn_shift = norm_backward(
        d_attn_out, normed_one, inv_one, attn_gain_wide
    )
    d_branch_low = d_first.astype(jnp.bfloat16)
    d_out_w = jnp.einsum(
        "rsa,rsd->ad", context_low, d_branch_low, preferred_element_type=jnp.float32
    )
    d_context_low = jnp.einsum(
        "rsd,ad->rsa", d_branch_low, out_weight, preferred_element_type=jnp.float32
    ).astype(jnp.bfloat16)
    d_attended = d_context_low[..., :heads_width].reshape(row_count, local_len, HEADS, HEAD_DIM)
    d_conv_heads = (
        d_context_low[..., heads_width:]
        .astype(jnp.float32)
        .reshape(row_count, local_len, HEADS, HEAD_DIM)
    )
    d_probs = jnp.einsum(
        "rqhe,rkhe->rhqk", d_attended, values_heads, preferred_element_type=jnp.float32
    )
    d_values_part = jnp.einsum(
        "rhqk,rqhe->rkhe", probs_low, d_attended, preferred_element_type=jnp.float32
    )
    row_dot = jnp.sum(probs * d_probs, -1, keepdims=True)
    d_scores_low = (probs * (d_probs - row_dot)).astype(jnp.bfloat16)
    d_query_attn = (
        jnp.einsum("rhqk,rkhe->rqhe", d_scores_low, keys_heads, preferred_element_type=jnp.float32)
        * score_scale
    )
    d_keys_part = (
        jnp.einsum("rhqk,rqhe->rkhe", d_scores_low, query_heads, preferred_element_type=jnp.float32)
        * score_scale
    )
    d_keys, d_values = (
        lax.psum_scatter(
            d_keys_part.reshape(row_count, full_len, heads_width).astype(jnp.bfloat16),
            "seq",
            scatter_dimension=1,
            tiled=True,
        ).astype(jnp.float32),
        lax.psum_scatter(
            d_values_part.reshape(row_count, full_len, heads_width).astype(jnp.bfloat16),
            "seq",
            scatter_dimension=1,
            tiled=True,
        ).astype(jnp.float32),
    )
    d_keys_low = d_keys.astype(jnp.bfloat16)
    d_values_low = d_values.astype(jnp.bfloat16)
    d_values_pad = jnp.zeros((row_count, local_len + 2 * half_span, heads_width), jnp.float32)
    d_tap_list = []
    for tap_index in range(KERNEL):
        window = conv_values[:, tap_index : tap_index + local_len].reshape(
            row_count, local_len, HEADS, HEAD_DIM
        )
        d_tap_list.append(jnp.sum(d_conv_heads * window, -1) * same_masks[tap_index][:, :, None])
        spread_back = (tap_weights[tap_index][..., None] * d_conv_heads).reshape(
            row_count, local_len, heads_width
        )
        d_values_pad = d_values_pad.at[:, tap_index : tap_index + local_len].add(spread_back)
    d_kernel_probs = jnp.stack(d_tap_list, -1)
    d_logits_low = kernel_probs * (
        d_kernel_probs - jnp.sum(kernel_probs * d_kernel_probs, -1, keepdims=True)
    )
    d_logits_low = d_logits_low.astype(jnp.bfloat16).reshape(row_count, local_len, HEADS * KERNEL)
    d_kernel_w = jnp.einsum(
        "rsa,rsk->ak", conv_attn_low, d_logits_low, preferred_element_type=jnp.float32
    ).reshape(-1)
    d_conv_attn = jnp.einsum(
        "rsk,ak->rsa", d_logits_low, kernel_weight, preferred_element_type=jnp.float32
    )
    d_key_conv_low = (d_conv_attn * query_wide).astype(jnp.bfloat16)
    d_point_w = jnp.einsum(
        "rsd,rsa->da", depth_low, d_key_conv_low, preferred_element_type=jnp.float32
    )
    d_depth = jnp.einsum(
        "rsa,da->rsd", d_key_conv_low, point_weight, preferred_element_type=jnp.float32
    )
    d_input_pad = jnp.zeros((row_count, local_len + 2 * half_span, width), jnp.float32)
    d_depth_rows = []
    for tap_index in range(KERNEL):
        d_depth_rows.append(
            jnp.sum(d_depth * padded_wide[:, tap_index : tap_index + local_len], axis=(0, 1))
        )
        d_input_pad = d_input_pad.at[:, tap_index : tap_index + local_len].add(
            depth_wide[tap_index] * d_depth
        )
    d_depth_w = jnp.stack(d_depth_rows, 0)
    left_rim = jnp.concatenate([d_values_pad[:, :half_span], d_input_pad[:, :half_span]], -1)
    right_rim = jnp.concatenate(
        [d_values_pad[:, local_len + half_span :], d_input_pad[:, local_len + half_span :]], -1
    )
    rim_rows = jnp.concatenate([left_rim, right_rim], 1)
    arrived = extended(rim_rows.astype(jnp.bfloat16), (("seq", 1),), half_span).astype(
        rim_rows.dtype
    )
    incoming = jnp.pad(
        arrived[:, :half_span], ((0, 0), (0, local_len - half_span), (0, 0))
    ) + jnp.pad(arrived[:, 3 * half_span :], ((0, 0), (local_len - half_span, 0), (0, 0)))
    d_conv_values_low = (
        d_values_pad[:, half_span : half_span + local_len] + incoming[..., :heads_width]
    ).astype(jnp.bfloat16)
    d_query_low = (
        d_query_attn.reshape(row_count, local_len, heads_width) + d_conv_attn * key_conv
    ).astype(jnp.bfloat16)
    d_query_w = jnp.einsum("rsd,rsa->da", tokens, d_query_low, preferred_element_type=jnp.float32)
    d_key_w = jnp.einsum("rsd,rsa->da", tokens, d_keys_low, preferred_element_type=jnp.float32)
    d_value_w = jnp.einsum("rsd,rsa->da", tokens, d_values_low, preferred_element_type=jnp.float32)
    d_conv_w = jnp.einsum(
        "rsd,rsa->da", tokens, d_conv_values_low, preferred_element_type=jnp.float32
    )
    input_grad = (
        d_first
        + d_input_pad[:, half_span : half_span + local_len]
        + incoming[..., heads_width:]
        + jnp.einsum("rsa,da->rsd", d_query_low, query_weight, preferred_element_type=jnp.float32)
        + jnp.einsum("rsa,da->rsd", d_keys_low, key_weight, preferred_element_type=jnp.float32)
        + jnp.einsum("rsa,da->rsd", d_values_low, value_weight, preferred_element_type=jnp.float32)
        + jnp.einsum(
            "rsa,da->rsd", d_conv_values_low, conv_weight, preferred_element_type=jnp.float32
        )
    )
    grads = (
        d_query_w,
        d_key_w,
        d_value_w,
        d_depth_w,
        d_point_w,
        d_kernel_w,
        d_conv_w,
        d_out_w,
        d_attn_gain,
        d_attn_shift,
        d_up_w,
        d_down_w,
        d_out_gain,
        d_out_shift,
    )
    return (final_out.astype(jnp.bfloat16), input_grad, grads)


def local(
    layer_in,
    cotangent,
    valid_len,
    sep_pos,
    w_query,
    w_key,
    w_value,
    w_depth,
    w_point,
    w_kernel,
    w_convout,
    w_output,
    gain_attn,
    shift_attn,
    w_up,
    w_down,
    gain_out,
    shift_out,
):
    first_pos = lax.axis_index("seq") * layer_in.shape[2]
    outputs = []
    input_grads = []
    totals = None
    for micro_step in range(layer_in.shape[0]):
        gathered = (
            lax.all_gather(w_query, ("seq", "dp"), axis=0, tiled=True),
            lax.all_gather(w_key, ("seq", "dp"), axis=0, tiled=True),
            lax.all_gather(w_value, ("seq", "dp"), axis=0, tiled=True),
            lax.all_gather(w_depth, ("seq", "dp"), axis=1, tiled=True),
            lax.all_gather(w_point, ("seq", "dp"), axis=0, tiled=True),
            lax.all_gather(w_kernel, ("seq", "dp"), axis=0, tiled=True),
            lax.all_gather(w_convout, ("seq", "dp"), axis=0, tiled=True),
            lax.all_gather(w_output, ("seq", "dp"), axis=0, tiled=True),
            lax.all_gather(gain_attn, ("seq", "dp"), axis=0, tiled=True),
            lax.all_gather(shift_attn, ("seq", "dp"), axis=0, tiled=True),
            lax.all_gather(w_up, ("seq", "dp"), axis=2, tiled=True),
            lax.all_gather(w_down, ("seq", "dp"), axis=1, tiled=True),
            lax.all_gather(gain_out, ("seq", "dp"), axis=0, tiled=True),
            lax.all_gather(shift_out, ("seq", "dp"), axis=0, tiled=True),
        )
        layer_rows, grad_input, grads = run_batch(
            gathered,
            layer_in[micro_step],
            cotangent[micro_step],
            valid_len[micro_step],
            sep_pos[micro_step],
            first_pos,
        )
        outputs.append(layer_rows)
        input_grads.append(grad_input)
        partial_sum = (
            lax.psum_scatter(grads[0], ("seq", "dp"), scatter_dimension=0, tiled=True),
            lax.psum_scatter(grads[1], ("seq", "dp"), scatter_dimension=0, tiled=True),
            lax.psum_scatter(grads[2], ("seq", "dp"), scatter_dimension=0, tiled=True),
            lax.psum_scatter(grads[3], ("seq", "dp"), scatter_dimension=1, tiled=True),
            lax.psum_scatter(grads[4], ("seq", "dp"), scatter_dimension=0, tiled=True),
            lax.psum_scatter(grads[5], ("seq", "dp"), scatter_dimension=0, tiled=True),
            lax.psum_scatter(grads[6], ("seq", "dp"), scatter_dimension=0, tiled=True),
            lax.psum_scatter(grads[7], ("seq", "dp"), scatter_dimension=0, tiled=True),
            lax.psum_scatter(grads[8], ("seq", "dp"), scatter_dimension=0, tiled=True),
            lax.psum_scatter(grads[9], ("seq", "dp"), scatter_dimension=0, tiled=True),
            lax.psum_scatter(grads[10], ("seq", "dp"), scatter_dimension=2, tiled=True),
            lax.psum_scatter(grads[11], ("seq", "dp"), scatter_dimension=1, tiled=True),
            lax.psum_scatter(grads[12], ("seq", "dp"), scatter_dimension=0, tiled=True),
            lax.psum_scatter(grads[13], ("seq", "dp"), scatter_dimension=0, tiled=True),
        )
        totals = partial_sum if totals is None else jax.tree.map(jnp.add, totals, partial_sum)
    (
        grad_query,
        grad_key,
        grad_value,
        grad_depth,
        grad_point,
        grad_kernel,
        grad_convout,
        grad_output,
        grad_gain_attn,
        grad_shift_attn,
        grad_up,
        grad_down,
        grad_gain_out,
        grad_shift_out,
    ) = totals
    return (
        jnp.stack(outputs),
        jnp.stack(input_grads),
        grad_query,
        grad_key,
        grad_value,
        grad_depth,
        grad_point,
        grad_kernel,
        grad_convout,
        grad_output,
        grad_gain_attn,
        grad_shift_attn,
        grad_up,
        grad_down,
        grad_gain_out,
        grad_shift_out,
    )


def solution(mesh):
    in_specs = (
        P(None, "dp", "seq", None),
        P(None, "dp", "seq", None),
        P(None, "dp"),
        P(None, "dp"),
        P(("seq", "dp"), None),
        P(("seq", "dp"), None),
        P(("seq", "dp"), None),
        P(None, ("seq", "dp")),
        P(("seq", "dp"), None),
        P(("seq", "dp")),
        P(("seq", "dp"), None),
        P(("seq", "dp"), None),
        P(("seq", "dp")),
        P(("seq", "dp")),
        P(None, None, ("seq", "dp")),
        P(None, ("seq", "dp"), None),
        P(("seq", "dp")),
        P(("seq", "dp")),
    )
    out_specs = (
        P(None, "dp", "seq", None),
        P(None, "dp", "seq", None),
        P(("seq", "dp"), None),
        P(("seq", "dp"), None),
        P(("seq", "dp"), None),
        P(None, ("seq", "dp")),
        P(("seq", "dp"), None),
        P(("seq", "dp")),
        P(("seq", "dp"), None),
        P(("seq", "dp"), None),
        P(("seq", "dp")),
        P(("seq", "dp")),
        P(None, None, ("seq", "dp")),
        P(None, ("seq", "dp"), None),
        P(("seq", "dp")),
        P(("seq", "dp")),
    )
    return jax.shard_map(local, mesh=mesh, in_specs=in_specs, out_specs=out_specs, check_vma=False)
```

profile of v0, /device:TPU:0, one launch (start us, length us, event | category | flops | bytes accessed | tf_op | source)
XLA Modules:
  0.0 1407.6 jit_solution(14693471208364770289)
XLA Ops:
  10.6 5.5 collective-permute-start.2
  18.0 5.1 collective-permute-start
  24.6 45.0 %all_gather.70 = bf16[768,384]{1,0:T(8,128)(2,1)S(1)} all-gather(bf16[24,384]{1,0:T(8,128)(2,1)} %param.94), channel_id=1, replica_groups=mesh['seq'=4,'dp'=8] {'seq','dp'}, dimensions={0}, use_global_device_ids=true | all-gather | bytes 608256 | tf_op jit(solution)/shard_map/all_gather | solution.py:350
  71.7 38.6 %all_gather.71 = bf16[768,384]{1,0:T(8,128)(2,1)S(1)} all-gather(bf16[24,384]{1,0:T(8,128)(2,1)S(1)} %copy-done.164), channel_id=1, replica_groups=mesh['seq'=4,'dp'=8] {'seq','dp'}, dimensions={0}, use_global_device_ids=true | all-gather | bytes 608256 | tf_op jit(solution)/shard_map/all_gather | solution.py:351
  112.3 40.2 %all_gather.68 = bf16[768,384]{1,0:T(8,128)(2,1)S(1)} all-gather(bf16[24,384]{1,0:T(8,128)(2,1)S(1)} %copy-done.165), channel_id=1, replica_groups=mesh['seq'=4,'dp'=8] {'seq','dp'}, dimensions={0}, use_global_device_ids=true | all-gather | bytes 608256 | tf_op jit(solution)/shard_map/all_gather | solution.py:352
  162.5 38.6 %all-reduce.26 = (bf16[20736]{0:T(1024)(128)(2,1)S(1)}, bf16[768]{0:T(1024)(128)(2,1)}, bf16[768]{0:T(1024)(128)(2,1)}, bf16[768]{0:T(1024)(128)(2,1)}, bf16[768]{0:T(1024)(128)(2,1)S(1)}) all-reduce(bf16[20736]{0:T(1024)(128)(2,1)S(1)} %dynamic-update-slice.108, ...), channel_id=1, replica_groups=mesh['seq'=4,'dp'=8] {'seq','dp'}, use_global_device_ids=true, to_apply=%add.8 | all-reduce | flops 23808 | bytes 95232
  201.1 40.0 %all-gather.4 = bf16[32,24,9]{1,2,0:T(8,128)(2,1)S(1)} all-gather(bf16[1,24,9]{1,2,0:T(8,128)(2,1)S(1)} %bitcast.963), channel_id=1, replica_groups=mesh['seq'=4,'dp'=8] {'seq','dp'}, dimensions={0}, use_global_device_ids=true | all-gather | bytes 14256 | tf_op jit(solution)/shard_map/all_gather | solution.py:353
  241.9 38.4 %all_gather.74 = bf16[768,384]{1,0:T(8,128)(2,1)S(1)} all-gather(bf16[24,384]{1,0:T(8,128)(2,1)S(1)} %copy-done.166), channel_id=1, replica_groups=mesh['seq'=4,'dp'=8] {'seq','dp'}, dimensions={0}, use_global_device_ids=true | all-gather | bytes 608256 | tf_op jit(solution)/shard_map/all_gather | solution.py:354
  280.3 42.5 %all_gather.76 = bf16[768,384]{1,0:T(8,128)(2,1)} all-gather(bf16[24,384]{1,0:T(8,128)(2,1)S(1)} %copy-done.167), channel_id=1, replica_groups=mesh['seq'=4,'dp'=8] {'seq','dp'}, dimensions={0}, use_global_device_ids=true | all-gather | bytes 608256 | tf_op jit(solution)/shard_map/all_gather | solution.py:356
  322.8 17.7 %all-gather = bf16[1024,384]{1,0:T(8,128)(2,1)S(1)} all-gather(bf16[256,384]{1,0:T(8,128)(2,1)S(1)} %convolution_convert_fusion.7), channel_id=2, replica_groups=mesh['seq'=4,'dp'=8] {'seq'}, dimensions={0}, use_global_device_ids=true | all-gather | bytes 983040 | tf_op jit(solution)/shard_map/all_gather | solution.py:99
  341.7 18.1 %all-gather.2 = bf16[1024,384]{1,0:T(8,128)(2,1)S(1)} all-gather(bf16[256,384]{1,0:T(8,128)(2,1)S(1)} %convolution_convert_fusion.4), channel_id=4, replica_groups=mesh['seq'=4,'dp'=8] {'seq'}, dimensions={0}, use_global_device_ids=true | all-gather | bytes 983040 | tf_op jit(solution)/shard_map/all_gather | solution.py:99
  361.0 17.7 %all-gather.1 = bf16[1024,384]{1,0:T(8,128)(2,1)S(1)} all-gather(bf16[256,384]{1,0:T(8,128)(2,1)S(1)} %copy-done.127), channel_id=3, replica_groups=mesh['seq'=4,'dp'=8] {'seq'}, dimensions={0}, use_global_device_ids=true | all-gather | bytes 983040 | tf_op jit(solution)/shard_map/all_gather | solution.py:98
  379.8 16.8 %all-gather.3 = bf16[1024,384]{1,0:T(8,128)(2,1)S(1)} all-gather(bf16[256,384]{1,0:T(8,128)(2,1)S(1)} %convolution_convert_fusion.2), channel_id=5, replica_groups=mesh['seq'=4,'dp'=8] {'seq'}, dimensions={0}, use_global_device_ids=true | all-gather | bytes 983040 | tf_op jit(solution)/shard_map/all_gather | solution.py:98
  398.7 5.9 fusion.299
  404.6 5.0 fusion.59
  409.6 4.8 fusion.301
  414.4 4.2 fusion.56
  456.5 3.2 fusion.198
  471.8 3.2 convolution_bitcast_fusion.15
  509.5 4.6 fusion.38
  514.1 5.8 multiply_reduce_fusion.1
  591.1 4.4 multiply_reduce_fusion
  604.5 5.2 multiply_convert_fusion.1
  672.5 3.3 scatter-add.121
  675.8 3.2 scatter-add.151
  681.7 3.1 scatter-add.124
  684.8 3.1 scatter-add.154
  690.7 3.1 scatter-add.125
  693.9 3.1 scatter-add.155
  702.8 3.1 scatter-add.156
  711.8 3.1 scatter-add.159
  720.8 3.1 scatter-add.160
  728.9 3.1 scatter-add.131
  732.0 3.1 scatter-add.161
  737.3 3.6 multiply_convert_fusion.5
  753.3 3.2 collective-permute-start.6
  758.0 4.6 fusion.41
  765.0 3.6 multiply_convert_fusion.4
  777.1 15.6 %reduce-scatter.22.cloned.1.call-done = bf16[1,256,384]{1,2,0:T(8,128)(2,1)} async-done(((bf16[1,1024,384]{1,2,0:T(8,128)(2,1)}), bf16[1,256,384]{1,2,0:T(8,128)(2,1)}) %reduce-scatter.22.cloned.1.call-update) | async-done | bytes 196624 | tf_op jit(solution)/shard_map/reduce_scatter | solution.py:223
  795.4 22.1 %reduce-scatter.20.cloned.1.call-done = bf16[1,256,384]{1,2,0:T(8,128)(2,1)} async-done(((bf16[1,1024,384]{1,2,0:T(8,128)(2,1)}), bf16[1,256,384]{1,2,0:T(8,128)(2,1)}) %reduce-scatter.20.cloned.1.call-update) | async-done | bytes 196624 | tf_op jit(solution)/shard_map/reduce_scatter | solution.py:217
  830.7 3.2 convolution_add_fusion.1
  836.9 3.2 convolution_add_fusion
  841.9 39.4 %all-reduce.24 = (f32[9,768]{1,0:T(8,128)S(1)}, f32[768]{0:T(1024)S(1)}, f32[768]{0:T(1024)S(1)}, f32[768]{0:T(1024)S(1)}, f32[768]{0:T(1024)S(1)}) all-reduce(f32[9,768]{1,0:T(8,128)S(1)} %add.809, f32[768]{0:T(1024)S(1)} %add.814, f32[768]{0:T(1024)S(1)} %add.815, ...), channel_id=27, replica_groups=mesh['seq'=4,'dp'=8] {'seq','dp'}, use_global_device_ids=true, to_apply=%region_65.66.clone | all-reduce | flops 9984 | bytes 79872
  892.0 78.8 %all-reduce.29.cloned.1.call-done = (f32[768,384]{0,1:T(8,128)}, f32[768,384]{0,1:T(8,128)}, f32[768,384]{0,1:T(8,128)}, f32[20736]{0:T(1024)}, f32[768,384]{0,1:T(8,128)}) async-done(((f32[768,384]{0,1:T(8,128)}, f32[768,384]{0,1:T(8,128)}, f32[768,384]{0,1:T(8,128)}, f32[20736]{0:T(1024)}, f32[768,384]{0,1:T(8,128)}), (f32[768,384]{0,1:T(8,128)}, f32[768,384]{0,1:T(8,128)}, f32[768,384]{0,1:T(8,128)}, ...) | async-done | bytes 4801552
  979.6 92.1 %reduce-scatter.30.cloned.1.call-done = f32[24,384]{1,0:T(8,128)} async-done(((f32[768,384]{1,0:T(8,128)}), f32[24,384]{1,0:T(8,128)}) %reduce-scatter.30.cloned.1.call-update) | async-done | bytes 36880
  1071.7 103.9 %reduce-scatter.24.cloned.1.call-done = f32[24,768]{1,0:T(8,128)} async-done(((f32[768,768]{1,0:T(8,128)}), f32[24,768]{1,0:T(8,128)}) %reduce-scatter.24.cloned.1.call-update) | async-done | bytes 73744 | tf_op jit(solution)/shard_map/reduce_scatter | solution.py:383
  1175.5 113.0 %reduce-scatter.26.cloned.1.call-done = f32[2,384,48]{1,2,0:T(8,128)} async-done(((f32[2,384,1536]{1,2,0:T(8,128)}), f32[2,384,48]{1,2,0:T(8,128)}) %reduce-scatter.26.cloned.1.call-update) | async-done | bytes 147472 | tf_op jit(solution)/shard_map/reduce_scatter | solution.py:386
  1288.5 112.0 %reduce-scatter.28.cloned.1.call-done = f32[2,48,384]{2,1,0:T(8,128)} async-done(((f32[2,1536,384]{2,1,0:T(8,128)}), f32[2,48,384]{2,1,0:T(8,128)}) %reduce-scatter.28.cloned.1.call-update) | async-done | bytes 147472 | tf_op jit(solution)/shard_map/reduce_scatter | solution.py:387
  (919 shorter events, 346.1 us)
Async XLA Ops:
  7.2 64.0 %copy-start.13 = (bf16[2,1,256,768]{3,2,1,0:T(8,128)(2,1)S(1)}, bf16[2,1,256,768]{3,2,1,0:T(8,128)(2,1)}, u32[]{:S(2)}) copy-start(bf16[2,1,256,768]{3,2,1,0:T(8,128)(2,1)} %param.90) | copy-start | bytes 2359300
  7.2 64.4 %copy-start.164 = (bf16[24,384]{1,0:T(8,128)(2,1)S(1)}, bf16[24,384]{1,0:T(8,128)(2,1)}, u32[]{:S(2)}) copy-start(bf16[24,384]{1,0:T(8,128)(2,1)} %param.95) | copy-start | bytes 55300
  7.2 453.7 %all-gather.9.cloned.1.call-start = ((), (), s32[]{:S(2)}) async-start(), calls=%async_computation.8 | async-start | bytes 1216512 | tf_op jit(solution)/shard_map/all_gather | solution.py:357
  7.9 458.0 %all-gather.11.cloned.1.call-start = ((), (), s32[]{:S(2)}) async-start(), calls=%async_computation.9 | async-start | bytes 2433024 | tf_op jit(solution)/shard_map/all_gather | solution.py:360
  8.7 463.1 %all-gather.13.cloned.1.call-start = ((), (), s32[]{:S(2)}) async-start(), calls=%async_computation.10 | async-start | bytes 2433024 | tf_op jit(solution)/shard_map/all_gather | solution.py:361
  10.6 415.7 %collective-permute-start.2 = (bf16[1,4,768]{2,1,0:T(4,128)(2,1)}, bf16[1,4,768]{2,1,0:T(4,128)(2,1)}, u32[]{:S(2)}, u32[]{:S(2)}) collective-permute-start(bf16[1,4,768]{2,1,0:T(4,128)(2,1)} %get-tuple-element.616), channel_id=1, source_target_pairs={{0,8},{8,16},{16,24},{1,9},{9,17},{17,25},{2,10},{10,18},{18,26},{... | collective-permute-start | bytes 18440 | tf_op jit(solution)/shard_map/ppermute | solution.py:22
  16.1 410.2 %collective-permute-start.3 = (bf16[1,4,768]{2,1,0:T(4,128)(2,1)}, bf16[1,4,768]{2,1,0:T(4,128)(2,1)}, u32[]{:S(2)}, u32[]{:S(2)}) collective-permute-start(bf16[1,4,768]{2,1,0:T(4,128)(2,1)} %get-tuple-element.617), channel_id=1, source_target_pairs={{8,0},{16,8},{24,16},{9,1},{17,9},{25,17},{10,2},{18,10},{26,18},{... | collective-permute-start | bytes 18440 | tf_op jit(solution)/shard_map/ppermute | solution.py:25
  18.0 404.0 %collective-permute-start = (bf16[1,4,768]{2,1,0:T(4,128)(2,1)}, bf16[1,4,768]{2,1,0:T(4,128)(2,1)}, u32[]{:S(2)}, u32[]{:S(2)}) collective-permute-start(bf16[1,4,768]{2,1,0:T(4,128)(2,1)} %get-tuple-element.614), channel_id=1, source_target_pairs={{0,8},{8,16},{16,24},{1,9},{9,17},{17,25},{2,10},{10,18},{18,26},{... | collective-permute-start | bytes 18440 | tf_op jit(solution)/shard_map/ppermute | solution.py:22
  23.1 89.2 %copy-start.165 = (bf16[24,384]{1,0:T(8,128)(2,1)S(1)}, bf16[24,384]{1,0:T(8,128)(2,1)}, u32[]{:S(2)}) copy-start(bf16[24,384]{1,0:T(8,128)(2,1)} %param.96) | copy-start | bytes 55300
  23.1 398.9 %collective-permute-start.1 = (bf16[1,4,768]{2,1,0:T(4,128)(2,1)}, bf16[1,4,768]{2,1,0:T(4,128)(2,1)}, u32[]{:S(2)}, u32[]{:S(2)}) collective-permute-start(bf16[1,4,768]{2,1,0:T(4,128)(2,1)} %get-tuple-element.615), channel_id=1, source_target_pairs={{8,0},{16,8},{24,16},{9,1},{17,9},{25,17},{10,2},{18,10},{26,18},{... | collective-permute-start | bytes 18440 | tf_op jit(solution)/shard_map/ppermute | solution.py:25
  24.6 749.0 %reduce-scatter.18.cloned.1.call-start = ((), (), s32[]{:S(2)}) async-start(), calls=%async_computation.12 | async-start | bytes 983040 | tf_op jit(solution)/shard_map/reduce_scatter | solution.py:223
  69.6 83.2 %copy-start.46 = (bf16[768,384]{1,0:T(8,128)(2,1)}, bf16[768,384]{1,0:T(8,128)(2,1)S(1)}, u32[]{:S(2)}) copy-start(bf16[768,384]{1,0:T(8,128)(2,1)S(1)} %all_gather.70) | copy-start | bytes 1769476
  71.2 357.5 %copy-start.53 = (bf16[256,384]{1,0:T(8,128)(2,1)}, bf16[256,384]{1,0:T(8,128)(2,1)S(1)}, u32[]{:S(2)}) copy-start(bf16[256,384]{1,0:T(8,128)(2,1)S(1)} %convolution_convert_fusion.3) | copy-start | bytes 589828
  71.6 353.2 %copy-start.55 = (bf16[256,384]{1,0:T(8,128)(2,1)}, bf16[256,384]{1,0:T(8,128)(2,1)S(1)}, u32[]{:S(2)}) copy-start(bf16[256,384]{1,0:T(8,128)(2,1)S(1)} %convolution_convert_fusion.6) | copy-start | bytes 589828
  71.6 82.1 %copy-start.216 = (s32[2,1]{0,1:T(1,128)S(1)}, s32[2,1]{0,1:T(1,128)}, u32[]{:S(2)}) copy-start(s32[2,1]{0,1:T(1,128)} %param.92) | copy-start | bytes 28
  71.6 85.1 %copy-start.217 = (s32[2,1]{0,1:T(1,128)S(1)}, s32[2,1]{0,1:T(1,128)}, u32[]{:S(2)}) copy-start(s32[2,1]{0,1:T(1,128)} %param.93) | copy-start | bytes 28
  71.7 89.7 %copy-start.218 = (bf16[24]{0:T(256)(128)(2,1)S(1)}, bf16[24]{0:T(256)(128)(2,1)}, u32[]{:S(2)}) copy-start(bf16[24]{0:T(256)(128)(2,1)} %param.107) | copy-start | bytes 148
  71.7 89.9 %copy-start.219 = (bf16[24]{0:T(256)(128)(2,1)S(1)}, bf16[24]{0:T(256)(128)(2,1)}, u32[]{:S(2)}) copy-start(bf16[24]{0:T(256)(128)(2,1)} %param.102) | copy-start | bytes 148
  71.7 90.1 %copy-start.220 = (bf16[24]{0:T(256)(128)(2,1)S(1)}, bf16[24]{0:T(256)(128)(2,1)}, u32[]{:S(2)}) copy-start(bf16[24]{0:T(256)(128)(2,1)} %param.103) | copy-start | bytes 148
  71.7 90.4 %copy-start.221 = (bf16[24]{0:T(256)(128)(2,1)S(1)}, bf16[24]{0:T(256)(128)(2,1)}, u32[]{:S(2)}) copy-start(bf16[24]{0:T(256)(128)(2,1)} %param.106) | copy-start | bytes 148
  71.7 90.6 %copy-start.215 = (bf16[648]{0:T(1024)(128)(2,1)S(1)}, bf16[648]{0:T(1024)(128)(2,1)}, u32[]{:S(2)}) copy-start(bf16[648]{0:T(1024)(128)(2,1)} %param.99) | copy-start | bytes 3892
  71.7 129.4 %copy-start.211 = (bf16[9,24]{1,0:T(8,128)(2,1)S(1)}, bf16[9,24]{1,0:T(8,128)(2,1)}, u32[]{:S(2)}) copy-start(bf16[9,24]{1,0:T(8,128)(2,1)} %param.97) | copy-start | bytes 1300
  111.2 130.7 %copy-start.166 = (bf16[24,384]{1,0:T(8,128)(2,1)S(1)}, bf16[24,384]{1,0:T(8,128)(2,1)}, u32[]{:S(2)}) copy-start(bf16[24,384]{1,0:T(8,128)(2,1)} %param.98) | copy-start | bytes 55300
  111.2 169.1 %copy-start.167 = (bf16[24,384]{1,0:T(8,128)(2,1)S(1)}, bf16[24,384]{1,0:T(8,128)(2,1)}, u32[]{:S(2)}) copy-start(bf16[24,384]{1,0:T(8,128)(2,1)} %param.100) | copy-start | bytes 55300
  161.3 273.9 %copy-start.190 = (f32[1,256]{1,0:T(1,128)}, f32[1,256]{1,0:T(1,128)S(1)}, u32[]{:S(2)}) copy-start(f32[1,256]{1,0:T(1,128)S(1)} %get-tuple-element.661) | copy-start | bytes 3076
  161.3 274.9 %copy-start.188 = (f32[1,256]{1,0:T(1,128)}, f32[1,256]{1,0:T(1,128)S(1)}, u32[]{:S(2)}) copy-start(f32[1,256]{1,0:T(1,128)S(1)} %get-tuple-element.660) | copy-start | bytes 3076
  201.1 196.7 %copy-start.128 = (f32[768]{0:T(1024)}, f32[768]{0:T(1024)S(1)}, u32[]{:S(2)}) copy-start(f32[768]{0:T(1024)S(1)} %convert_element_type.546) | copy-start | bytes 9220
  241.7 167.9 %copy-start.108 = (bf16[256,384]{0,1:T(8,128)(2,1)}, bf16[256,384]{0,1:T(8,128)(2,1)S(1)}, u32[]{:S(2)}) copy-start(bf16[256,384]{0,1:T(8,128)(2,1)S(1)} %copy.367) | copy-start | bytes 589828
  241.9 156.8 %copy-start.107 = (bf16[256,384]{0,1:T(8,128)(2,1)}, bf16[256,384]{0,1:T(8,128)(2,1)S(1)}, u32[]{:S(2)}) copy-start(bf16[256,384]{0,1:T(8,128)(2,1)S(1)} %copy.392) | copy-start | bytes 589828
  241.9 119.1 %copy-start.127 = (bf16[256,384]{1,0:T(8,128)(2,1)S(1)}, bf16[256,384]{1,0:T(8,128)(2,1)}, u32[]{:S(2)}) copy-start(bf16[256,384]{1,0:T(8,128)(2,1)} %convolution_convert_fusion.5) | copy-start | bytes 589828
  280.3 148.0 %copy-start.22 = (bf16[768,384]{1,0:T(8,128)(2,1)}, bf16[768,384]{1,0:T(8,128)(2,1)S(1)}, u32[]{:S(2)}) copy-start(bf16[768,384]{1,0:T(8,128)(2,1)S(1)} %all_gather.74) | copy-start | bytes 1769476
  359.8 38.0 %copy-start.11 = (bf16[2,1,256,768]{3,2,1,0:T(8,128)(2,1)S(1)}, bf16[2,1,256,768]{3,2,1,0:T(8,128)(2,1)}, u32[]{:S(2)}) copy-start(bf16[2,1,256,768]{3,2,1,0:T(8,128)(2,1)} %param.91) | copy-start | bytes 2359300
  672.4 103.4 %reduce-scatter.16.cloned.1.call-start = ((), (), s32[]{:S(2)}) async-start(), calls=%async_computation.11 | async-start | bytes 983040 | tf_op jit(solution)/shard_map/reduce_scatter | solution.py:217
  745.9 46.8 %reduce-scatter.22.cloned.1.call-start = ((), (), s32[]{:S(2)}) async-start(), calls=%async_computation.14 | async-start | bytes 983040 | tf_op jit(solution)/shard_map/reduce_scatter | solution.py:223
  750.7 19.4 %collective-permute-start.4 = (bf16[1,4,1152]{2,1,0:T(4,128)(2,1)S(1)}, bf16[1,4,1152]{2,1,0:T(4,128)(2,1)S(1)}, u32[]{:S(2)}, u32[]{:S(2)}) collective-permute-start(bf16[1,4,1152]{2,1,0:T(4,128)(2,1)S(1)} %maximum_convert_fusion), channel_id=1, source_target_pairs={{0,8},{8,16},{16,24},{1,9},{9,17},{17,25},{2,10},{10,18},{18,26},{... | collective-permute-start | bytes 27656 | tf_op jit(solution)/shard_map/ppermute | solution.py:22
  753.3 17.7 %collective-permute-start.6 = (bf16[1,4,1152]{2,1,0:T(4,128)(2,1)}, bf16[1,4,1152]{2,1,0:T(4,128)(2,1)S(1)}, u32[]{:S(2)}, u32[]{:S(2)}) collective-permute-start(bf16[1,4,1152]{2,1,0:T(4,128)(2,1)} %maximum_convert_fusion.2), channel_id=1, source_target_pairs={{0,8},{8,16},{16,24},{1,9},{9,17},{17,25},{2,10},{10,18},{18,26},{... | collective-permute-start | bytes 27656 | tf_op jit(solution)/shard_map/ppermute | solution.py:22
  756.5 13.6 collective-permute-start.5
  762.6 55.0 %reduce-scatter.20.cloned.1.call-start = ((), (), s32[]{:S(2)}) async-start(), calls=%async_computation.13 | async-start | bytes 983040 | tf_op jit(solution)/shard_map/reduce_scatter | solution.py:217
  763.2 7.8 collective-permute-start.7
  768.6 202.2 %all-reduce.29.cloned.1.call-start = ((), (), s32[]{:S(2)}) async-start(), calls=%async_computation.19 | async-start | bytes 9609216
  819.9 251.8 %reduce-scatter.30.cloned.1.call-start = ((), (), s32[]{:S(2)}) async-start(), calls=%async_computation.18 | async-start | bytes 1216512
  824.1 351.4 %reduce-scatter.24.cloned.1.call-start = ((), (), s32[]{:S(2)}) async-start(), calls=%async_computation.15 | async-start | bytes 2433024 | tf_op jit(solution)/shard_map/reduce_scatter | solution.py:383
  827.7 460.8 %reduce-scatter.26.cloned.1.call-start = ((), (), s32[]{:S(2)}) async-start(), calls=%async_computation.16 | async-start | bytes 4866048 | tf_op jit(solution)/shard_map/reduce_scatter | solution.py:386
  834.0 566.6 %reduce-scatter.28.cloned.1.call-start = ((), (), s32[]{:S(2)}) async-start(), calls=%async_computation.17 | async-start | bytes 4866048 | tf_op jit(solution)/shard_map/reduce_scatter | solution.py:387
  840.2 44.1 %copy-start.100 = (bf16[1,1,256,768]{3,2,1,0:T(8,128)(2,1)S(1)}, bf16[1,1,256,768]{3,2,1,0:T(8,128)(2,1)}, u32[]{:S(2)}) copy-start(bf16[1,1,256,768]{3,2,1,0:T(8,128)(2,1)} %get-tuple-element.604) | copy-start | bytes 1179652
  840.2 46.1 %copy-start.52 = (bf16[768,384]{1,0:T(8,128)(2,1)S(1)}, bf16[768,384]{1,0:T(8,128)(2,1)}, u32[]{:S(2)}) copy-start(bf16[768,384]{1,0:T(8,128)(2,1)} %all_gather.76) | copy-start | bytes 1769476
  841.3 45.9 %copy-start.51 = (bf16[768,384]{1,0:T(8,128)(2,1)S(1)}, bf16[768,384]{1,0:T(8,128)(2,1)}, u32[]{:S(2)}) copy-start(bf16[768,384]{1,0:T(8,128)(2,1)} %copy-done.50) | copy-start | bytes 1769476
  841.3 45.9 %copy-start.110 = (bf16[1,256,384]{1,2,0:T(8,128)(2,1)S(1)}, bf16[1,256,384]{1,2,0:T(8,128)(2,1)}, u32[]{:S(2)}) copy-start(bf16[1,256,384]{1,2,0:T(8,128)(2,1)} %reduce-scatter.18.cloned.1.call-done) | copy-start | bytes 589828
  (200 other events, 1093.0 us)
Sparse Core Ops, SparseCore 0:
  10.9 57.4 all-gather.8
  71.3 57.7 all-gather.10
  132.1 56.4 all-gather.12
  672.6 21.2 reduce-scatter.17
  746.0 21.2 reduce-scatter.15
  770.1 22.5 reduce-scatter.21
  795.0 22.5 reduce-scatter.19
  824.0 146.7 all-reduce.28
  976.5 95.0 reduce-scatter.29
  1077.4 98.1 reduce-scatter.23
  1182.5 106.0 reduce-scatter.25
  1294.4 106.0 reduce-scatter.27
where the time goes:
time: 1420 us; the launch traced here: 1410 us
  waiting for transfers between devices  539 us (38%)
  blocking collectives  393 us (28%)
  local copies, waits for them, and re-layouts  188 us (13%)
  other arithmetic  136 us (10%)
  matrix products  112 us (8%)
  starting transfers between devices  21.9 us (2%)
  between operations  17.8 us (1%)
    unnamed x14, waiting for transfers between devices  172 us
    reduce_scatter x1, waiting for transfers between devices, local(): lax.psum_scatter(grads[10], ('seq', 'dp'), scatter_dimension=2, tiled=True)  113 us
    reduce_scatter x1, waiting for transfers between devices, local(): lax.psum_scatter(grads[11], ('seq', 'dp'), scatter_dimension=1, tiled=True)  112 us
    reduce_scatter x1, waiting for transfers between devices, local(): lax.psum_scatter(grads[7], ('seq', 'dp'), scatter_dimension=0, tiled=True)  104 us
    unnamed x2, blocking collectives  78 us
    scatter-add x16, local copies, waits for them, and re-layouts, run_batch(): d_input_pad.at[:, tap_index:tap_index + local_len]  45.9 us
    all_gather x1, blocking collectives, local(): lax.all_gather(w_query, ('seq', 'dp'), axis=0, tiled=True)  45 us
    all_gather x1, blocking collectives, local(): lax.all_gather(w_convout, ('seq', 'dp'), axis=0, tiled=True)  42.5 us
  transfers between devices with their start and end apart: 20, of which 7 were waited for; matrix products, arithmetic and copies ran while one was open for 16% of the time, Pallas kernels for 0%

commit v1 on v0

--- a/solution.py
+++ b/solution.py
@@ -1,6 +1,11 @@
+import functools
+
 import jax
 import jax.numpy as jnp
+import numpy as np
 from jax import lax
+from jax.experimental import pallas as pl
+from jax.experimental.pallas import tpu as pltpu
 from jax.sharding import PartitionSpec as P
 
 HEADS = 6
@@ -12,19 +17,6 @@
 
 inv_root_two = 0.7071067811865476
 inv_root_tau = 0.3989422804014327
-
-
-def extended(block, sides, width):
-    for axis, dim in sides:
-        count = lax.axis_size(axis)
-        forward = [(i, i + 1) for i in range(count - 1)]
-        backward = [(target, source) for source, target in forward]
-        low = lax.ppermute(
-            lax.slice_in_dim(block, block.shape[dim] - width, None, axis=dim), axis, forward
-        )
-        high = lax.ppermute(lax.slice_in_dim(block, 0, width, axis=dim), axis, backward)
-        block = jnp.concatenate([low, block, high], axis=dim)
-    return block
 
 
 def erf_gelu(pre_act):
@@ -63,7 +55,7 @@
     return (d_signal, d_gain, d_shift)
 
 
-def run_batch(gathered, tokens, grad_rows, valid_rows, sep_rows, first_pos):
+def run_batch(gathered, tokens, row_tokens, grad_rows, valid_row, sep_row, core):
     (
         query_weight,
         key_weight,
@@ -80,7 +72,13 @@
         out_gain,
         out_shift,
     ) = gathered
+    tokens = tokens[None]
+    row_tokens = row_tokens[None]
+    grad_rows = grad_rows[None]
+    valid_rows = valid_row[None]
+    sep_rows = sep_row[None]
     row_count, local_len, width = tokens.shape
+    first_pos = core * local_len
     half_span = (KERNEL - 1) // 2
     heads_width = HEADS * HEAD_DIM
     group_width = width // GROUPS
@@ -90,13 +88,11 @@
     query_low = jnp.dot(tokens, query_weight, preferred_element_type=jnp.float32).astype(
         jnp.bfloat16
     )
-    keys_low = jnp.dot(tokens, key_weight, preferred_element_type=jnp.float32).astype(jnp.bfloat16)
-    values_low = jnp.dot(tokens, value_weight, preferred_element_type=jnp.float32).astype(
+    keys_all = jnp.dot(row_tokens, key_weight, preferred_element_type=jnp.float32).astype(
         jnp.bfloat16
     )
-    keys_all, values_all = (
-        lax.all_gather(keys_low, "seq", axis=1, tiled=True),
-        lax.all_gather(values_low, "seq", axis=1, tiled=True),
+    values_all = jnp.dot(row_tokens, value_weight, preferred_element_type=jnp.float32).astype(
+        jnp.bfloat16
     )
     full_len = keys_all.shape[1]
     query_heads = query_low.reshape(row_count, local_len, HEADS, HEAD_DIM)
@@ -113,7 +109,12 @@
     attended = jnp.einsum(
         "rhqk,rkhe->rqhe", probs_low, values_heads, preferred_element_type=jnp.float32
     ).reshape(row_count, local_len, heads_width)
-    padded = extended(tokens, (("seq", 1),), half_span)
+    padded = lax.dynamic_slice_in_dim(
+        jnp.pad(row_tokens, ((0, 0), (half_span, half_span), (0, 0))),
+        first_pos,
+        local_len + 2 * half_span,
+        1,
+    )
     padded_wide = padded.astype(jnp.float32)
     depth_wide = depth_kernel.astype(jnp.float32)
     depth_out = jnp.zeros((row_count, local_len, width), jnp.float32)
@@ -161,7 +162,7 @@
         branch + tokens_wide, attn_gain_wide, attn_shift.astype(jnp.float32)
     )
     grouped = attn_out.astype(jnp.bfloat16).reshape(row_count, local_len, GROUPS, group_width)
-    pre_act = jnp.einsum("rsgd,gdf->rsgf", grouped, up_weight, preferred_element_type=jnp.float32)
+    pre_act = jnp.einsum("rsgd,gfd->rsgf", grouped, up_weight, preferred_element_type=jnp.float32)
     act_low = erf_gelu(pre_act).astype(jnp.bfloat16)
     down_out = jnp.einsum(
         "rsgf,gfd->rsgd", act_low, down_weight, preferred_element_type=jnp.float32
@@ -177,9 +178,9 @@
         "rsgd,gfd->rsgf", d_down_low, down_weight, preferred_element_type=jnp.float32
     )
     d_pre_low = (d_act * gelu_slope(pre_act)).astype(jnp.bfloat16)
-    d_up_w = jnp.einsum("rsgd,rsgf->gdf", grouped, d_pre_low, preferred_element_type=jnp.float32)
+    d_up_w = jnp.einsum("rsgd,rsgf->gfd", grouped, d_pre_low, preferred_element_type=jnp.float32)
     d_attn_out = d_second + jnp.einsum(
-        "rsgf,gdf->rsgd", d_pre_low, up_weight, preferred_element_type=jnp.float32
+        "rsgf,gfd->rsgd", d_pre_low, up_weight, preferred_element_type=jnp.float32
     ).reshape(row_count, local_len, width)
     d_first, d_attn_gain, d_attn_shift = norm_backward(
         d_attn_out, normed_one, inv_one, attn_gain_wide
@@ -213,22 +214,18 @@
         jnp.einsum("rhqk,rqhe->rkhe", d_scores_low, query_heads, preferred_element_type=jnp.float32)
         * score_scale
     )
-    d_keys, d_values = (
-        lax.psum_scatter(
-            d_keys_part.reshape(row_count, full_len, heads_width).astype(jnp.bfloat16),
-            "seq",
-            scatter_dimension=1,
-            tiled=True,
-        ).astype(jnp.float32),
-        lax.psum_scatter(
-            d_values_part.reshape(row_count, full_len, heads_width).astype(jnp.bfloat16),
-            "seq",
-            scatter_dimension=1,
-            tiled=True,
-        ).astype(jnp.float32),
-    )
-    d_keys_low = d_keys.astype(jnp.bfloat16)
-    d_values_low = d_values.astype(jnp.bfloat16)
+    parts = jnp.concatenate(
+        [
+            d_keys_part.reshape(full_len, heads_width),
+            d_values_part.reshape(full_len, heads_width),
+        ],
+        -1,
+    ).astype(jnp.bfloat16)
+    other_half = lax.dynamic_slice_in_dim(parts, (1 - core) * local_len, local_len, 0)
+    own_half = lax.dynamic_slice_in_dim(parts, core * local_len, local_len, 0)
+    whole = (add_up([own_half, swap(other_half, "dp", 1)]).astype(jnp.bfloat16))[None]
+    d_keys_low = whole[..., :heads_width]
+    d_values_low = whole[..., heads_width:]
     d_values_pad = jnp.zeros((row_count, local_len + 2 * half_span, heads_width), jnp.float32)
     d_tap_list = []
     for tap_index in range(KERNEL):
@@ -272,13 +269,14 @@
     right_rim = jnp.concatenate(
         [d_values_pad[:, local_len + half_span :], d_input_pad[:, local_len + half_span :]], -1
     )
-    rim_rows = jnp.concatenate([left_rim, right_rim], 1)
-    arrived = extended(rim_rows.astype(jnp.bfloat16), (("seq", 1),), half_span).astype(
-        rim_rows.dtype
-    )
-    incoming = jnp.pad(
-        arrived[:, :half_span], ((0, 0), (0, local_len - half_span), (0, 0))
-    ) + jnp.pad(arrived[:, 3 * half_span :], ((0, 0), (local_len - half_span, 0), (0, 0)))
+    rim = jnp.where(core == 0, right_rim, left_rim).astype(jnp.bfloat16)
+    arrived = swap(rim, "dp", 1).astype(jnp.float32)
+    gap = ((0, 0), (local_len - half_span, 0), (0, 0))
+    incoming = jnp.where(
+        core == 0,
+        jnp.pad(arrived, gap),
+        jnp.pad(arrived, ((0, 0), (0, local_len - half_span), (0, 0))),
+    )
     d_conv_values_low = (
         d_values_pad[:, half_span : half_span + local_len] + incoming[..., :heads_width]
     ).astype(jnp.bfloat16)
@@ -318,7 +316,128 @@
         d_out_gain,
         d_out_shift,
     )
-    return (final_out.astype(jnp.bfloat16), input_grad, grads)
+    return (final_out.astype(jnp.bfloat16)[0], input_grad[0], grads)
+
+
+def dp_groups(count):
+    masks = []
+    bit = 2
+    while bit < count:
+        if bit * 2 < count:
+            masks.append((bit, 2 * bit, 3 * bit))
+            bit *= 4
+        else:
+            masks.append((bit,))
+            bit *= 2
+    return masks
+
+
+def swap(x, axis, mask):
+    count = lax.axis_size(axis)
+    return lax.ppermute(x, axis, [(i, i ^ mask) for i in range(count)])
+
+
+def relative_codes():
+    seq, dp = lax.axis_size("seq"), lax.axis_size("dp")
+    codes = [j * dp for j in range(seq)]
+    for masks in dp_groups(dp):
+        codes = [c ^ m for m in (0,) + masks for c in codes]
+    return codes + [c ^ 1 for c in codes]
+
+
+def gather_relative(x):
+    seq, dp = lax.axis_size("seq"), lax.axis_size("dp")
+    held = jnp.stack([x] + [swap(x, "seq", j) for j in range(1, seq)])
+    for masks in dp_groups(dp):
+        held = jnp.concatenate([held] + [swap(held, "dp", m) for m in masks])
+    return held, swap(held, "dp", 1)
+
+
+def add_up(parts):
+    total = parts[0].astype(jnp.float32)
+    for part in parts[1:]:
+        total = total + part.astype(jnp.float32)
+    return total
+
+
+def scatter_relative(kept, sent):
+    seq, dp = lax.axis_size("seq"), lax.axis_size("dp")
+    held = add_up([kept, swap(sent, "dp", 1)]).astype(jnp.bfloat16)
+    for masks in reversed(dp_groups(dp)):
+        held = held.reshape((len(masks) + 1, -1) + held.shape[1:])
+        parts = [held[0]] + [swap(held[i + 1], "dp", m) for i, m in enumerate(masks)]
+        held = add_up(parts).astype(jnp.bfloat16)
+    return add_up([held[0]] + [swap(held[j], "seq", j) for j in range(1, seq)])
+
+
+def reorder_kernel(count, index, *refs):
+    sources, target, sems = refs[:-2], refs[-2], refs[-1]
+    per = count // len(sources)
+    copies = []
+    for i in range(count):
+        copies.append(
+            pltpu.make_async_copy(
+                sources[i // per].at[i % per], target.at[index[i]], sems.at[i]
+            )
+        )
+    for copy in copies:
+        copy.start()
+    for copy in copies:
+        copy.wait()
+
+
+def reorder(parts, index):
+    count = sum(p.shape[0] for p in parts)
+    return pl.pallas_call(
+        functools.partial(reorder_kernel, count),
+        out_shape=jax.ShapeDtypeStruct((count,) + parts[0].shape[1:], parts[0].dtype),
+        in_specs=[pl.BlockSpec(memory_space=pltpu.SMEM)]
+        + [pl.BlockSpec(memory_space=pltpu.VMEM)] * len(parts),
+        out_specs=pl.BlockSpec(memory_space=pl.ANY),
+        scratch_shapes=[pltpu.SemaphoreType.DMA((count,))],
+        compiler_params=pltpu.CompilerParams(vmem_limit_bytes=40 * 1024 * 1024),
+    )(index, *parts)
+
+
+def token_perms():
+    seq, dp = lax.axis_size("seq"), lax.axis_size("dp")
+    first, second = [], []
+    for z in range(seq):
+        for d in range(dp):
+            core, rest = d & 1, d & ~1
+            odd = z & 1
+            first.append((z * dp + d, (2 * odd + core) * dp + rest + (z >> 1)))
+            second.append((z * dp + d, (2 * (1 - odd) + core) * dp + rest + (z >> 1)))
+    return first, second
+
+
+def to_rows(x):
+    first, second = token_perms()
+    z = lax.axis_index("seq")
+    odd, high = z & 1, z >> 1
+    a = lax.ppermute(lax.dynamic_index_in_dim(x, odd, 0, False), ("seq", "dp"), first)
+    b = lax.ppermute(lax.dynamic_index_in_dim(x, 1 - odd, 0, False), ("seq", "dp"), second)
+    return jnp.where(high == 0, jnp.concatenate([a, b]), jnp.concatenate([b, a]))
+
+
+def from_rows(x):
+    first, second = token_perms()
+    z = lax.axis_index("seq")
+    odd, high = z & 1, z >> 1
+    half = x.reshape(2, x.shape[0] // 2, x.shape[1])
+    a = lax.ppermute(
+        lax.dynamic_index_in_dim(half, high, 0, False), ("seq", "dp"), [(t, s) for s, t in first]
+    )
+    b = lax.ppermute(
+        lax.dynamic_index_in_dim(half, 1 - high, 0, False),
+        ("seq", "dp"),
+        [(t, s) for s, t in second],
+    )
+    return jnp.where(odd == 0, jnp.stack([a, b]), jnp.stack([b, a]))
+
+
+def pad_rows(x, multiple):
+    return jnp.pad(x, ((0, -x.shape[0] % multiple), (0, 0)))
 
 
 def local(
@@ -341,87 +460,183 @@
     gain_out,
     shift_out,
 ):
-    first_pos = lax.axis_index("seq") * layer_in.shape[2]
-    outputs = []
-    input_grads = []
-    totals = None
-    for micro_step in range(layer_in.shape[0]):
-        gathered = (
-            lax.all_gather(w_query, ("seq", "dp"), axis=0, tiled=True),
-            lax.all_gather(w_key, ("seq", "dp"), axis=0, tiled=True),
-            lax.all_gather(w_value, ("seq", "dp"), axis=0, tiled=True),
-            lax.all_gather(w_depth, ("seq", "dp"), axis=1, tiled=True),
-            lax.all_gather(w_point, ("seq", "dp"), axis=0, tiled=True),
-            lax.all_gather(w_kernel, ("seq", "dp"), axis=0, tiled=True),
-            lax.all_gather(w_convout, ("seq", "dp"), axis=0, tiled=True),
-            lax.all_gather(w_output, ("seq", "dp"), axis=0, tiled=True),
-            lax.all_gather(gain_attn, ("seq", "dp"), axis=0, tiled=True),
-            lax.all_gather(shift_attn, ("seq", "dp"), axis=0, tiled=True),
-            lax.all_gather(w_up, ("seq", "dp"), axis=2, tiled=True),
-            lax.all_gather(w_down, ("seq", "dp"), axis=1, tiled=True),
-            lax.all_gather(gain_out, ("seq", "dp"), axis=0, tiled=True),
-            lax.all_gather(shift_out, ("seq", "dp"), axis=0, tiled=True),
-        )
-        layer_rows, grad_input, grads = run_batch(
-            gathered,
-            layer_in[micro_step],
-            cotangent[micro_step],
-            valid_len[micro_step],
-            sep_pos[micro_step],
-            first_pos,
-        )
-        outputs.append(layer_rows)
-        input_grads.append(grad_input)
-        partial_sum = (
-            lax.psum_scatter(grads[0], ("seq", "dp"), scatter_dimension=0, tiled=True),
-            lax.psum_scatter(grads[1], ("seq", "dp"), scatter_dimension=0, tiled=True),
-            lax.psum_scatter(grads[2], ("seq", "dp"), scatter_dimension=0, tiled=True),
-            lax.psum_scatter(grads[3], ("seq", "dp"), scatter_dimension=1, tiled=True),
-            lax.psum_scatter(grads[4], ("seq", "dp"), scatter_dimension=0, tiled=True),
-            lax.psum_scatter(grads[5], ("seq", "dp"), scatter_dimension=0, tiled=True),
-            lax.psum_scatter(grads[6], ("seq", "dp"), scatter_dimension=0, tiled=True),
-            lax.psum_scatter(grads[7], ("seq", "dp"), scatter_dimension=0, tiled=True),
-            lax.psum_scatter(grads[8], ("seq", "dp"), scatter_dimension=0, tiled=True),
-            lax.psum_scatter(grads[9], ("seq", "dp"), scatter_dimension=0, tiled=True),
-            lax.psum_scatter(grads[10], ("seq", "dp"), scatter_dimension=2, tiled=True),
-            lax.psum_scatter(grads[11], ("seq", "dp"), scatter_dimension=1, tiled=True),
-            lax.psum_scatter(grads[12], ("seq", "dp"), scatter_dimension=0, tiled=True),
-            lax.psum_scatter(grads[13], ("seq", "dp"), scatter_dimension=0, tiled=True),
-        )
-        totals = partial_sum if totals is None else jax.tree.map(jnp.add, totals, partial_sum)
+    seq, dp = lax.axis_size("seq"), lax.axis_size("dp")
+    count = seq * dp
+    z, d = lax.axis_index("seq"), lax.axis_index("dp")
+    core = d & 1
+    me = z * dp + d
+    codes = relative_codes()
+    absolute = jnp.asarray(np.array(codes, np.int32)) ^ me
+    inverse = np.zeros(count, np.int32)
+    inverse[np.array(codes)] = np.arange(count)
+    relative = jnp.asarray(inverse)[jnp.arange(count, dtype=jnp.int32) ^ me]
+    width = layer_in.shape[-1]
+    wide = w_query.shape[1]
+    rows = w_query.shape[0]
+    hidden = w_up.shape[2]
+
+    small = jnp.concatenate(
+        [w_kernel, w_depth.reshape(-1), gain_attn, shift_attn, gain_out, shift_out]
+    )
+    small_size = small.shape[0]
+    small = pad_rows(jnp.pad(small, (0, -small_size % wide)).reshape(-1, wide), 8)
+    early = pad_rows(
+        jnp.concatenate([w_query, w_key, w_value, w_point, w_convout, small]), 16
+    )
+    late = pad_rows(
+        jnp.concatenate(
+            [
+                w_output[:, :wide],
+                w_output[:, wide:],
+                jnp.swapaxes(w_up, 1, 2).reshape(2 * hidden, wide),
+                w_down.reshape(2 * hidden, wide),
+            ]
+        ),
+        16,
+    )
+    late_rows = late.shape[0]
+    tokens_own = to_rows(layer_in[:, 0])
+    tokens_other = swap(tokens_own, "dp", 1)
+    row_tokens = jnp.where(
+        core == 0,
+        jnp.concatenate([tokens_own, tokens_other]),
+        jnp.concatenate([tokens_other, tokens_own]),
+    )
+    late_all = lax.all_gather(late, ("seq", "dp"), axis=0, tiled=False)
+    early_all = reorder(gather_relative(early), absolute)
+    cot_own = to_rows(cotangent[:, 0])
+
+    def take(index):
+        return early_all[:, index * rows : (index + 1) * rows].reshape(count * rows, wide)
+
+    small_all = early_all[:, 5 * rows : 5 * rows + small.shape[0]].reshape(count, -1)
+    sizes = [w_kernel.shape[0], w_depth.size, rows, rows, rows, rows]
+    offsets = np.cumsum([0] + sizes)
+    pieces = [small_all[:, offsets[i] : offsets[i + 1]] for i in range(6)]
+    kernel_flat = pieces[0].reshape(-1)
+    depth_kernel = (
+        pieces[1].reshape(count, KERNEL, rows).transpose(1, 0, 2).reshape(KERNEL, width)
+    )
+    gains = [p.reshape(-1) for p in pieces[2:]]
+    out_weight = jnp.concatenate(
+        [late_all[:, :rows].reshape(-1, wide), late_all[:, rows : 2 * rows].reshape(-1, wide)], 1
+    )
+    up_t = (
+        late_all[:, 2 * rows : 2 * rows + 2 * hidden]
+        .reshape(count, 2, hidden, wide)
+        .transpose(1, 0, 2, 3)
+        .reshape(2, count * hidden, wide)
+    )
+    down = (
+        late_all[:, 2 * rows + 2 * hidden : 2 * rows + 4 * hidden]
+        .reshape(count, 2, hidden, wide)
+        .transpose(1, 0, 2, 3)
+        .reshape(2, count * hidden, wide)
+    )
+    slot_valid = valid_len[:, 0]
+    slot_sep = sep_pos[:, 0]
+    pair_valid = jnp.stack([slot_valid, slot_sep]).astype(jnp.float32)
+    pair_other = swap(pair_valid, "dp", 1)
+    row_info = jnp.where((z & 1) == core, pair_valid, pair_other)[:, z >> 1].astype(jnp.int32)
+    gathered = (
+        take(0),
+        take(1),
+        take(2),
+        depth_kernel,
+        take(3),
+        kernel_flat,
+        take(4),
+        out_weight,
+        gains[0],
+        gains[1],
+        up_t,
+        down,
+        gains[2],
+        gains[3],
+    )
+    layer_rows, grad_input, grads = run_batch(
+        gathered, tokens_own, row_tokens, cot_own, row_info[0], row_info[1], core
+    )
     (
-        grad_query,
-        grad_key,
-        grad_value,
-        grad_depth,
-        grad_point,
-        grad_kernel,
-        grad_convout,
-        grad_output,
-        grad_gain_attn,
-        grad_shift_attn,
-        grad_up,
-        grad_down,
-        grad_gain_out,
-        grad_shift_out,
-    ) = totals
+        d_query_w,
+        d_key_w,
+        d_value_w,
+        d_depth_w,
+        d_point_w,
+        d_kernel_w,
+        d_conv_w,
+        d_out_w,
+        d_attn_gain,
+        d_attn_shift,
+        d_up_w,
+        d_down_w,
+        d_out_gain,
+        d_out_shift,
+    ) = grads
+
+    def blocks(x):
+        return x.reshape(count, rows, wide)
+
+    first_pack = jnp.concatenate(
+        [
+            blocks(d_out_w[:, :wide]),
+            blocks(d_out_w[:, wide:]),
+            d_up_w.reshape(2, count, hidden, wide)
+            .transpose(1, 0, 2, 3)
+            .reshape(count, 2 * hidden, wide),
+            d_down_w.reshape(2, count, hidden, wide)
+            .transpose(1, 0, 2, 3)
+            .reshape(count, 2 * hidden, wide),
+        ],
+        1,
+    ).astype(jnp.bfloat16)
+    first_pack = jnp.pad(first_pack, ((0, 0), (0, late_rows - first_pack.shape[1]), (0, 0)))
+    small_pack = jnp.concatenate(
+        [
+            d_kernel_w.reshape(count, -1),
+            d_depth_w.reshape(KERNEL, count, rows).transpose(1, 0, 2).reshape(count, -1),
+        ]
+        + [g.reshape(count, rows) for g in (d_attn_gain, d_attn_shift, d_out_gain, d_out_shift)],
+        1,
+    )
+    small_pack = jnp.pad(small_pack, ((0, 0), (0, small.size - small_size))).reshape(
+        count, small.shape[0], wide
+    )
+    second_pack = jnp.concatenate(
+        [blocks(g) for g in (d_query_w, d_key_w, d_value_w, d_point_w, d_conv_w)] + [small_pack], 1
+    ).astype(jnp.bfloat16)
+    second_pack = jnp.pad(
+        second_pack, ((0, 0), (0, early.shape[0] - second_pack.shape[1]), (0, 0))
+    )
+    half = count // 2
+    first_rel = reorder([first_pack], relative)
+    second_rel = reorder([second_pack], relative)
+    first = scatter_relative(first_rel[:half], first_rel[half:])
+    second = scatter_relative(second_rel[:half], second_rel[half:])
+
+    def part(index):
+        return second[index * rows : (index + 1) * rows]
+
+    flat = second[5 * rows : 5 * rows + small.shape[0]].reshape(-1)
+    outs = [flat[offsets[i] : offsets[i + 1]] for i in range(6)]
+    x_grad = from_rows(grad_input.astype(jnp.bfloat16)).astype(jnp.float32)
     return (
-        jnp.stack(outputs),
-        jnp.stack(input_grads),
-        grad_query,
-        grad_key,
-        grad_value,
-        grad_depth,
-        grad_point,
-        grad_kernel,
-        grad_convout,
-        grad_output,
-        grad_gain_attn,
-        grad_shift_attn,
-        grad_up,
-        grad_down,
-        grad_gain_out,
-        grad_shift_out,
+        from_rows(layer_rows)[:, None],
+        x_grad[:, None],
+        part(0),
+        part(1),
+        part(2),
+        outs[1].reshape(KERNEL, rows),
+        part(3),
+        outs[0],
+        part(4),
+        jnp.concatenate([first[:rows], first[rows : 2 * rows]], 1),
+        outs[2],
+        outs[3],
+        jnp.swapaxes(first[2 * rows : 2 * rows + 2 * hidden].reshape(2, hidden, wide), 1, 2),
+        first[2 * rows + 2 * hidden : 2 * rows + 4 * hidden].reshape(2, hidden, wide),
+        outs[4],
+        outs[5],
     )
 
 

time: 1420 us -> 557 us (0.39)
  waiting for transfers between devices: 539 us -> 67.9 us
  blocking collectives: 393 us -> 0 us
  starting transfers between devices: 21.9 us -> 62.3 us
  Pallas kernels: 0 us -> 19 us
  other arithmetic: 136 us -> 117 us
  matrix products: 112 us -> 93.4 us
  local copies, waits for them, and re-layouts: 188 us -> 172 us
    reduce_scatter x7 -> x0, waiting for transfers between devices: 367 us -> none  [the longest x1 113 us: local(): lax.psum_scatter(grads[10], ('seq', 'dp'), scatter_dimension=2, tiled=True)]
    all_gather x10 -> x0, blocking collectives: 315 us -> none  [the longest x1 45 us: local(): lax.all_gather(w_query, ('seq', 'dp'), axis=0, tiled=True)]
    unnamed x14 -> x1, waiting for transfers between devices: 172 us -> 0.02 us
    unnamed x2 -> x0, blocking collectives: 78 us -> none
    ppermute x8 -> x33, waiting for transfers between devices: 0.02 us -> 67.9 us  [the longest x25 52.7 us: swap(): return lax.ppermute(x, axis, [(i, i ^ mask) for i in range(count)])]
    ppermute x8 -> x33, starting transfers between devices: 21.2 us -> 62.2 us  [the longest x25 40.6 us: swap(): return lax.ppermute(x, axis, [(i, i ^ mask) for i in range(count)])]
    pallas_call x0 -> x3, Pallas kernels: none -> 19 us  [reorder(): pl.pallas_call(functools.partial(reorder_kernel, count), out_shape=jax.Sh...]
    scatter-add x16 -> x8, local copies, waits for them, and re-layouts: 45.9 us -> 37.8 us  [run_batch(): d_input_pad.at[:, tap_index:tap_index + local_len]]
  transfers between devices with their start and end apart: 20 -> 34, of which waited for: 7 -> 10; matrix products, arithmetic and copies ran while one was open for 16% -> 26% of each run, Pallas kernels for 0% -> 3%
where the time goes in v1:
time: 557 us; the launch traced here: 549 us
  local copies, waits for them, and re-layouts  172 us (31%)
  other arithmetic  117 us (21%)
  matrix products  93.4 us (17%)
  waiting for transfers between devices  67.9 us (12%)
  starting transfers between devices  62.3 us (11%)
  Pallas kernels  19 us (3%)
  between operations  16.7 us (3%)
    ppermute x25, waiting for transfers between devices, swap(): return lax.ppermute(x, axis, [(i, i ^ mask) for i in range(count)])  52.7 us
    ppermute x25, starting transfers between devices, swap(): return lax.ppermute(x, axis, [(i, i ^ mask) for i in range(count)])  40.6 us
    scatter-add x8, local copies, waits for them, and re-layouts, run_batch(): d_input_pad.at[:, tap_index:tap_index + local_len]  37.8 us
    unnamed x356, local copies, waits for them, and re-layouts  28.9 us
    scatter-add x8, local copies, waits for them, and re-layouts, run_batch(): d_values_pad.at[:, tap_index:tap_index + local_len].add(spread_back)  23.4 us
    pallas_call x3, Pallas kernels, reorder(): pl.pallas_call(functools.partial(reorder_kernel, count), out_shape=jax.Sh...  19 us
    add x6, other arithmetic, run_batch(): d_input_pad.at[:, tap_index:tap_index + local_len]  15.2 us
    add x7, other arithmetic, run_batch(): d_values_pad.at[:, tap_index:tap_index + local_len].add(spread_back)  14.9 us
  transfers between devices with their start and end apart: 34, of which 10 were waited for; matrix products, arithmetic and copies ran while one was open for 26% of the time, Pallas kernels for 3%

profile of v1, /device:TPU:0, one launch (start us, length us, event | category | flops | bytes accessed | tf_op | source)
XLA Modules:
  0.0 548.7 jit_solution(630618501719985732)
XLA Ops:
  8.8 3.4 concatenate.254
  15.2 3.1 collective-permute-start.3
  33.2 7.4 %collective-permute-done.6 = bf16[4,128,384]{2,1,0:T(8,128)(2,1)S(1)} collective-permute-done((bf16[4,128,384]{2,1,0:T(8,128)(2,1)S(1)}, bf16[4,128,384]{2,1,0:T(8,128)(2,1)S(1)}, u32[]{:S(2)}, u32[]{:S(2)}) %collective-permute-start.6) | collective-permute-done | bytes 393248 | tf_op jit(solution)/shard_map/ppermute | solution.py:337
  40.6 3.7 collective-permute-start.10
  44.3 6.7 %collective-permute-done.7 = bf16[4,128,384]{2,1,0:T(8,128)(2,1)S(1)} collective-permute-done((bf16[4,128,384]{2,1,0:T(8,128)(2,1)S(1)}, bf16[4,128,384]{2,1,0:T(8,128)(2,1)S(1)}, u32[]{:S(2)}, u32[]{:S(2)}) %collective-permute-start.7) | collective-permute-done | bytes 393248 | tf_op jit(solution)/shard_map/ppermute | solution.py:337
  52.8 3.7 collective-permute-start.9
  63.0 6.7 %collective-permute-done.14 = bf16[256,768]{1,0:T(8,128)(2,1)S(1)} collective-permute-done((bf16[256,768]{1,0:T(8,128)(2,1)S(1)}, bf16[256,768]{1,0:T(8,128)(2,1)S(1)}, u32[]{:S(2)}, u32[]{:S(2)}) %collective-permute-start.14) | collective-permute-done | bytes 393248 | tf_op jit(solution)/shard_map/ppermute | solution.py:419
  80.5 5.4 shard_map.315
  102.0 7.1 %fusion.171 = (f32[6,512]{1,0:T(8,128)S(1)}, f32[6,512,1024]{2,1,0:T(8,128)}) fusion(pred[1024]{0:T(1024)(128)(4,1)S(1)} %iota_compare_fusion, bf16[512,6,64]{0,2,1:T(8,128)(2,1)S(1)} %bitcast.470, bf16[1024,6,64]{0,2,1:T(8,128)(2,1)S(1)} %bitcast.539), kind=kOutput, calls=%fused_computation.376 | convolution fusion | flops 415237120 | bytes 13775872 | tf_op jit(solution)/shard_map/sub | solution.py:35
  109.1 6.8 %fusion.52 = bf16[6,64,512]{2,1,0:T(8,128)(2,1)S(1)} fusion(bf16[1024,6,64]{0,2,1:T(8,128)(2,1)S(1)} %bitcast.596, f32[6,512,1024]{2,1,0:T(8,128)} %get-tuple-element.346, f32[6,512]{1,0:T(8,128)S(1)} %get-tuple-element.345), kind=kOutput, calls=%fused_computation.139 | convolution fusion | flops 409141248 | bytes 13774848 | tf_op jit(solution)/shard_map/rhqk,rkhe->rqhe/dot_general | solution.py:109
  138.8 3.4 fusion.96
  143.7 3.3 fusion.158
  151.0 13.6 %fusion.72 = f32[2,1536,512]{2,1,0:T(8,128)S(1)} fusion(bf16[2,1536,384]{2,1,0:T(8,128)(2,1)S(1)} %bitcast.474, bf16[64,2,8,384]{3,2,1,0:T(8,128)(2,1)S(1)} %bitcast.489), kind=kOutput, calls=%fused_computation.162 | convolution fusion | flops 1207959552 | bytes 9437184 | tf_op jit(solution)/shard_map/rsgd,gfd->rsgf/dot_general | solution.py:165
  164.7 4.3 fusion.109
  179.3 3.4 fusion.15
  182.7 3.3 convolution_convert_fusion
  188.6 3.2 convolution_convert_fusion.1
  194.8 3.9 multiply_reduce_fusion.1
  202.8 3.2 convert_multiply_fusion.9
  248.7 11.6 %multiply_reduce_fusion = (f32[6,512]{1,0:T(8,128)S(1)}, f32[6,512,1024]{2,1,0:T(8,128)}) fusion(f32[6,512,1024]{2,1,0:T(8,128)} %get-tuple-element.346, f32[6,512]{1,0:T(8,128)S(1)} %copy-done.145, bf16[512,6,64]{0,2,1:T(8,128)(2,1)S(1)} %bitcast.551, bf16[1024,6,64]{0,2,1:T(8,128)(2,1)S(1)} %bitcast.597), kind=kOutput, calls=%fused_computation.3 | convolution fusion | flops 412087296 | bytes 26370048 | tf_op jit(solution)/shard_map/rqhe,rkhe->rhqk/dot_general | solution.py:201
  261.4 6.2 %multiply_convert_fusion = bf16[6,512,1024]{2,1,0:T(8,128)(2,1)S(1)} fusion(f32[6,512,1024]{2,1,0:T(8,128)} %get-tuple-element.350, f32[6,512]{1,0:T(8,128)S(1)} %get-tuple-element.349, f32[6,512,1024]{2,1,0:T(8,128)S(1)} %bitcast.469, f32[6,512]{1,0:T(8,128)S(1)} %copy-done.145), kind=kLoop, calls=%fused_computation.2 | loop fusion | flops 12582912 | bytes 31481856 | tf_op jit(solution)/shard_map/convert_element_type | solution.py:208
  283.1 6.6 %fusion.41 = bf16[6,64,1024]{2,1,0:T(8,128)(2,1)} fusion(bf16[512,6,64]{0,2,1:T(8,128)(2,1)S(1)} %bitcast.552, f32[6,512,1024]{2,1,0:T(8,128)} %get-tuple-element.346, f32[6,512]{1,0:T(8,128)S(1)} %copy-done.146), kind=kOutput, calls=%fused_computation.122 | convolution fusion | flops 409337856 | bytes 13774848 | tf_op jit(solution)/shard_map/rhqk,rqhe->rkhe/dot_general | solution.py:204
  296.2 5.0 scatter-add.61
  303.9 5.0 scatter-add.64
  311.7 5.0 scatter-add.65
  319.4 5.0 scatter-add.66
  327.2 5.0 scatter-add.69
  334.9 5.0 scatter-add.70
  339.9 3.9 fusion.40
  349.4 9.9 %collective-permute-start.16 = (bf16[512,768]{1,0:T(8,128)(2,1)}, bf16[512,768]{1,0:T(8,128)(2,1)}, u32[]{:S(2)}, u32[]{:S(2)}) collective-permute-start(bf16[512,768]{1,0:T(8,128)(2,1)} %fusion.59), channel_id=1, source_target_pairs={{0,1},{1,0},{2,3},{3,2},{4,5},{5,4},{6,7},{7,6},{8,9},{9,8},{10,11... | collective-permute-start | bytes 2359304 | tf_op jit(solution)/shard_map/ppermute | solution.py:337
  359.3 3.2 scatter-add.76
  365.0 3.2 scatter-add.79
  370.4 3.3 scatter-add.80
  375.9 3.2 scatter-add.81
  381.6 3.2 scatter-add.84
  387.0 3.3 scatter-add.85
  392.4 3.2 scatter-add.86
  399.0 6.6 %scatter-add.71 = f32[1,520,768]{2,1,0:T(8,128)S(1)} dynamic-update-slice(f32[1,520,768]{2,1,0:T(8,128)S(1)} %copy-done.10, f32[1,512,768]{2,1,0:T(8,128)} %get-tuple-element.281, s32[]{:T(128)} %constant.498.clone.1, s32[]{:T(128)} %constant.523.clone.1, s32[]{:T(128)} %constant.498.clone.1) | dynamic-update-slice | bytes 3145732 | tf_op jit(solution)/shard_map/scatter-add | solution.py:264
  425.5 5.0 shard_map.316
  433.9 8.6 %shard_map.317 = bf16[32,240,384]{2,1,0:T(8,128)(2,1)S(1)} custom-call(s32[32]{0:T(128)S(1)} %gather_fusion, bf16[32,240,384]{2,1,0:T(8,128)(2,1)S(1)} %pad_maximum_fusion.refs_0_), custom_call_target="tpu_custom_call" | custom-call | tf_op jit(solution)/shard_map/pallas_call | solution.py:391
  457.5 3.2 collective-permute-done.20
  460.7 6.7 %collective-permute-start.12 = (bf16[256,768]{1,0:T(8,128)(2,1)S(1)}, bf16[256,768]{1,0:T(8,128)(2,1)S(1)}, u32[]{:S(2)}, u32[]{:S(2)}) collective-permute-start(bf16[256,768]{1,0:T(8,128)(2,1)S(1)} %get-tuple-element.289), channel_id=1, source_target_pairs={{16,0},{24,1},{18,2},{26,3},{20,4},{28,5},{22,6},{30,7},{0,8},{8,9... | collective-permute-start | bytes 1179656 | tf_op jit(solution)/shard_map/ppermute | solution.py:431
  468.0 3.4 collective-permute-done.22
  471.4 6.8 %collective-permute-start.18 = (bf16[256,768]{1,0:T(8,128)(2,1)S(1)}, bf16[256,768]{1,0:T(8,128)(2,1)S(1)}, u32[]{:S(2)}, u32[]{:S(2)}) collective-permute-start(bf16[256,768]{1,0:T(8,128)(2,1)S(1)} %get-tuple-element.285), channel_id=1, source_target_pairs={{16,0},{24,1},{18,2},{26,3},{20,4},{28,5},{22,6},{30,7},{0,8},{8,9... | collective-permute-start | bytes 1179656 | tf_op jit(solution)/shard_map/ppermute | solution.py:431
  489.3 8.4 %collective-permute-done.18 = bf16[256,768]{1,0:T(8,128)(2,1)S(1)} collective-permute-done((bf16[256,768]{1,0:T(8,128)(2,1)S(1)}, bf16[256,768]{1,0:T(8,128)(2,1)S(1)}, u32[]{:S(2)}, u32[]{:S(2)}) %collective-permute-start.18) | collective-permute-done | bytes 393248 | tf_op jit(solution)/shard_map/ppermute | solution.py:431
  499.1 6.4 %collective-permute-done.24 = bf16[128,384]{1,0:T(8,128)(2,1)S(1)} collective-permute-done((bf16[128,384]{1,0:T(8,128)(2,1)S(1)}, bf16[128,384]{1,0:T(8,128)(2,1)S(1)}, u32[]{:S(2)}, u32[]{:S(2)}) %collective-permute-start.24) | collective-permute-done | bytes 98336 | tf_op jit(solution)/shard_map/ppermute | solution.py:337
  507.5 14.3 %collective-permute-done.28 = bf16[4,240,384]{2,1,0:T(8,128)(2,1)} collective-permute-done((bf16[4,240,384]{2,1,0:T(8,128)(2,1)}, bf16[4,240,384]{2,1,0:T(8,128)(2,1)}, u32[]{:S(2)}, u32[]{:S(2)}) %collective-permute-start.28) | collective-permute-done | bytes 737312 | tf_op jit(solution)/shard_map/ppermute | solution.py:337
  531.9 8.3 %collective-permute-done.31 = bf16[240,384]{1,0:T(8,128)(2,1)S(1)} collective-permute-done((bf16[240,384]{1,0:T(8,128)(2,1)S(1)}, bf16[240,384]{1,0:T(8,128)(2,1)S(1)}, u32[]{:S(2)}, u32[]{:S(2)}) %collective-permute-start.31) | collective-permute-done | bytes 184352 | tf_op jit(solution)/shard_map/ppermute | solution.py:337
  (687 shorter events, 268.4 us)
Async XLA Ops:
  7.2 19.8 %copy-start.111 = (bf16[24,768]{1,0:T(8,128)(2,1)S(1)}, bf16[24,768]{1,0:T(8,128)(2,1)}, u32[]{:S(2)}) copy-start(bf16[24,768]{1,0:T(8,128)(2,1)} %param.67) | copy-start | bytes 110596
  7.2 19.8 %copy-start.110 = (bf16[2,384,48]{1,2,0:T(8,128)(2,1)S(1)}, bf16[2,384,48]{1,2,0:T(8,128)(2,1)}, u32[]{:S(2)}) copy-start(bf16[2,384,48]{1,2,0:T(8,128)(2,1)} %param.70) | copy-start | bytes 221188
  7.2 19.8 %copy-start.109 = (bf16[2,48,384]{2,1,0:T(8,128)(2,1)S(1)}, bf16[2,48,384]{2,1,0:T(8,128)(2,1)}, u32[]{:S(2)}) copy-start(bf16[2,48,384]{2,1,0:T(8,128)(2,1)} %param.71) | copy-start | bytes 221188
  7.2 20.6 %copy-start.88 = (bf16[2,1,256,768]{3,2,1,0:T(8,128)(2,1)S(1)}, bf16[2,1,256,768]{3,2,1,0:T(8,128)(2,1)}, u32[]{:S(2)}) copy-start(bf16[2,1,256,768]{3,2,1,0:T(8,128)(2,1)} %param.57) | copy-start | bytes 2359300
  7.2 135.0 %all-gather.3.cloned.1.call-start = ((), (), s32[]{:S(2)}) async-start(), calls=%async_computation | async-start | bytes 6082560 | tf_op jit(solution)/shard_map/all_gather | solution.py:505
  15.2 14.2 %collective-permute-start.3 = (bf16[128,384]{1,0:T(8,128)(2,1)S(1)}, bf16[128,384]{1,0:T(8,128)(2,1)S(1)}, u32[]{:S(2)}, u32[]{:S(2)}) collective-permute-start(bf16[128,384]{1,0:T(8,128)(2,1)S(1)} %constant_dynamic-update-slice_fusion), channel_id=1, source_target_pairs={{0,8},{8,0},{16,24},{24,16},{1,9},{9,1},{17,25},{25,17},{2,10},{10... | collective-permute-start | bytes 294920 | tf_op jit(solution)/shard_map/ppermute | solution.py:337
  18.3 11.2 %collective-permute-start.4 = (bf16[128,384]{1,0:T(8,128)(2,1)S(1)}, bf16[128,384]{1,0:T(8,128)(2,1)S(1)}, u32[]{:S(2)}, u32[]{:S(2)}) collective-permute-start(bf16[128,384]{1,0:T(8,128)(2,1)S(1)} %constant_dynamic-update-slice_fusion), channel_id=1, source_target_pairs={{0,16},{8,24},{16,0},{24,8},{1,17},{9,25},{17,1},{25,9},{2,18},{10... | collective-permute-start | bytes 294920 | tf_op jit(solution)/shard_map/ppermute | solution.py:337
  20.9 8.6 %collective-permute-start.5 = (bf16[128,384]{1,0:T(8,128)(2,1)S(1)}, bf16[128,384]{1,0:T(8,128)(2,1)S(1)}, u32[]{:S(2)}, u32[]{:S(2)}) collective-permute-start(bf16[128,384]{1,0:T(8,128)(2,1)S(1)} %constant_dynamic-update-slice_fusion), channel_id=1, source_target_pairs={{0,24},{8,16},{16,8},{24,0},{1,25},{9,17},{17,9},{25,1},{2,26},{10... | collective-permute-start | bytes 294920 | tf_op jit(solution)/shard_map/ppermute | solution.py:337
  23.0 33.6 %collective-permute-start = (bf16[256,768]{1,0:T(8,128)(2,1)}, bf16[256,768]{1,0:T(8,128)(2,1)S(1)}, u32[]{:S(2)}, u32[]{:S(2)}) collective-permute-start(bf16[256,768]{1,0:T(8,128)(2,1)} %get-tuple-element.290), channel_id=1, source_target_pairs={{0,0},{1,8},{2,2},{3,10},{4,4},{5,12},{6,6},{7,14},{8,16},{9,24},{... | collective-permute-start | bytes 1179656 | tf_op jit(solution)/shard_map/ppermute | solution.py:418
  24.8 32.7 %collective-permute-start.1 = (bf16[256,768]{1,0:T(8,128)(2,1)}, bf16[256,768]{1,0:T(8,128)(2,1)}, u32[]{:S(2)}, u32[]{:S(2)}) collective-permute-start(bf16[256,768]{1,0:T(8,128)(2,1)} %get-tuple-element.291), channel_id=1, source_target_pairs={{0,16},{1,24},{2,18},{3,26},{4,20},{5,28},{6,22},{7,30},{8,0},{9,8... | collective-permute-start | bytes 1179656 | tf_op jit(solution)/shard_map/ppermute | solution.py:419
  29.6 26.9 %copy-start.156 = (s32[32]{0:T(128)S(1)}, s32[32]{0:T(128)}, u32[]{:S(2)}) copy-start(s32[32]{0:T(128)} %constant.525.clone) | copy-start | bytes 388
  29.6 26.9 %copy-start.100 = (bf16[256,768]{1,0:T(8,128)(2,1)S(1)}, bf16[256,768]{1,0:T(8,128)(2,1)}, u32[]{:S(2)}) copy-start(bf16[256,768]{1,0:T(8,128)(2,1)} %get-tuple-element.286) | copy-start | bytes 1179652
  29.6 11.0 %collective-permute-start.6 = (bf16[4,128,384]{2,1,0:T(8,128)(2,1)S(1)}, bf16[4,128,384]{2,1,0:T(8,128)(2,1)S(1)}, u32[]{:S(2)}, u32[]{:S(2)}) collective-permute-start(bf16[4,128,384]{2,1,0:T(8,128)(2,1)S(1)} %pad_maximum_fusion.9), channel_id=1, source_target_pairs={{0,2},{1,3},{2,0},{3,1},{4,6},{5,7},{6,4},{7,5},{8,10},{9,11},{10,... | collective-permute-start | bytes 1179656 | tf_op jit(solution)/shard_map/ppermute | solution.py:337
  31.2 19.9 %collective-permute-start.7 = (bf16[4,128,384]{2,1,0:T(8,128)(2,1)S(1)}, bf16[4,128,384]{2,1,0:T(8,128)(2,1)S(1)}, u32[]{:S(2)}, u32[]{:S(2)}) collective-permute-start(bf16[4,128,384]{2,1,0:T(8,128)(2,1)S(1)} %pad_maximum_fusion.9), channel_id=1, source_target_pairs={{0,4},{1,5},{2,6},{3,7},{4,0},{5,1},{6,2},{7,3},{8,12},{9,13},{10,... | collective-permute-start | bytes 1179656 | tf_op jit(solution)/shard_map/ppermute | solution.py:337
  32.7 20.1 %collective-permute-start.8 = (bf16[4,128,384]{2,1,0:T(8,128)(2,1)S(1)}, bf16[4,128,384]{2,1,0:T(8,128)(2,1)S(1)}, u32[]{:S(2)}, u32[]{:S(2)}) collective-permute-start(bf16[4,128,384]{2,1,0:T(8,128)(2,1)S(1)} %pad_maximum_fusion.9), channel_id=1, source_target_pairs={{0,6},{1,7},{2,4},{3,5},{4,2},{5,3},{6,0},{7,1},{8,14},{9,15},{10,... | collective-permute-start | bytes 1179656 | tf_op jit(solution)/shard_map/ppermute | solution.py:337
  40.6 19.1 %collective-permute-start.10 = (f32[2,2]{1,0:T(2,128)S(1)}, f32[2,2]{1,0:T(2,128)S(1)}, u32[]{:S(2)}, u32[]{:S(2)}) collective-permute-start(f32[2,2]{1,0:T(2,128)S(1)} %add_convert_fusion.9), channel_id=1, source_target_pairs={{0,1},{1,0},{2,3},{3,2},{4,5},{5,4},{6,7},{7,6},{8,9},{9,8},{10,11... | collective-permute-start | bytes 56 | tf_op jit(solution)/shard_map/ppermute | solution.py:337
  51.0 12.0 %collective-permute-start.13 = (bf16[256,768]{1,0:T(8,128)(2,1)}, bf16[256,768]{1,0:T(8,128)(2,1)S(1)}, u32[]{:S(2)}, u32[]{:S(2)}) collective-permute-start(bf16[256,768]{1,0:T(8,128)(2,1)} %get-tuple-element.287), channel_id=1, source_target_pairs={{0,0},{1,8},{2,2},{3,10},{4,4},{5,12},{6,6},{7,14},{8,16},{9,24},{... | collective-permute-start | bytes 1179656 | tf_op jit(solution)/shard_map/ppermute | solution.py:418
  52.8 21.1 %copy-start.3 = (bf16[16,128,384]{2,1,0:T(8,128)(2,1)}, bf16[16,128,384]{2,1,0:T(8,128)(2,1)S(1)}, u32[]{:S(2)}) copy-start(bf16[16,128,384]{2,1,0:T(8,128)(2,1)S(1)} %constant_dynamic-update-slice_fusion.6.refs_0_) | copy-start | bytes 4718596
  52.8 25.1 %collective-permute-start.9 = (bf16[16,128,384]{2,1,0:T(8,128)(2,1)S(1)}, bf16[16,128,384]{2,1,0:T(8,128)(2,1)S(1)}, u32[]{:S(2)}, u32[]{:S(2)}) collective-permute-start(bf16[16,128,384]{2,1,0:T(8,128)(2,1)S(1)} %constant_dynamic-update-slice_fusion.6.refs_0_), channel_id=1, source_target_pairs={{0,1},{1,0},{2,3},{3,2},{4,5},{5,4},{6,7},{7,6},{8,9},{9,8},{10,11... | collective-permute-start | bytes 4718600 | tf_op jit(solution)/shard_map/ppermute | solution.py:337
  56.5 13.2 %collective-permute-start.14 = (bf16[256,768]{1,0:T(8,128)(2,1)S(1)}, bf16[256,768]{1,0:T(8,128)(2,1)S(1)}, u32[]{:S(2)}, u32[]{:S(2)}) collective-permute-start(bf16[256,768]{1,0:T(8,128)(2,1)S(1)} %copy-done.100), channel_id=1, source_target_pairs={{0,16},{1,24},{2,18},{3,26},{4,20},{5,28},{6,22},{7,30},{8,0},{9,8... | collective-permute-start | bytes 1179656 | tf_op jit(solution)/shard_map/ppermute | solution.py:419
  59.7 14.2 %collective-permute-start.2 = (bf16[512,768]{1,0:T(8,128)(2,1)}, bf16[512,768]{1,0:T(8,128)(2,1)}, u32[]{:S(2)}, u32[]{:S(2)}) collective-permute-start(bf16[512,768]{1,0:T(8,128)(2,1)} %maximum_select_fusion.2), channel_id=1, source_target_pairs={{0,1},{1,0},{2,3},{3,2},{4,5},{5,4},{6,7},{7,6},{8,9},{9,8},{10,11... | collective-permute-start | bytes 2359304 | tf_op jit(solution)/shard_map/ppermute | solution.py:337
  63.0 60.8 %copy-start.132 = (f32[1,512]{1,0:T(1,128)}, f32[1,512]{1,0:T(1,128)S(1)}, u32[]{:S(2)}) copy-start(f32[1,512]{1,0:T(1,128)S(1)} %get-tuple-element.336) | copy-start | bytes 6148
  87.0 44.1 %copy-start.114 = (f32[768]{0:T(1024)}, f32[768]{0:T(1024)S(1)}, u32[]{:S(2)}) copy-start(f32[768]{0:T(1024)S(1)} %mul.1156) | copy-start | bytes 9220
  88.3 42.9 %copy-start.112 = (f32[768]{0:T(1024)}, f32[768]{0:T(1024)S(1)}, u32[]{:S(2)}) copy-start(f32[768]{0:T(1024)S(1)} %mul.1178) | copy-start | bytes 9220
  123.8 15.0 %copy-start.29 = (f32[1,512,384]{2,1,0:T(8,128)}, f32[1,512,384]{2,1,0:T(8,128)S(1)}, u32[]{:S(2)}) copy-start(f32[1,512,384]{2,1,0:T(8,128)S(1)} %copy.111) | copy-start | bytes 2359300
  347.4 15.1 %copy-start.18 = (bf16[1,512,768]{2,1,0:T(8,128)(2,1)S(1)}, bf16[1,512,768]{2,1,0:T(8,128)(2,1)}, u32[]{:S(2)}) copy-start(bf16[1,512,768]{2,1,0:T(8,128)(2,1)} %copy-done.16) | copy-start | bytes 2359300
  349.4 67.3 %collective-permute-start.16 = (bf16[512,768]{1,0:T(8,128)(2,1)}, bf16[512,768]{1,0:T(8,128)(2,1)}, u32[]{:S(2)}, u32[]{:S(2)}) collective-permute-start(bf16[512,768]{1,0:T(8,128)(2,1)} %fusion.59), channel_id=1, source_target_pairs={{0,1},{1,0},{2,3},{3,2},{4,5},{5,4},{6,7},{7,6},{8,9},{9,8},{10,11... | collective-permute-start | bytes 2359304 | tf_op jit(solution)/shard_map/ppermute | solution.py:337
  406.3 7.5 %collective-permute-start.15 = (bf16[1,4,1152]{2,1,0:T(4,128)(2,1)S(1)}, bf16[1,4,1152]{2,1,0:T(4,128)(2,1)S(1)}, u32[]{:S(2)}, u32[]{:S(2)}) collective-permute-start(bf16[1,4,1152]{2,1,0:T(4,128)(2,1)S(1)} %fusion.111), channel_id=1, source_target_pairs={{0,1},{1,0},{2,3},{3,2},{4,5},{5,4},{6,7},{7,6},{8,9},{9,8},{10,11... | collective-permute-start | bytes 27656 | tf_op jit(solution)/shard_map/ppermute | solution.py:337
  431.9 18.4 %collective-permute-start.19 = (bf16[16,128,384]{2,1,0:T(8,128)(2,1)}, bf16[16,128,384]{2,1,0:T(8,128)(2,1)}, u32[]{:S(2)}, u32[]{:S(2)}) collective-permute-start(bf16[16,128,384]{2,1,0:T(8,128)(2,1)} %slice.1047), channel_id=1, source_target_pairs={{0,1},{1,0},{2,3},{3,2},{4,5},{5,4},{6,7},{7,6},{8,9},{9,8},{10,11... | collective-permute-start | bytes 4718600 | tf_op jit(solution)/shard_map/ppermute | solution.py:337
  445.8 32.7 %collective-permute-start.26 = (bf16[16,240,384]{2,1,0:T(8,128)(2,1)}, bf16[16,240,384]{2,1,0:T(8,128)(2,1)}, u32[]{:S(2)}, u32[]{:S(2)}) collective-permute-start(bf16[16,240,384]{2,1,0:T(8,128)(2,1)} %slice.1067), channel_id=1, source_target_pairs={{0,1},{1,0},{2,3},{3,2},{4,5},{5,4},{6,7},{7,6},{8,9},{9,8},{10,11... | collective-permute-start | bytes 8847368 | tf_op jit(solution)/shard_map/ppermute | solution.py:337
  447.1 37.1 %collective-permute-start.11 = (bf16[256,768]{1,0:T(8,128)(2,1)S(1)}, bf16[256,768]{1,0:T(8,128)(2,1)S(1)}, u32[]{:S(2)}, u32[]{:S(2)}) collective-permute-start(bf16[256,768]{1,0:T(8,128)(2,1)S(1)} %get-tuple-element.288), channel_id=1, source_target_pairs={{0,0},{8,1},{2,2},{10,3},{4,4},{12,5},{6,6},{14,7},{16,8},{24,9},{... | collective-permute-start | bytes 1179656 | tf_op jit(solution)/shard_map/ppermute | solution.py:428
  452.5 8.2 %collective-permute-start.20 = (bf16[4,128,384]{2,1,0:T(8,128)(2,1)S(1)}, bf16[4,128,384]{2,1,0:T(8,128)(2,1)S(1)}, u32[]{:S(2)}, u32[]{:S(2)}) collective-permute-start(bf16[4,128,384]{2,1,0:T(8,128)(2,1)S(1)} %get-tuple-element.278), channel_id=1, source_target_pairs={{0,2},{1,3},{2,0},{3,1},{4,6},{5,7},{6,4},{7,5},{8,10},{9,11},{10,... | collective-permute-start | bytes 1179656 | tf_op jit(solution)/shard_map/ppermute | solution.py:337
  452.6 14.8 %collective-permute-start.21 = (bf16[4,128,384]{2,1,0:T(8,128)(2,1)S(1)}, bf16[4,128,384]{2,1,0:T(8,128)(2,1)S(1)}, u32[]{:S(2)}, u32[]{:S(2)}) collective-permute-start(bf16[4,128,384]{2,1,0:T(8,128)(2,1)S(1)} %get-tuple-element.280), channel_id=1, source_target_pairs={{0,4},{1,5},{2,6},{3,7},{4,0},{5,1},{6,2},{7,3},{8,12},{9,13},{10,... | collective-permute-start | bytes 1179656 | tf_op jit(solution)/shard_map/ppermute | solution.py:337
  455.0 25.0 %slice-start = ((s8[5898240]{0:T(1024)(128)(4,1)}), s8[4194304]{0:T(1024)(128)(4,1)S(1)}, s32[]{:S(2)}) async-start(s8[5898240]{0:T(1024)(128)(4,1)} %bitcast.464), calls=%async_computation.1 | async-start | bytes 8388608
  455.0 25.1 %slice-start.1 = ((s8[5898240]{0:T(1024)(128)(4,1)}), s8[1703936]{0:T(1024)(128)(4,1)S(1)}, s32[]{:S(2)}) async-start(s8[5898240]{0:T(1024)(128)(4,1)} %bitcast.464), calls=%async_computation.2 | async-start | bytes 3407872
  455.0 16.4 %collective-permute-start.22 = (bf16[4,128,384]{2,1,0:T(8,128)(2,1)S(1)}, bf16[4,128,384]{2,1,0:T(8,128)(2,1)S(1)}, u32[]{:S(2)}, u32[]{:S(2)}) collective-permute-start(bf16[4,128,384]{2,1,0:T(8,128)(2,1)S(1)} %get-tuple-element.279), channel_id=1, source_target_pairs={{0,6},{1,7},{2,4},{3,5},{4,2},{5,3},{6,0},{7,1},{8,14},{9,15},{10,... | collective-permute-start | bytes 1179656 | tf_op jit(solution)/shard_map/ppermute | solution.py:337
  460.7 25.7 %collective-permute-start.12 = (bf16[256,768]{1,0:T(8,128)(2,1)S(1)}, bf16[256,768]{1,0:T(8,128)(2,1)S(1)}, u32[]{:S(2)}, u32[]{:S(2)}) collective-permute-start(bf16[256,768]{1,0:T(8,128)(2,1)S(1)} %get-tuple-element.289), channel_id=1, source_target_pairs={{16,0},{24,1},{18,2},{26,3},{20,4},{28,5},{22,6},{30,7},{0,8},{8,9... | collective-permute-start | bytes 1179656 | tf_op jit(solution)/shard_map/ppermute | solution.py:431
  467.3 21.0 %collective-permute-start.17 = (bf16[256,768]{1,0:T(8,128)(2,1)S(1)}, bf16[256,768]{1,0:T(8,128)(2,1)S(1)}, u32[]{:S(2)}, u32[]{:S(2)}) collective-permute-start(bf16[256,768]{1,0:T(8,128)(2,1)S(1)} %get-tuple-element.284), channel_id=1, source_target_pairs={{0,0},{8,1},{2,2},{10,3},{4,4},{12,5},{6,6},{14,7},{16,8},{24,9},{... | collective-permute-start | bytes 1179656 | tf_op jit(solution)/shard_map/ppermute | solution.py:428
  471.4 26.4 %collective-permute-start.18 = (bf16[256,768]{1,0:T(8,128)(2,1)S(1)}, bf16[256,768]{1,0:T(8,128)(2,1)S(1)}, u32[]{:S(2)}, u32[]{:S(2)}) collective-permute-start(bf16[256,768]{1,0:T(8,128)(2,1)S(1)} %get-tuple-element.285), channel_id=1, source_target_pairs={{16,0},{24,1},{18,2},{26,3},{20,4},{28,5},{22,6},{30,7},{0,8},{8,9... | collective-permute-start | bytes 1179656 | tf_op jit(solution)/shard_map/ppermute | solution.py:431
  478.5 19.3 %collective-permute-start.23 = (bf16[128,384]{1,0:T(8,128)(2,1)S(1)}, bf16[128,384]{1,0:T(8,128)(2,1)S(1)}, u32[]{:S(2)}, u32[]{:S(2)}) collective-permute-start(bf16[128,384]{1,0:T(8,128)(2,1)S(1)} %get-tuple-element.295), channel_id=1, source_target_pairs={{0,8},{8,0},{16,24},{24,16},{1,9},{9,1},{17,25},{25,17},{2,10},{10... | collective-permute-start | bytes 294920 | tf_op jit(solution)/shard_map/ppermute | solution.py:337
  484.2 23.3 %collective-permute-start.27 = (bf16[4,240,384]{2,1,0:T(8,128)(2,1)}, bf16[4,240,384]{2,1,0:T(8,128)(2,1)}, u32[]{:S(2)}, u32[]{:S(2)}) collective-permute-start(bf16[4,240,384]{2,1,0:T(8,128)(2,1)} %get-tuple-element.265), channel_id=1, source_target_pairs={{0,2},{1,3},{2,0},{3,1},{4,6},{5,7},{6,4},{7,5},{8,10},{9,11},{10,... | collective-permute-start | bytes 2211848 | tf_op jit(solution)/shard_map/ppermute | solution.py:337
  486.4 35.4 %collective-permute-start.28 = (bf16[4,240,384]{2,1,0:T(8,128)(2,1)}, bf16[4,240,384]{2,1,0:T(8,128)(2,1)}, u32[]{:S(2)}, u32[]{:S(2)}) collective-permute-start(bf16[4,240,384]{2,1,0:T(8,128)(2,1)} %get-tuple-element.267), channel_id=1, source_target_pairs={{0,4},{1,5},{2,6},{3,7},{4,0},{5,1},{6,2},{7,3},{8,12},{9,13},{10,... | collective-permute-start | bytes 2211848 | tf_op jit(solution)/shard_map/ppermute | solution.py:337
  488.3 33.5 %collective-permute-start.29 = (bf16[4,240,384]{2,1,0:T(8,128)(2,1)}, bf16[4,240,384]{2,1,0:T(8,128)(2,1)}, u32[]{:S(2)}, u32[]{:S(2)}) collective-permute-start(bf16[4,240,384]{2,1,0:T(8,128)(2,1)} %get-tuple-element.266), channel_id=1, source_target_pairs={{0,6},{1,7},{2,4},{3,5},{4,2},{5,3},{6,0},{7,1},{8,14},{9,15},{10,... | collective-permute-start | bytes 2211848 | tf_op jit(solution)/shard_map/ppermute | solution.py:337
  497.8 7.7 %collective-permute-start.24 = (bf16[128,384]{1,0:T(8,128)(2,1)S(1)}, bf16[128,384]{1,0:T(8,128)(2,1)S(1)}, u32[]{:S(2)}, u32[]{:S(2)}) collective-permute-start(bf16[128,384]{1,0:T(8,128)(2,1)S(1)} %get-tuple-element.297), channel_id=1, source_target_pairs={{0,16},{8,24},{16,0},{24,8},{1,17},{9,25},{17,1},{25,9},{2,18},{10... | collective-permute-start | bytes 294920 | tf_op jit(solution)/shard_map/ppermute | solution.py:337
  497.8 7.7 %collective-permute-start.25 = (bf16[128,384]{1,0:T(8,128)(2,1)S(1)}, bf16[128,384]{1,0:T(8,128)(2,1)S(1)}, u32[]{:S(2)}, u32[]{:S(2)}) collective-permute-start(bf16[128,384]{1,0:T(8,128)(2,1)S(1)} %get-tuple-element.296), channel_id=1, source_target_pairs={{0,24},{8,16},{16,8},{24,0},{1,25},{9,17},{17,9},{25,1},{2,26},{10... | collective-permute-start | bytes 294920 | tf_op jit(solution)/shard_map/ppermute | solution.py:337
  523.8 8.1 %collective-permute-start.30 = (bf16[240,384]{1,0:T(8,128)(2,1)S(1)}, bf16[240,384]{1,0:T(8,128)(2,1)S(1)}, u32[]{:S(2)}, u32[]{:S(2)}) collective-permute-start(bf16[240,384]{1,0:T(8,128)(2,1)S(1)} %get-tuple-element.292), channel_id=1, source_target_pairs={{0,8},{8,0},{16,24},{24,16},{1,9},{9,1},{17,25},{25,17},{2,10},{10... | collective-permute-start | bytes 552968 | tf_op jit(solution)/shard_map/ppermute | solution.py:337
  523.9 16.3 %collective-permute-start.31 = (bf16[240,384]{1,0:T(8,128)(2,1)S(1)}, bf16[240,384]{1,0:T(8,128)(2,1)S(1)}, u32[]{:S(2)}, u32[]{:S(2)}) collective-permute-start(bf16[240,384]{1,0:T(8,128)(2,1)S(1)} %get-tuple-element.294), channel_id=1, source_target_pairs={{0,16},{8,24},{16,0},{24,8},{1,17},{9,25},{17,1},{25,9},{2,18},{10... | collective-permute-start | bytes 552968 | tf_op jit(solution)/shard_map/ppermute | solution.py:337
  525.5 14.7 %collective-permute-start.32 = (bf16[240,384]{1,0:T(8,128)(2,1)S(1)}, bf16[240,384]{1,0:T(8,128)(2,1)S(1)}, u32[]{:S(2)}, u32[]{:S(2)}) collective-permute-start(bf16[240,384]{1,0:T(8,128)(2,1)S(1)} %get-tuple-element.293), channel_id=1, source_target_pairs={{0,24},{8,16},{16,8},{24,0},{1,25},{9,17},{17,9},{25,1},{2,26},{10... | collective-permute-start | bytes 552968 | tf_op jit(solution)/shard_map/ppermute | solution.py:337
  (153 other events, 557.1 us)
Sparse Core Ops, SparseCore 0:
  27.9 83.4 all-gather.2

commit v2 on v1

v2 whole, which is shorter than its diff:
```python
import functools

import jax
import jax.numpy as jnp
import numpy as np
from jax import lax
from jax.experimental import pallas as pl
from jax.experimental.pallas import tpu as pltpu
from jax.sharding import PartitionSpec as P

HEADS = 6
HEAD_DIM = 64
KERNEL = 9
GROUPS = 2
LEN = 1024
HALF = LEN // 2
WIDTH = 768
WIDE = HEADS * HEAD_DIM
CHUNK = 128
EDGE = 16
WINDOW = HALF + 2 * EDGE
BLOCKS = 32
HIDDEN = 48
PACK = 240

F32 = jnp.float32
BF16 = jnp.bfloat16

inv_root_two = 0.7071067811865476
inv_root_tau = 0.3989422804014327


def nn(a, b):
    return jnp.dot(a, b, preferred_element_type=F32)


def nt(a, b):
    return lax.dot_general(a, b, (((1,), (1,)), ((), ())), preferred_element_type=F32)


def tn(a, b):
    return lax.dot_general(a, b, (((0,), (0,)), ((), ())), preferred_element_type=F32)


def call(kernel, out_shape, args, scalars=1, scratch=(), flops=0):
    vmem = pl.BlockSpec(memory_space=pltpu.VMEM)
    return pl.pallas_call(
        kernel,
        out_shape=out_shape,
        in_specs=[pl.BlockSpec(memory_space=pltpu.SMEM)] * scalars
        + [vmem] * (len(args) - scalars),
        out_specs=jax.tree.map(lambda _: vmem, out_shape),
        scratch_shapes=list(scratch),
        compiler_params=pltpu.CompilerParams(vmem_limit_bytes=56 * 1024 * 1024),
        cost_estimate=pl.CostEstimate(flops=flops, bytes_accessed=0, transcendentals=0),
    )(*args)


def shape(dims, dtype):
    return jax.ShapeDtypeStruct(dims, dtype)


def lane(rows):
    return lax.broadcasted_iota(jnp.int32, (rows, CHUNK), 1)


def load_window(core, source, target, chunks):
    value = source(pl.ds(pl.multiple_of(core * (HALF - EDGE), EDGE), HALF + EDGE))
    start = pl.multiple_of(EDGE - core * EDGE, EDGE)
    edge = pl.multiple_of(core * (HALF + EDGE), EDGE)
    for c in range(chunks):
        target[c, pl.ds(edge, EDGE), :] = jnp.zeros((EDGE, CHUNK), F32)
        target[c, pl.ds(start, HALF + EDGE), :] = value[:, c * CHUNK : (c + 1) * CHUNK].astype(F32)


def weight(own, other, index):
    rows = slice(index * WIDE, (index + 1) * WIDE)
    return own[rows, :], other[rows, :]


def project(tokens, own, other, index):
    first, second = weight(own, other, index)
    return nn(tokens[:, :WIDE], first) + nn(tokens[:, WIDE:], second)


def fill_masks(info, masks):
    sep, valid, core = info[1], info[0], info[2]

    def segment(position):
        return jnp.where(position < sep, 0, jnp.where(position < valid, 1, 2))

    row = core * HALF + lax.broadcasted_iota(jnp.int32, (HALF, CHUNK), 0)
    own = segment(row)
    for j in range(KERNEL):
        masks[j] = (segment(row + (j - 4)) == own).astype(F32)


def permute_kernel(tokens, matrix, out):
    out[...] = nn(tokens[...], matrix[...]).astype(BF16)


def attend_kernel(info, tokens, own, other, q_out, k_out, v_out, att_out, stat_out):
    core, valid = info[2], info[0]
    mine = tokens[pl.ds(pl.multiple_of(core * HALF, HALF), HALF), :]
    q_out[...] = project(mine, own, other, 0).astype(BF16)
    k_out[...] = project(tokens[...], own, other, 1).astype(BF16)
    v_out[...] = project(tokens[...], own, other, 2).astype(BF16)
    rows = 256
    bias = jnp.where(
        lax.broadcasted_iota(jnp.int32, (1, LEN), 1) < valid, 0.0, -1e30
    ).astype(F32)
    for block in range(HALF // rows):
        at = slice(block * rows, (block + 1) * rows)
        stats = jnp.zeros((rows, CHUNK), F32)
        for pair in range(HEADS // 2):
            cols = slice(pair * CHUNK, (pair + 1) * CHUNK)
            q = q_out[at, cols] * BF16(0.125)
            k, v = k_out[:, cols], v_out[:, cols]
            results = []
            for head in range(2):
                keep = (lane(rows) < HEAD_DIM) == (head == 0)
                scores = nt(jnp.where(keep, q, BF16(0)), k) + bias
                peak = jnp.max(scores, -1, keepdims=True)
                exponent = jnp.exp(scores - peak)
                total = jnp.sum(exponent, -1, keepdims=True)
                results.append(nn(exponent.astype(BF16), v) / total)
                stats = jnp.where(
                    lane(rows) == 2 * pair + head, peak + jnp.log(total), stats
                )
            att_out[at, cols] = jnp.where(lane(rows) < HEAD_DIM, *results).astype(BF16)
        stat_out[at, :] = stats


def spread(j):
    row = lax.broadcasted_iota(jnp.int32, (CHUNK, WIDE), 0)
    col = lax.broadcasted_iota(jnp.int32, (CHUNK, WIDE), 1)
    return (row == (col >> 6) * KERNEL + j).astype(F32).astype(BF16)


def conv_kernel(
    info,
    tokens,
    own,
    other,
    q,
    att,
    taps_weight,
    depth_weight,
    context,
    key_out,
    attn_out,
    depth_out,
    values_out,
    spread_out,
    window,
    logits,
    masks,
):
    core = info[2]
    load_window(core, lambda rows: tokens[rows, :], window, WIDTH // CHUNK)
    fill_masks(info, masks)
    rows = 64
    for c in range(WIDTH // CHUNK):
        cols = slice(c * CHUNK, (c + 1) * CHUNK)
        for b in range(HALF // rows):
            total = jnp.zeros((rows, CHUNK), F32)
            for j in range(KERNEL):
                first = EDGE - 4 + b * rows + j
                total = total + depth_weight[j : j + 1, cols] * window[c, first : first + rows, :]
            depth_out[b * rows : (b + 1) * rows, cols] = total.astype(BF16)
    key_conv = project(depth_out[...], own, other, 3)
    key_out[...] = key_conv
    attn_out[...] = (key_conv * q[...].astype(F32)).astype(BF16)
    load_window(
        core, lambda rows: project(tokens[rows, :], own, other, 4), values_out, WIDE // CHUNK
    )
    for j in range(KERNEL):
        spread_out[j] = nn(taps_weight[...], spread(j)).astype(BF16)
        logits[j] = nn(attn_out[...], spread_out[j])
    context[:, :WIDE] = att[...]
    for b in range(HALF // rows):
        at = slice(b * rows, (b + 1) * rows)
        for c in range(WIDE // CHUNK):
            cols = slice(c * CHUNK, (c + 1) * CHUNK)
            peak = logits[0, at, cols]
            for j in range(1, KERNEL):
                peak = jnp.maximum(peak, logits[j, at, cols])
            total = jnp.zeros((rows, CHUNK), F32)
            result = jnp.zeros((rows, CHUNK), F32)
            for j in range(KERNEL):
                first = EDGE - 4 + b * rows + j
                exponent = jnp.exp(logits[j, at, cols] - peak)
                total = total + exponent
                result = result + exponent * masks[j, at, :] * values_out[
                    c, first : first + rows, :
                ]
            context[at, WIDE + c * CHUNK : WIDE + (c + 1) * CHUNK] = (result / total).astype(BF16)


def normalize(value):
    centred = value - jnp.mean(value, -1, keepdims=True)
    inv = lax.rsqrt(jnp.mean(centred * centred, -1, keepdims=True) + 1e-06)
    return centred * inv, inv


def normalize_back(grad, normed, inv, gain):
    e = grad * gain
    return inv * (
        e - jnp.mean(e, -1, keepdims=True) - normed * jnp.mean(e * normed, -1, keepdims=True)
    )


def feed_kernel(
    order,
    context,
    tokens,
    late,
    cotangent,
    gains,
    matrix,
    layer_out,
    first_out,
    context_grad,
    kept,
    sent,
    small_out,
    out_weight,
    up,
    down,
    act,
    slope,
    normed,
    attn,
    attn_low,
    grad_low,
    branch_low,
    second,
    scale,
):
    rows = 128
    steps = [slice(i * rows, (i + 1) * rows) for i in range(HALF // rows)]
    gain_attn, shift_attn = gains[0:1, :], gains[1:2, :]
    gain_out, shift_out = gains[2:3, :], gains[3:4, :]
    for i in range(BLOCKS // 2):
        sides = [late[2 * i + k, 0:HIDDEN, :].astype(F32) for k in range(2)]
        out_weight[i * HIDDEN : (i + 1) * HIDDEN, :] = jnp.concatenate(
            [jnp.concatenate([s[: HIDDEN // 2], s[HIDDEN // 2 :]], 1) for s in sides], 0
        ).astype(BF16)
    for h in range(2):
        for i in range(BLOCKS // 2):
            source = order[h * (BLOCKS // 2) + i]
            for g in range(GROUPS):
                at = slice(i * HIDDEN, (i + 1) * HIDDEN)
                up[g, h, at, :] = late[source, (1 + g) * HIDDEN : (2 + g) * HIDDEN, :]
                down[g, h, at, :] = late[source, (3 + g) * HIDDEN : (4 + g) * HIDDEN, :]
    for at in steps:
        branch = nn(context[at, :], out_weight[...]) + tokens[at, :].astype(F32)
        n, inv = normalize(branch)
        normed[at, :] = n
        scale[at, :] = inv
        value = n * gain_attn + shift_attn
        attn[at, :] = value
        attn_low[at, :] = value.astype(BF16)
    for g in range(GROUPS):
        part = slice(g * WIDE, (g + 1) * WIDE)
        for h in range(2):
            for at in steps:
                pre = nt(attn_low[at, part], up[g, h])
                cdf = 0.5 * (1.0 + lax.erf(pre * inv_root_two))
                act[g, h, at, :] = (pre * cdf).astype(BF16)
                slope[g, h, at, :] = cdf + pre * jnp.exp(-0.5 * pre * pre) * inv_root_tau
    gain_grad = jnp.zeros((1, WIDTH), F32)
    shift_grad = jnp.zeros((1, WIDTH), F32)
    for at in steps:
        value = attn[at, :] + jnp.concatenate(
            [
                nn(act[g, 0, at, :], down[g, 0]) + nn(act[g, 1, at, :], down[g, 1])
                for g in range(GROUPS)
            ],
            1,
        )
        n, inv = normalize(value)
        layer_out[at, :] = (n * gain_out + shift_out).astype(BF16)
        grad = cotangent[at, :].astype(F32)
        gain_grad = gain_grad + jnp.sum(grad * n, 0, keepdims=True)
        shift_grad = shift_grad + jnp.sum(grad, 0, keepdims=True)
        value = normalize_back(grad, n, inv, gain_out)
        second[at, :] = value
        grad_low[at, :] = value.astype(BF16)
    small_out[2:3, :] = gain_grad
    small_out[3:4, :] = shift_grad
    for g in range(GROUPS):
        part = slice(g * WIDE, (g + 1) * WIDE)
        for h in range(2):
            target = (kept, sent)[h]
            result = tn(act[g, h], grad_low[:, part]).astype(BF16)
            for i in range(BLOCKS // 2):
                target[i, (3 + g) * HIDDEN : (4 + g) * HIDDEN, :] = result[
                    i * HIDDEN : (i + 1) * HIDDEN
                ]
            for at in steps:
                act[g, h, at, :] = (
                    nt(grad_low[at, part], down[g, h]) * slope[g, h, at, :]
                ).astype(BF16)
            result = tn(act[g, h], attn_low[:, part]).astype(BF16)
            for i in range(BLOCKS // 2):
                target[i, (1 + g) * HIDDEN : (2 + g) * HIDDEN, :] = result[
                    i * HIDDEN : (i + 1) * HIDDEN
                ]
    gain_grad = jnp.zeros((1, WIDTH), F32)
    shift_grad = jnp.zeros((1, WIDTH), F32)
    for at in steps:
        grad = second[at, :] + jnp.concatenate(
            [nn(act[g, 0, at, :], up[g, 0]) + nn(act[g, 1, at, :], up[g, 1]) for g in range(GROUPS)],
            1,
        )
        n = normed[at, :]
        gain_grad = gain_grad + jnp.sum(grad * n, 0, keepdims=True)
        shift_grad = shift_grad + jnp.sum(grad, 0, keepdims=True)
        value = normalize_back(grad, n, scale[at, :], gain_attn)
        first_out[at, :] = value
        branch_low[at, :] = value.astype(BF16)
        context_grad[at, :] = nt(branch_low[at, :], out_weight[...]).astype(BF16)
        grad_low[at, :] = nn(context[at, :], matrix[...]).astype(BF16)
    small_out[0:1, :] = gain_grad
    small_out[1:2, :] = shift_grad
    small_out[4:8, :] = jnp.zeros((4, WIDTH), F32)
    for h in range(2):
        result = tn(grad_low[:, h * WIDE : (h + 1) * WIDE], branch_low[...])
        for i in range(BLOCKS // 2):
            piece = result[i * (HIDDEN // 2) : (i + 1) * (HIDDEN // 2)]
            (kept, sent)[h][i, 0:HIDDEN, :] = jnp.concatenate(
                [piece[:, :WIDE], piece[:, WIDE:]], 0
            ).astype(BF16)


def conv_back_kernel(
    info,
    tokens,
    own,
    other,
    q,
    context_grad,
    key_conv,
    conv_attn,
    depth_low,
    values,
    spreads,
    taps_weight,
    depth_weight,
    query_out,
    point_out,
    kernel_out,
    depth_grad,
    values_grad,
    input_grad,
    rim_out,
    window,
    logits,
    masks,
    sums,
    pads,
    depth_back,
    compact,
):
    core = info[2]
    load_window(core, lambda rows: tokens[rows, :], window, WIDTH // CHUNK)
    fill_masks(info, masks)
    rows = 64
    steps = [slice(i * rows, (i + 1) * rows) for i in range(HALF // rows)]
    block = (lax.broadcasted_iota(jnp.int32, (CHUNK, CHUNK), 0) >> 6) == (
        lax.broadcasted_iota(jnp.int32, (CHUNK, CHUNK), 1) >> 6
    )
    ones = block.astype(F32).astype(BF16)
    pick_row = lax.broadcasted_iota(jnp.int32, (CHUNK, CHUNK), 0)
    pick_col = lax.broadcasted_iota(jnp.int32, (CHUNK, CHUNK), 1)
    for j in range(KERNEL):
        logits[j] = nn(conv_attn[...], spreads[j])
        pads[j, 0:EDGE, :] = jnp.zeros((EDGE, CHUNK), F32)
        pads[j, HALF + EDGE : WINDOW, :] = jnp.zeros((EDGE, CHUNK), F32)
    total_compact = jnp.zeros((HALF, CHUNK), F32)
    for c in range(WIDE // CHUNK):
        cols = slice(c * CHUNK, (c + 1) * CHUNK)
        grad_cols = slice(WIDE + c * CHUNK, WIDE + (c + 1) * CHUNK)
        for j in range(KERNEL):
            product = (
                context_grad[:, grad_cols].astype(F32)
                * values[c, EDGE - 4 + j : EDGE - 4 + j + HALF, :]
            )
            sums[j] = nn(product.astype(BF16), ones)
        for b, at in enumerate(steps):
            grad = context_grad[at, grad_cols].astype(F32)
            peak = logits[0, at, cols]
            for j in range(1, KERNEL):
                peak = jnp.maximum(peak, logits[j, at, cols])
            total = jnp.zeros((rows, CHUNK), F32)
            dot = jnp.zeros((rows, CHUNK), F32)
            for j in range(KERNEL):
                exponent = jnp.exp(logits[j, at, cols] - peak)
                mask = masks[j, at, :]
                logits[j, at, cols] = exponent
                change = sums[j, at, :] * mask
                sums[j, at, :] = change
                total = total + exponent
                dot = dot + exponent * change
            inv = 1.0 / total
            dot = dot * inv
            inside = slice(EDGE + b * rows, EDGE + (b + 1) * rows)
            for j in range(KERNEL):
                tap = logits[j, at, cols] * inv
                pads[j, inside, :] = tap * masks[j, at, :] * grad
                compact[j, at, :] = (tap * (sums[j, at, :] - dot)).astype(BF16)
        for j in range(KERNEL):
            pick = (pick_row & 63 == 0) & (pick_col == (2 * c + (pick_row >> 6)) * KERNEL + j)
            total_compact = total_compact + nn(compact[j], pick.astype(F32).astype(BF16))
        for b in range(WINDOW // 32):
            total = jnp.zeros((32, CHUNK), F32)
            for j in range(KERNEL):
                first = b * 32 + 4 - j
                low, high = max(first, 0), min(first + 32, WINDOW)
                piece = pads[j, low:high, :]
                if high - low < 32:
                    zero = jnp.zeros((32 - (high - low), CHUNK), F32)
                    piece = jnp.concatenate([zero, piece] if low > first else [piece, zero], 0)
                total = total + piece
            values_grad[c, b * 32 : (b + 1) * 32, :] = total
    compact_low = total_compact.astype(BF16)
    kernel_out[...] = tn(conv_attn[...], compact_low)
    attn_grad = nt(compact_low, taps_weight[...])
    query_out[...] = attn_grad * key_conv[...]
    key_low = (attn_grad * q[...].astype(F32)).astype(BF16)
    point_out[...] = tn(depth_low[...], key_low)
    depth_grad[...] = jnp.zeros((16, WIDTH), F32)
    for side, rows_weight in enumerate(weight(own, other, 3)):
        back = nt(key_low, rows_weight)
        for k in range(WIDE // CHUNK):
            c = side * (WIDE // CHUNK) + k
            depth_back[0:EDGE, :] = jnp.zeros((EDGE, CHUNK), F32)
            depth_back[HALF + EDGE : WINDOW, :] = jnp.zeros((EDGE, CHUNK), F32)
            depth_back[EDGE : HALF + EDGE, :] = back[:, k * CHUNK : (k + 1) * CHUNK]
            cols = slice(c * CHUNK, (c + 1) * CHUNK)
            totals = [jnp.zeros((8, CHUNK), F32) for _ in range(KERNEL)]
            for b in range(HALF // 32):
                grad = depth_back[EDGE + b * 32 : EDGE + (b + 1) * 32, :]
                for j in range(KERNEL):
                    first = EDGE - 4 + b * 32 + j
                    product = grad * window[c, first : first + 32, :]
                    totals[j] = totals[j] + (
                        (product[0:8] + product[8:16]) + (product[16:24] + product[24:32])
                    )
            for j in range(KERNEL):
                depth_grad[j : j + 1, cols] = jnp.sum(totals[j], 0, keepdims=True)
            for b in range(WINDOW // 32):
                total = jnp.zeros((32, CHUNK), F32)
                for j in range(KERNEL):
                    first = b * 32 + 4 - j
                    low, high = max(first, 0), min(first + 32, WINDOW)
                    piece = depth_back[low:high, :]
                    if high - low < 32:
                        zero = jnp.zeros((32 - (high - low), CHUNK), F32)
                        piece = jnp.concatenate([zero, piece] if low > first else [piece, zero], 0)
                    total = total + depth_weight[j : j + 1, cols] * piece
                input_grad[c, b * 32 : (b + 1) * 32, :] = total
    rim = pl.multiple_of((1 - core) * (HALF + EDGE), EDGE)
    rim_out[...] = jnp.zeros((2 * EDGE, WIDTH), BF16)
    for c in range(WIDTH // CHUNK):
        turned = (c + WIDE // CHUNK) % (WIDTH // CHUNK)
        rim_out[0:EDGE, turned * CHUNK : (turned + 1) * CHUNK] = input_grad[
            c, pl.ds(rim, EDGE), :
        ].astype(BF16)
    for c in range(WIDE // CHUNK):
        rim_out[EDGE : 2 * EDGE, c * CHUNK : (c + 1) * CHUNK] = values_grad[
            c, pl.ds(rim, EDGE), :
        ].astype(BF16)


def attend_back_kernel(
    info, q, k, v, context, context_grad, stats, rim, query_out, own_out, message, key_sum, value_sum
):
    core, valid = info[2], info[0]
    rows = 256
    live = lax.broadcasted_iota(jnp.int32, (LEN, CHUNK), 0) < valid
    for pair in range(HEADS // 2):
        cols = slice(pair * CHUNK, (pair + 1) * CHUNK)
        keys, vals = k[:, cols], v[:, cols]
        for head in range(2):
            even = head == 0
            base = HEAD_DIM if even else 0
            key_lane = lane(LEN)
            keep_key = (key_lane < HEAD_DIM) == even
            keys_more = jnp.where(
                keep_key,
                keys.astype(F32),
                jnp.where(
                    key_lane == base,
                    jnp.where(live, 0.0, -1e30),
                    jnp.where(key_lane < base + 4, 1.0, 0.0),
                ),
            ).astype(BF16)
            vals_more = jnp.where(
                keep_key, vals.astype(F32), jnp.where(key_lane < base + 3, 1.0, 0.0)
            ).astype(BF16)
            keys_turned = keys_more.T
            for block in range(HALF // rows):
                at = slice(block * rows, (block + 1) * rows)
                here = lane(rows)
                keep = (here < HEAD_DIM) == even

                def three(value):
                    high = value.astype(BF16).astype(F32)
                    middle = (value - high).astype(BF16).astype(F32)
                    return high, middle, value - high - middle

                grad = context_grad[at, cols].astype(F32)
                product = jnp.where(keep, grad * context[at, cols].astype(F32), 0.0)
                dots = three(-jnp.sum(product, -1, keepdims=True))
                stat = three(-stats[at, 2 * pair + head : 2 * pair + head + 1])
                grad_more = jnp.where(
                    keep,
                    grad,
                    jnp.where(
                        here == base,
                        dots[0],
                        jnp.where(
                            here == base + 1, dots[1], jnp.where(here == base + 2, dots[2], 0.0)
                        ),
                    ),
                ).astype(BF16)
                query_more = jnp.where(
                    keep,
                    q[at, cols].astype(F32) * 0.125,
                    jnp.where(
                        here == base,
                        1.0,
                        jnp.where(
                            here == base + 1,
                            stat[0],
                            jnp.where(
                                here == base + 2, stat[1], jnp.where(here == base + 3, stat[2], 0.0)
                            ),
                        ),
                    ),
                ).astype(BF16)
                probs = jnp.exp(nt(keys_more, query_more))
                change = (probs * nt(vals_more, grad_more)).astype(BF16)
                value_part = nn(probs.astype(BF16), grad_more)
                key_part = nn(change, query_more)
                query_part = nn(keys_turned, change).T * 0.125
                if block == 0:
                    value_total, key_total = value_part, key_part
                else:
                    value_total, key_total = value_total + value_part, key_total + key_part
                if even:
                    query_out[at, cols] = query_part
                else:
                    query_out[at, cols] = jnp.where(keep, query_part, query_out[at, cols])
            if even:
                key_sum[:, cols] = key_total
                value_sum[:, cols] = value_total
            else:
                key_sum[:, cols] = jnp.where(keep_key, key_total, key_sum[:, cols])
                value_sum[:, cols] = jnp.where(keep_key, value_total, value_sum[:, cols])
    mine = pl.ds(pl.multiple_of(core * HALF, HALF), HALF)
    theirs = pl.ds(pl.multiple_of((1 - core) * HALF, HALF), HALF)
    own_out[:, :WIDE] = key_sum[mine, :]
    own_out[:, WIDE:] = value_sum[mine, :]
    message[0:HALF, :WIDE] = key_sum[theirs, :].astype(BF16)
    message[0:HALF, WIDE:] = value_sum[theirs, :].astype(BF16)
    message[HALF:WINDOW, :] = rim[...]


def finish_kernel(
    info,
    tokens,
    own,
    other,
    matrix,
    query_attn,
    query_conv,
    own_part,
    arrived,
    values_grad,
    input_grad,
    point_grad,
    small,
    first_grad,
    kept,
    sent,
    x_grad,
    values_sum,
    inputs,
):
    core = info[2]
    query_low = (query_attn[...] + query_conv[...]).astype(BF16)
    both = own_part[...] + arrived[0:HALF, :].astype(F32)
    key_low = both[:, :WIDE].astype(BF16)
    value_low = both[:, WIDE:].astype(BF16)
    rim = pl.ds(pl.multiple_of((1 - core) * (HALF - EDGE), EDGE), EDGE)
    inside = slice(EDGE, EDGE + HALF)
    for c in range(WIDE // CHUNK):
        cols = slice(c * CHUNK, (c + 1) * CHUNK)
        values_sum[:, cols] = values_grad[c, inside, :]
    for c in range(WIDTH // CHUNK):
        cols = slice(c * CHUNK, (c + 1) * CHUNK)
        inputs[:, cols] = input_grad[c, inside, :]
    inputs[rim, :] = inputs[rim, :] + arrived[HALF : HALF + EDGE, :].astype(F32)
    values_sum[rim, :] = values_sum[rim, :] + arrived[HALF + EDGE : WINDOW, :WIDE].astype(F32)
    values_low = values_sum[...].astype(BF16)
    mine = tokens[pl.ds(pl.multiple_of(core * HALF, HALF), HALF), :]
    grads = [query_low, key_low, value_low, None, values_low]
    unit = HIDDEN // 2
    for h in range(2):
        part = mine[:, h * WIDE : (h + 1) * WIDE]
        results = [
            point_grad[h * WIDE : (h + 1) * WIDE, :] if g is None else tn(part, g) for g in grads
        ]
        target = (kept, sent)[h]
        for i in range(BLOCKS // 2):
            at = slice(i * unit, (i + 1) * unit)
            target[i, 0:48, :] = jnp.concatenate([results[0][at], results[1][at]], 0).astype(BF16)
            target[i, 48:96, :] = jnp.concatenate([results[2][at], results[3][at]], 0).astype(BF16)
            target[i, 96:128, :] = jnp.concatenate(
                [results[4][at], small[h * (BLOCKS // 2) + i]], 0
            ).astype(BF16)
        rows = (own, other)[h]
        total = inputs[:, h * WIDE : (h + 1) * WIDE]
        for index, g in enumerate(grads):
            if g is not None:
                total = total + nt(g, rows[index * WIDE : (index + 1) * WIDE, :])
        inputs[:, h * WIDE : (h + 1) * WIDE] = total
    x_grad[...] = (nt(inputs[...].astype(BF16), matrix[...]) + first_grad[...]).astype(BF16)


def dp_groups(count):
    masks = []
    bit = 2
    while bit < count:
        if bit * 2 < count:
            masks.append((bit, 2 * bit, 3 * bit))
            bit *= 4
        else:
            masks.append((bit,))
            bit *= 2
    return masks


def swap(x, axis, mask):
    count = lax.axis_size(axis)
    return lax.ppermute(x, axis, [(i, i ^ mask) for i in range(count)])


def relative_codes():
    seq, dp = lax.axis_size("seq"), lax.axis_size("dp")
    codes = [j * dp for j in range(seq)]
    for masks in dp_groups(dp):
        codes = [c ^ m for m in (0,) + masks for c in codes]
    return codes + [c ^ 1 for c in codes]


def add_up(parts):
    total = parts[0].astype(jnp.float32)
    for part in parts[1:]:
        total = total + part.astype(jnp.float32)
    return total


def scatter_relative(kept, sent):
    seq, dp = lax.axis_size("seq"), lax.axis_size("dp")
    held = add_up([kept, swap(sent, "dp", 1)]).astype(jnp.bfloat16)
    for masks in reversed(dp_groups(dp)):
        held = held.reshape((len(masks) + 1, -1) + held.shape[1:])
        parts = [held[0]] + [swap(held[i + 1], "dp", m) for i, m in enumerate(masks)]
        held = add_up(parts).astype(jnp.bfloat16)
    return add_up([held[0]] + [swap(held[j], "seq", j) for j in range(1, seq)])


def token_perms():
    seq, dp = lax.axis_size("seq"), lax.axis_size("dp")
    first, second = [], []
    for z in range(seq):
        for d in range(dp):
            core, rest = d & 1, d & ~1
            odd = z & 1
            first.append((z * dp + d, (2 * odd + core) * dp + rest + (z >> 1)))
            second.append((z * dp + d, (2 * (1 - odd) + core) * dp + rest + (z >> 1)))
    return first, second


def to_rows(x):
    first, second = token_perms()
    z = lax.axis_index("seq")
    odd, high = z & 1, z >> 1
    a = lax.ppermute(lax.dynamic_index_in_dim(x, odd, 0, False), ("seq", "dp"), first)
    b = lax.ppermute(lax.dynamic_index_in_dim(x, 1 - odd, 0, False), ("seq", "dp"), second)
    return jnp.where(high == 0, jnp.concatenate([a, b]), jnp.concatenate([b, a]))


def from_rows(x):
    first, second = token_perms()
    z = lax.axis_index("seq")
    odd, high = z & 1, z >> 1
    half = x.reshape(2, x.shape[0] // 2, x.shape[1])
    a = lax.ppermute(
        lax.dynamic_index_in_dim(half, high, 0, False), ("seq", "dp"), [(t, s) for s, t in first]
    )
    b = lax.ppermute(
        lax.dynamic_index_in_dim(half, 1 - high, 0, False),
        ("seq", "dp"),
        [(t, s) for s, t in second],
    )
    return jnp.where(odd == 0, jnp.stack([a, b]), jnp.stack([b, a]))


def pad_rows(x, multiple):
    return jnp.pad(x, ((0, -x.shape[0] % multiple), (0, 0)))


def merge(packs, rows):
    cut = packs[0].shape[0] // (5 * rows + 8) * (5 * rows)
    weights = jnp.concatenate([p[:cut].reshape(5, -1, WIDE) for p in packs], 1)
    return jnp.concatenate([weights.reshape(-1, WIDE)] + [p[cut:] for p in packs])


def gather_weights(pack, rows):
    held = merge([pack] + [swap(pack, "seq", j) for j in range(1, lax.axis_size("seq"))], rows)
    for masks in dp_groups(lax.axis_size("dp")):
        held = merge([held] + [swap(held, "dp", m) for m in masks], rows)
    return held, swap(held, "dp", 1)


def to_lines(x):
    return jnp.pad(x, (0, -x.shape[0] % WIDE)).reshape(-1, WIDE)


def to_block(x):
    return jnp.pad(x, ((0, 0), (0, -x.shape[1] % WIDE)))


def regroup(late_all, order, rows, hidden):
    count = late_all.shape[0]
    relative = jnp.take(late_all, order, axis=0)

    def out_rows(first):
        return late_all[:, first : first + rows].reshape(BLOCKS, HIDDEN // 2, WIDE)

    def units(first):
        return relative[:, first : first + hidden].reshape(BLOCKS, HIDDEN, WIDE)

    parts = [out_rows(0), out_rows(rows)]
    parts += [units(2 * rows + i * hidden) for i in range(2 * GROUPS)]
    return jnp.concatenate(parts, 1), jnp.arange(BLOCKS, dtype=jnp.int32)


def split_late(packs, rows, hidden):
    cuts = [0, HIDDEN // 2] + [HIDDEN * i for i in range(1, 2 * GROUPS + 2)]
    sizes = [rows, rows] + [hidden] * (2 * GROUPS)
    parts = [
        packs[:, cuts[i] : cuts[i + 1]].reshape(-1, sizes[i], WIDE) for i in range(len(sizes))
    ]
    whole = jnp.concatenate(parts, 1)
    return jnp.pad(whole, ((0, 0), (0, -whole.shape[1] % 16), (0, 0)))


def split_early(packs, small, rows):
    parts = [packs[:, 24 * i : 24 * (i + 1)].reshape(-1, rows, WIDE) for i in range(5)]
    return jnp.concatenate(parts + [small.astype(BF16)], 1)


def local(
    layer_in,
    cotangent,
    valid_len,
    sep_pos,
    w_query,
    w_key,
    w_value,
    w_depth,
    w_point,
    w_kernel,
    w_convout,
    w_output,
    gain_attn,
    shift_attn,
    w_up,
    w_down,
    gain_out,
    shift_out,
):
    seq, dp = lax.axis_size("seq"), lax.axis_size("dp")
    count = seq * dp
    z, d = lax.axis_index("seq"), lax.axis_index("dp")
    core = d & 1
    me = z * dp + d
    codes = np.array(relative_codes(), np.int32)
    order = jnp.asarray(codes) ^ me
    to_absolute = (jnp.arange(count)[:, None] == order[None, :]).astype(BF16)
    rows = w_query.shape[0]
    hidden = w_up.shape[2]
    half = count // 2
    features = (order[:, None] * rows + jnp.arange(rows)[None, :]).reshape(1, WIDTH)
    matrix = (jnp.arange(WIDTH)[:, None] == features).astype(BF16)

    tokens_own = to_rows(layer_in[:, 0])
    lines = [
        to_lines(w_kernel),
        to_lines(w_depth.reshape(-1)),
        to_lines(jnp.concatenate([gain_attn, shift_attn, gain_out, shift_out])),
    ]
    starts = np.cumsum([0] + [line.shape[0] for line in lines])
    early = jnp.concatenate(
        [w_query, w_key, w_value, w_point, w_convout, pad_rows(jnp.concatenate(lines), 8)]
    )
    late = pad_rows(
        jnp.concatenate(
            [
                w_output[:, :WIDE],
                w_output[:, WIDE:],
                jnp.swapaxes(w_up, 1, 2).reshape(GROUPS * hidden, WIDE),
                w_down.reshape(GROUPS * hidden, WIDE),
            ]
        ),
        16,
    )
    late_all = lax.all_gather(late, ("seq", "dp"), axis=0, tiled=False)
    own, other = gather_weights(early, rows)
    tokens_other = swap(tokens_own, "dp", 1)
    row_tokens = jnp.where(
        core == 0,
        jnp.concatenate([tokens_own, tokens_other]),
        jnp.concatenate([tokens_other, tokens_own]),
    )
    cot_own = to_rows(cotangent[:, 0])
    pair_info = jnp.stack([valid_len[:, 0], sep_pos[:, 0]]).astype(F32)
    row_info = jnp.where((z & 1) == core, pair_info, swap(pair_info, "dp", 1))[:, z >> 1]
    info = jnp.concatenate([row_info.astype(jnp.int32), core[None]])

    turned = call(
        permute_kernel,
        shape((LEN, WIDTH), BF16),
        (row_tokens, matrix),
        0,
        flops=2 * LEN * WIDTH * WIDTH,
    )
    q, k, v, att, stats = call(
        attend_kernel,
        (
            shape((HALF, WIDE), BF16),
            shape((LEN, WIDE), BF16),
            shape((LEN, WIDE), BF16),
            shape((HALF, WIDE), BF16),
            shape((HALF, CHUNK), F32),
        ),
        (info, turned, own, other),
        flops=10**10,
    )
    small_rel = jnp.concatenate([own[5 * WIDE :], other[5 * WIDE :]]).reshape(count, -1, WIDE)
    kernel_rel = small_rel[:, starts[0] : starts[1]].reshape(count, -1)[:, : w_kernel.shape[0]]
    depth_rel = small_rel[:, starts[1] : starts[2]].reshape(count, -1)[:, : w_depth.size]
    gains_rel = small_rel[:, starts[2] : starts[3]].reshape(count, -1)[:, : 4 * rows]
    kernel_abs = jnp.dot(to_absolute, kernel_rel, preferred_element_type=F32).astype(BF16)
    taps_weight = jnp.pad(
        kernel_abs.reshape(WIDE, HEADS * KERNEL), ((0, 0), (0, CHUNK - HEADS * KERNEL))
    )
    depth_weight = jnp.pad(
        depth_rel.astype(F32).reshape(count, KERNEL, rows).transpose(1, 0, 2).reshape(KERNEL, WIDTH),
        ((0, 16 - KERNEL), (0, 0)),
    )
    gains = jnp.pad(
        jnp.dot(to_absolute, gains_rel, preferred_element_type=F32)
        .reshape(count, 4, rows)
        .transpose(1, 0, 2)
        .reshape(4, WIDTH),
        ((0, 4), (0, 0)),
    )
    context, key_conv, conv_attn, depth_low, values, spreads = call(
        conv_kernel,
        (
            shape((HALF, WIDTH), BF16),
            shape((HALF, WIDE), F32),
            shape((HALF, WIDE), BF16),
            shape((HALF, WIDTH), BF16),
            shape((WIDE // CHUNK, WINDOW, CHUNK), F32),
            shape((KERNEL, WIDE, WIDE), BF16),
        ),
        (info, turned, own, other, q, att, taps_weight, depth_weight),
        scratch=(
            pltpu.VMEM((WIDTH // CHUNK, WINDOW, CHUNK), F32),
            pltpu.VMEM((KERNEL, HALF, WIDE), F32),
            pltpu.VMEM((KERNEL, HALF, CHUNK), F32),
        ),
        flops=10**10,
    )
    if count == BLOCKS:
        late_blocks, late_order = late_all, order
    else:
        late_blocks, late_order = regroup(late_all, order, rows, hidden)
    halves = (GROUPS, 2, BLOCKS // 2 * HIDDEN, WIDE)
    layer_rows, first_grad, context_grad, kept, sent, gain_grads = call(
        feed_kernel,
        (
            shape((HALF, WIDTH), BF16),
            shape((HALF, WIDTH), F32),
            shape((HALF, WIDTH), BF16),
            shape((BLOCKS // 2, PACK, WIDE), BF16),
            shape((BLOCKS // 2, PACK, WIDE), BF16),
            shape((8, WIDTH), F32),
        ),
        (late_order, context, tokens_own, late_blocks, cot_own, gains, matrix),
        scratch=(
            pltpu.VMEM((WIDTH, WIDTH), BF16),
            pltpu.VMEM(halves, BF16),
            pltpu.VMEM(halves, BF16),
            pltpu.VMEM((GROUPS, 2, HALF, WIDTH), BF16),
            pltpu.VMEM((GROUPS, 2, HALF, WIDTH), F32),
            pltpu.VMEM((HALF, WIDTH), F32),
            pltpu.VMEM((HALF, WIDTH), F32),
            pltpu.VMEM((HALF, WIDTH), BF16),
            pltpu.VMEM((HALF, WIDTH), BF16),
            pltpu.VMEM((HALF, WIDTH), BF16),
            pltpu.VMEM((HALF, WIDTH), F32),
            pltpu.VMEM((HALF, 1), F32),
        ),
        flops=2 * 10**10,
    )
    if count == BLOCKS:
        first = scatter_relative(kept, sent)
    else:
        first = scatter_relative(split_late(kept, rows, hidden), split_late(sent, rows, hidden))
    query_conv, point_grad, kernel_grad, depth_grad, values_grad, input_grad, rim = call(
        conv_back_kernel,
        (
            shape((HALF, WIDE), F32),
            shape((WIDTH, WIDE), F32),
            shape((WIDE, CHUNK), F32),
            shape((16, WIDTH), F32),
            shape((WIDE // CHUNK, WINDOW, CHUNK), F32),
            shape((WIDTH // CHUNK, WINDOW, CHUNK), F32),
            shape((2 * EDGE, WIDTH), BF16),
        ),
        (
            info,
            turned,
            own,
            other,
            q,
            context_grad,
            key_conv,
            conv_attn,
            depth_low,
            values,
            spreads,
            taps_weight,
            depth_weight,
        ),
        scratch=(
            pltpu.VMEM((WIDTH // CHUNK, WINDOW, CHUNK), F32),
            pltpu.VMEM((KERNEL, HALF, WIDE), F32),
            pltpu.VMEM((KERNEL, HALF, CHUNK), F32),
            pltpu.VMEM((KERNEL, HALF, CHUNK), F32),
            pltpu.VMEM((KERNEL, WINDOW, CHUNK), F32),
            pltpu.VMEM((WINDOW, CHUNK), F32),
            pltpu.VMEM((KERNEL, HALF, CHUNK), BF16),
        ),
        flops=10**10,
    )
    query_attn, own_part, message = call(
        attend_back_kernel,
        (shape((HALF, WIDE), F32), shape((HALF, WIDTH), F32), shape((WINDOW, WIDTH), BF16)),
        (info, q, k, v, context, context_grad, stats, rim),
        scratch=(pltpu.VMEM((LEN, WIDE), F32), pltpu.VMEM((LEN, WIDE), F32)),
        flops=2 * 10**10,
    )
    arrived = swap(message, "dp", 1)

    kernel_lines = kernel_grad[:, : HEADS * KERNEL].reshape(count, -1)
    gain_lines = gain_grads[:4].reshape(4, count, rows).transpose(1, 0, 2).reshape(count, -1)
    turned_lines = lax.dot_general(
        to_absolute,
        jnp.concatenate([to_block(kernel_lines), to_block(gain_lines)], 1).astype(BF16),
        (((0,), (0,)), ((), ())),
        preferred_element_type=F32,
    )
    cut = starts[1] * WIDE
    depth_lines = to_block(
        depth_grad[:KERNEL].reshape(KERNEL, count, rows).transpose(1, 0, 2).reshape(count, -1)
    )
    small = jnp.concatenate([turned_lines[:, :cut], depth_lines, turned_lines[:, cut:]], 1)
    small = jnp.pad(small, ((0, 0), (0, 8 * WIDE - small.shape[1]))).reshape(count, 8, WIDE)
    kept, sent, x_low = call(
        finish_kernel,
        (
            shape((BLOCKS // 2, 128, WIDE), BF16),
            shape((BLOCKS // 2, 128, WIDE), BF16),
            shape((HALF, WIDTH), BF16),
        ),
        (
            info,
            turned,
            own,
            other,
            matrix,
            query_attn,
            query_conv,
            own_part,
            arrived,
            values_grad,
            input_grad,
            point_grad,
            small[:BLOCKS],
            first_grad,
        ),
        scratch=(pltpu.VMEM((HALF, WIDE), F32), pltpu.VMEM((HALF, WIDTH), F32)),
        flops=10**10,
    )
    if count != BLOCKS:
        kept, sent = split_early(kept, small[:half], rows), split_early(sent, small[half:], rows)
    second = scatter_relative(kept, sent)
    x_grad = from_rows(x_low).astype(F32)

    def part(index):
        return second[index * rows : (index + 1) * rows]

    lines = second[5 * rows : 5 * rows + 8].reshape(-1)
    kernel_at, depth_at, gain_at = (start * WIDE for start in starts[:3])
    depth_line = lines[depth_at : depth_at + w_depth.size].reshape(KERNEL, rows)
    gain_line = lines[gain_at : gain_at + 4 * rows].reshape(4, rows)
    return (
        from_rows(layer_rows)[:, None],
        x_grad[:, None],
        part(0),
        part(1),
        part(2),
        depth_line,
        part(3),
        lines[kernel_at : kernel_at + w_kernel.shape[0]],
        part(4),
        jnp.concatenate([first[:rows], first[rows : 2 * rows]], 1),
        gain_line[0],
        gain_line[1],
        jnp.swapaxes(
            first[2 * rows : 2 * rows + GROUPS * hidden].reshape(GROUPS, hidden, WIDE), 1, 2
        ),
        first[2 * rows + GROUPS * hidden : 2 * rows + 2 * GROUPS * hidden].reshape(
            GROUPS, hidden, WIDE
        ),
        gain_line[2],
        gain_line[3],
    )


def solution(mesh):
    in_specs = (
        P(None, "dp", "seq", None),
        P(None, "dp", "seq", None),
        P(None, "dp"),
        P(None, "dp"),
        P(("seq", "dp"), None),
        P(("seq", "dp"), None),
        P(("seq", "dp"), None),
        P(None, ("seq", "dp")),
        P(("seq", "dp"), None),
        P(("seq", "dp")),
        P(("seq", "dp"), None),
        P(("seq", "dp"), None),
        P(("seq", "dp")),
        P(("seq", "dp")),
        P(None, None, ("seq", "dp")),
        P(None, ("seq", "dp"), None),
        P(("seq", "dp")),
        P(("seq", "dp")),
    )
    out_specs = (
        P(None, "dp", "seq", None),
        P(None, "dp", "seq", None),
        P(("seq", "dp"), None),
        P(("seq", "dp"), None),
        P(("seq", "dp"), None),
        P(None, ("seq", "dp")),
        P(("seq", "dp"), None),
        P(("seq", "dp")),
        P(("seq", "dp"), None),
        P(("seq", "dp"), None),
        P(("seq", "dp")),
        P(("seq", "dp")),
        P(None, None, ("seq", "dp")),
        P(None, ("seq", "dp"), None),
        P(("seq", "dp")),
        P(("seq", "dp")),
    )
    return jax.shard_map(local, mesh=mesh, in_specs=in_specs, out_specs=out_specs, check_vma=False)
```

time: 557 us -> 310 us (0.56)
  local copies, waits for them, and re-layouts: 172 us -> 29.2 us
  matrix products: 93.4 us -> 0.45 us
  other arithmetic: 117 us -> 24.9 us
  Pallas kernels: 19 us -> 95.5 us
  waiting for transfers between devices: 67.9 us -> 93.7 us
  starting transfers between devices: 62.3 us -> 47.3 us
    dot_general x32 -> x3, matrix products: 86.3 us -> 0.45 us  [the longest x1 0.2 us: local(): lax.dot_general(to_absolute, jnp.concatenate([to_block(kernel_lines), to_...]
    pallas_call x3 -> x7, Pallas kernels: 19 us -> 95.5 us  [call(): pl.pallas_call(kernel, out_shape=out_shape, in_specs=[pl.BlockSpec(memory...]
    scatter-add x16 -> x0, local copies, waits for them, and re-layouts: 61.1 us -> none  [the longest x8 37.8 us: run_batch(): d_input_pad.at[:, tap_index:tap_index + local_len]]
    add x13 -> x1, other arithmetic: 30.1 us -> 0.07 us  [local(): order[:, None] * rows + jnp.arange(rows)[None, :]]
    reduce_sum x19 -> x0, other arithmetic: 26.3 us -> none  [the longest x9 12.1 us: run_batch(): jnp.sum(d_conv_heads * window, -1) * same_masks[tap_index][:, :, None]]
    mul x36 -> x0, local copies, waits for them, and re-layouts: 22.2 us -> none  [the longest x9 11.1 us: run_batch(): d_conv_heads * window]
    ppermute x25 -> x24, waiting for transfers between devices: 52.7 us -> 72.6 us  [swap(): return lax.ppermute(x, axis, [(i, i ^ mask) for i in range(count)])]
    unnamed x356 -> x61, local copies, waits for them, and re-layouts: 28.9 us -> 13.3 us
  transfers between devices with their start and end apart: 34 -> 33, of which waited for: 10 -> 15; matrix products, arithmetic and copies ran while one was open for 26% -> 15% of each run, Pallas kernels for 3% -> 9%
where the time goes in v2:
time: 310 us; the launch traced here: 306 us
  Pallas kernels  95.5 us (31%)
  waiting for transfers between devices  93.7 us (30%)
  starting transfers between devices  47.3 us (15%)
  local copies, waits for them, and re-layouts  29.2 us (9%)
  other arithmetic  24.9 us (8%)
  between operations  14.9 us (5%)
    pallas_call x7, Pallas kernels, call(): pl.pallas_call(kernel, out_shape=out_shape, in_specs=[pl.BlockSpec(memory...  95.5 us
    ppermute x24, waiting for transfers between devices, swap(): return lax.ppermute(x, axis, [(i, i ^ mask) for i in range(count)])  72.6 us
    ppermute x24, starting transfers between devices, swap(): return lax.ppermute(x, axis, [(i, i ^ mask) for i in range(count)])  33.5 us
    unnamed x61, local copies, waits for them, and re-layouts  13.3 us
    ppermute x2, waiting for transfers between devices, to_rows(): lax.ppermute(lax.dynamic_index_in_dim(x, 1 - odd, 0, False), ('seq', 'dp'...  12.5 us
    ppermute x2, starting transfers between devices, to_rows(): lax.ppermute(lax.dynamic_index_in_dim(x, odd, 0, False), ('seq', 'dp'), f...  8.94 us
    ppermute x2, waiting for transfers between devices, from_rows(): lax.ppermute(lax.dynamic_index_in_dim(half, 1 - high, 0, False), ('seq',...  8.61 us
  transfers between devices with their start and end apart: 33, of which 15 were waited for; matrix products, arithmetic and copies ran while one was open for 15% of the time, Pallas kernels for 9%

profile of v2, /device:TPU:0, one launch (start us, length us, event | category | flops | bytes accessed | tf_op | source)
XLA Modules:
  0.0 306.0 jit_solution(2277826932257522633)
XLA Ops:
  8.0 1.6 pad_maximum_fusion.1
  16.2 5.0 %collective-permute-start.6 = (bf16[128,384]{1,0:T(8,128)(2,1)S(1)}, bf16[128,384]{1,0:T(8,128)(2,1)S(1)}, u32[]{:S(2)}, u32[]{:S(2)}) collective-permute-start(bf16[128,384]{1,0:T(8,128)(2,1)S(1)} %get-tuple-element.136), channel_id=1, source_target_pairs={{0,24},{8,16},{16,8},{24,0},{1,25},{9,17},{17,9},{25,1},{2,26},{10... | collective-permute-start | bytes 294920 | tf_op jit(solution)/shard_map/ppermute | solution.py:649
  23.1 2.0 dynamic-slice_bitcast_fusion.7
  25.1 4.5 %collective-permute-start.1 = (bf16[256,768]{1,0:T(8,128)(2,1)}, bf16[256,768]{1,0:T(8,128)(2,1)}, u32[]{:S(2)}, u32[]{:S(2)}) collective-permute-start(bf16[256,768]{1,0:T(8,128)(2,1)} %get-tuple-element.88), channel_id=1, source_target_pairs={{0,0},{1,8},{2,2},{3,10},{4,4},{5,12},{6,6},{7,14},{8,16},{9,24},{... | collective-permute-start | bytes 1179656 | tf_op jit(solution)/shard_map/ppermute | solution.py:693
  30.5 1.7 collective-permute-done.5
  32.9 2.4 collective-permute-start.9
  36.5 11.1 %collective-permute-done.9 = bf16[512,384]{1,0:T(8,128)(2,1)S(1)} collective-permute-done((bf16[512,384]{1,0:T(8,128)(2,1)S(1)}, bf16[512,384]{1,0:T(8,128)(2,1)S(1)}, u32[]{:S(2)}, u32[]{:S(2)}) %collective-permute-start.9) | collective-permute-done | bytes 393248 | tf_op jit(solution)/shard_map/ppermute | solution.py:649
  47.6 6.3 %collective-permute-done.8 = bf16[512,384]{1,0:T(8,128)(2,1)S(1)} collective-permute-done((bf16[512,384]{1,0:T(8,128)(2,1)S(1)}, bf16[512,384]{1,0:T(8,128)(2,1)S(1)}, u32[]{:S(2)}, u32[]{:S(2)}) %collective-permute-start.8) | collective-permute-done | bytes 393248 | tf_op jit(solution)/shard_map/ppermute | solution.py:649
  53.9 4.5 %collective-permute-start.11 = (bf16[256,768]{1,0:T(8,128)(2,1)}, bf16[256,768]{1,0:T(8,128)(2,1)}, u32[]{:S(2)}, u32[]{:S(2)}) collective-permute-start(bf16[256,768]{1,0:T(8,128)(2,1)} %get-tuple-element.86), channel_id=1, source_target_pairs={{0,0},{1,8},{2,2},{3,10},{4,4},{5,12},{6,6},{7,14},{8,16},{9,24},{... | collective-permute-start | bytes 1179656 | tf_op jit(solution)/shard_map/ppermute | solution.py:693
  59.4 1.3 constant_dynamic-update-slice_fusion.36
  62.5 1.3 constant_dynamic-update-slice_fusion.33
  63.9 1.3 constant_dynamic-update-slice_fusion.32
  65.8 1.4 collective-permute-start.12
  67.2 1.3 maximum_select_fusion.1.tokens
  68.6 3.9 %collective-permute-start.3 = (bf16[512,768]{1,0:T(8,128)(2,1)S(1)}, bf16[512,768]{1,0:T(8,128)(2,1)}, u32[]{:S(2)}, u32[]{:S(2)}) collective-permute-start(bf16[512,768]{1,0:T(8,128)(2,1)S(1)} %maximum_select_fusion.1.tokens), channel_id=1, source_target_pairs={{0,1},{1,0},{2,3},{3,2},{4,5},{5,4},{6,7},{7,6},{8,9},{9,8},{10,11... | collective-permute-start | bytes 2359304 | tf_op jit(solution)/shard_map/ppermute | solution.py:649
  72.7 1.4 fusion.matrix
  74.9 12.5 %collective-permute-done.12 = bf16[256,768]{1,0:T(8,128)(2,1)S(1)} collective-permute-done((bf16[256,768]{1,0:T(8,128)(2,1)}, bf16[256,768]{1,0:T(8,128)(2,1)S(1)}, u32[]{:S(2)}, u32[]{:S(2)}) %collective-permute-start.12) | collective-permute-done | bytes 393248 | tf_op jit(solution)/shard_map/ppermute | solution.py:694
  87.4 2.2 maximum_select_fusion.2.cotangent
  89.6 3.1 %maximum_select_fusion.tokens = bf16[1024,768]{1,0:T(8,128)(2,1)} fusion(bf16[512,768]{1,0:T(8,128)(2,1)} %collective-permute-done.3, bf16[512,768]{1,0:T(8,128)(2,1)S(1)} %maximum_select_fusion.1.tokens, pred[]{:T(512)S(6)} %eq.42), kind=kLoop, calls=%fused_computation.4 | loop fusion | flops 7077888 | bytes 3145729 | tf_op jit(solution)/shard_map/jit(_where)/select_n | solution.py:827
  92.7 4.3 %shard_map.306.tokens = bf16[1024,768]{1,0:T(8,128)(2,1)} custom-call(bf16[1024,768]{1,0:T(8,128)(2,1)} %maximum_select_fusion.tokens, bf16[768,768]{1,0:T(8,128)(2,1)} %fusion.matrix), custom_call_target="tpu_custom_call" | custom-call | flops 1207959552 | tf_op jit(solution)/shard_map/pallas_call | solution.py:47
  101.1 11.7 %shard_map.307 = (bf16[512,384]{1,0:T(8,128)(2,1)}, bf16[1024,384]{1,0:T(8,128)(2,1)}, bf16[1024,384]{1,0:T(8,128)(2,1)}, bf16[512,384]{1,0:T(8,128)(2,1)}, f32[512,128]{1,0:T(8,128)}) custom-call(s32[3]{0:T(128)} %pad_add_fusion.info, bf16[1024,768]{1,0:T(8,128)(2,1)} %shard_map.306.tokens, bf16[2048,384]{1,0:T(8,128)(2,1)} %copy-done.2, ...), custom_call_target="tpu_custom_call" | custom-call | flops 10000000000 | tf_op jit(solution)/shard_map/pallas_call | solution.py:47
  112.8 12.1 %shard_map.308 = (bf16[512,768]{1,0:T(8,128)(2,1)}, f32[512,384]{1,0:T(8,128)}, bf16[512,384]{1,0:T(8,128)(2,1)}, bf16[512,768]{1,0:T(8,128)(2,1)}, f32[3,544,12...) custom-call(s32[3]{0:T(128)} %pad_add_fusion.info, bf16[1024,768]{1,0:T(8,128)(2,1)} %shard_map.306.tokens, ...), custom_call_target="tpu_custom_call" | custom-call | flops 10000000000 | tf_op jit(solution)/shard_map/pallas_call | solution.py:47
  124.8 23.7 %shard_map.309 = (bf16[512,768]{1,0:T(8,128)(2,1)}, f32[512,768]{1,0:T(8,128)}, bf16[512,768]{1,0:T(8,128)(2,1)}, bf16[16,240,384]{2,1,0:T(8,128)(2,1)}, bf16[16...) custom-call(s32[32]{0:T(128)} %copy-done.13, bf16[512,768]{1,0:T(8,128)(2,1)} %get-tuple-element.48.context, ...), custom_call_target="tpu_custom_call" | custom-call | flops 20000000000 | tf_op jit(solution)/shard_map/pallas_call | solution.py:47
  148.6 18.4 %shard_map.310 = (f32[512,384]{1,0:T(8,128)}, f32[768,384]{1,0:T(8,128)}, f32[384,128]{1,0:T(8,128)}, f32[16,768]{1,0:T(8,128)}, f32[3,544,128]{2,1,0:T(8,128)},...) custom-call(s32[3]{0:T(128)} %pad_add_fusion.info, bf16[1024,768]{1,0:T(8,128)(2,1)} %shard_map.306.tokens, ...), custom_call_target="tpu_custom_call" | custom-call | flops 10000000000 | tf_op jit(solution)/shard_map/pallas_call | solution.py:47
  167.0 12.9 %shard_map.311 = (f32[512,384]{1,0:T(8,128)}, f32[512,768]{1,0:T(8,128)}, bf16[544,768]{1,0:T(8,128)(2,1)}) custom-call(s32[3]{0:T(128)} %pad_add_fusion.info, bf16[512,384]{1,0:T(8,128)(2,1)} %get-tuple-element.46.q, bf16[1024,384]{1,0:T(8,128)(2,1)} %get-tuple-element.50.k, bf16[1024,384]{1,0:T(8,128)(2,1)} %get-tuple-element.51.v, ...), custom_call_target="tpu_custom_call" | custom-call | flops 20000000000 | tf_op jit(solution)/shard_map/pallas_call | solution.py:47
  183.5 12.3 %shard_map.312 = (bf16[16,128,384]{2,1,0:T(8,128)(2,1)}, bf16[16,128,384]{2,1,0:T(8,128)(2,1)}, bf16[512,768]{1,0:T(8,128)(2,1)}) custom-call(s32[3]{0:T(128)} %pad_add_fusion.info, bf16[1024,768]{1,0:T(8,128)(2,1)} %shard_map.306.tokens, bf16[2048,384]{1,0:T(8,128)(2,1)} %copy-done.2, bf16[2048,384]{1,0:T(8,128)(2,1)} %collective-permute-done.10.other, ...), custom_call_target="tpu_custom_call" | custom-call | flops 10000000000 | tf_op jit(solution)/shard_map/pallas_call | solution.py:47
  196.3 4.7 %collective-permute-done.18 = bf16[16,128,384]{2,1,0:T(8,128)(2,1)S(1)} collective-permute-done((bf16[16,128,384]{2,1,0:T(8,128)(2,1)}, bf16[16,128,384]{2,1,0:T(8,128)(2,1)S(1)}, u32[]{:S(2)}, u32[]{:S(2)}) %collective-permute-start.18) | collective-permute-done | bytes 1572896 | tf_op jit(solution)/shard_map/ppermute | solution.py:649
  201.1 1.9 add_convert_fusion.1
  204.0 1.5 collective-permute-start.19
  205.5 2.0 collective-permute-start.21
  208.9 7.4 %collective-permute-done.19 = bf16[4,128,384]{2,1,0:T(8,128)(2,1)} collective-permute-done((bf16[4,128,384]{2,1,0:T(8,128)(2,1)}, bf16[4,128,384]{2,1,0:T(8,128)(2,1)}, u32[]{:S(2)}, u32[]{:S(2)}) %collective-permute-start.19) | collective-permute-done | bytes 393248 | tf_op jit(solution)/shard_map/ppermute | solution.py:649
  216.3 9.7 %collective-permute-done.21 = bf16[4,128,384]{2,1,0:T(8,128)(2,1)} collective-permute-done((bf16[4,128,384]{2,1,0:T(8,128)(2,1)}, bf16[4,128,384]{2,1,0:T(8,128)(2,1)}, u32[]{:S(2)}, u32[]{:S(2)}) %collective-permute-start.21) | collective-permute-done | bytes 393248 | tf_op jit(solution)/shard_map/ppermute | solution.py:649
  227.1 2.2 collective-permute-start.17
  229.3 1.4 add_convert_fusion.3
  230.8 2.1 collective-permute-start.22
  232.9 2.7 add_convert_fusion
  235.6 1.4 fusion.41
  238.4 2.0 collective-permute-start.27
  241.5 8.6 %collective-permute-done.17 = bf16[256,768]{1,0:T(8,128)(2,1)S(1)} collective-permute-done((bf16[256,768]{1,0:T(8,128)(2,1)S(1)}, bf16[256,768]{1,0:T(8,128)(2,1)S(1)}, u32[]{:S(2)}, u32[]{:S(2)}) %collective-permute-start.17) | collective-permute-done | bytes 393248 | tf_op jit(solution)/shard_map/ppermute | solution.py:706
  251.3 1.3 fusion.1
  252.6 4.6 %collective-permute-done.24 = bf16[128,384]{1,0:T(8,128)(2,1)S(1)} collective-permute-done((bf16[128,384]{1,0:T(8,128)(2,1)S(1)}, bf16[128,384]{1,0:T(8,128)(2,1)S(1)}, u32[]{:S(2)}, u32[]{:S(2)}) %collective-permute-start.24) | collective-permute-done | bytes 98336 | tf_op jit(solution)/shard_map/ppermute | solution.py:649
  257.2 3.1 %collective-permute-done.23 = bf16[128,384]{1,0:T(8,128)(2,1)S(1)} collective-permute-done((bf16[128,384]{1,0:T(8,128)(2,1)S(1)}, bf16[128,384]{1,0:T(8,128)(2,1)S(1)}, u32[]{:S(2)}, u32[]{:S(2)}) %collective-permute-start.23) | collective-permute-done | bytes 98336 | tf_op jit(solution)/shard_map/ppermute | solution.py:649
  262.3 7.4 %collective-permute-done.28 = bf16[4,240,384]{2,1,0:T(8,128)(2,1)} collective-permute-done((bf16[4,240,384]{2,1,0:T(8,128)(2,1)}, bf16[4,240,384]{2,1,0:T(8,128)(2,1)}, u32[]{:S(2)}, u32[]{:S(2)}) %collective-permute-start.28) | collective-permute-done | bytes 737312 | tf_op jit(solution)/shard_map/ppermute | solution.py:649
  269.6 1.9 add_convert_fusion.2
  271.6 5.0 %collective-permute-start.29 = (bf16[240,384]{1,0:T(8,128)(2,1)S(1)}, bf16[240,384]{1,0:T(8,128)(2,1)S(1)}, u32[]{:S(2)}, u32[]{:S(2)}) collective-permute-start(bf16[240,384]{1,0:T(8,128)(2,1)S(1)} %get-tuple-element.90), channel_id=1, source_target_pairs={{0,8},{8,0},{16,24},{24,16},{1,9},{9,1},{17,25},{25,17},{2,10},{10... | collective-permute-start | bytes 552968 | tf_op jit(solution)/shard_map/ppermute | solution.py:649
  276.6 4.0 %collective-permute-start.31 = (bf16[240,384]{1,0:T(8,128)(2,1)S(1)}, bf16[240,384]{1,0:T(8,128)(2,1)S(1)}, u32[]{:S(2)}, u32[]{:S(2)}) collective-permute-start(bf16[240,384]{1,0:T(8,128)(2,1)S(1)} %get-tuple-element.91), channel_id=1, source_target_pairs={{0,24},{8,16},{16,8},{24,0},{1,25},{9,17},{17,9},{25,1},{2,26},{10... | collective-permute-start | bytes 552968 | tf_op jit(solution)/shard_map/ppermute | solution.py:649
  281.3 8.3 %collective-permute-done.31 = bf16[240,384]{1,0:T(8,128)(2,1)S(1)} collective-permute-done((bf16[240,384]{1,0:T(8,128)(2,1)S(1)}, bf16[240,384]{1,0:T(8,128)(2,1)S(1)}, u32[]{:S(2)}, u32[]{:S(2)}) %collective-permute-start.31) | collective-permute-done | bytes 184352 | tf_op jit(solution)/shard_map/ppermute | solution.py:649
  289.6 7.9 %collective-permute-done.30 = bf16[240,384]{1,0:T(8,128)(2,1)S(1)} collective-permute-done((bf16[240,384]{1,0:T(8,128)(2,1)S(1)}, bf16[240,384]{1,0:T(8,128)(2,1)S(1)}, u32[]{:S(2)}, u32[]{:S(2)}) %collective-permute-start.30) | collective-permute-done | bytes 184352 | tf_op jit(solution)/shard_map/ppermute | solution.py:649
  (176 shorter events, 35.9 us)
Async XLA Ops:
  7.2 22.4 %copy-start.3 = (bf16[2,1,256,768]{3,2,1,0:T(8,128)(2,1)S(1)}, bf16[2,1,256,768]{3,2,1,0:T(8,128)(2,1)}, u32[]{:S(2)}) copy-start(bf16[2,1,256,768]{3,2,1,0:T(8,128)(2,1)} %param.20) | copy-start | bytes 2359300
  7.2 117.7 %all-gather.3.cloned.1.call-start = ((), (), s32[]{:S(2)}) async-start(), calls=%async_computation | async-start | bytes 6082560 | tf_op jit(solution)/shard_map/all_gather | solution.py:824
  16.2 14.3 %collective-permute-start.6 = (bf16[128,384]{1,0:T(8,128)(2,1)S(1)}, bf16[128,384]{1,0:T(8,128)(2,1)S(1)}, u32[]{:S(2)}, u32[]{:S(2)}) collective-permute-start(bf16[128,384]{1,0:T(8,128)(2,1)S(1)} %get-tuple-element.136), channel_id=1, source_target_pairs={{0,24},{8,16},{16,8},{24,0},{1,25},{9,17},{17,9},{25,1},{2,26},{10... | collective-permute-start | bytes 294920 | tf_op jit(solution)/shard_map/ppermute | solution.py:649
  21.3 11.0 %collective-permute-start.5 = (bf16[128,384]{1,0:T(8,128)(2,1)S(1)}, bf16[128,384]{1,0:T(8,128)(2,1)S(1)}, u32[]{:S(2)}, u32[]{:S(2)}) collective-permute-start(bf16[128,384]{1,0:T(8,128)(2,1)S(1)} %get-tuple-element.136), channel_id=1, source_target_pairs={{0,16},{8,24},{16,0},{24,8},{1,17},{9,25},{17,1},{25,9},{2,18},{10... | collective-permute-start | bytes 294920 | tf_op jit(solution)/shard_map/ppermute | solution.py:649
  21.3 11.0 %collective-permute-start.4 = (bf16[128,384]{1,0:T(8,128)(2,1)S(1)}, bf16[128,384]{1,0:T(8,128)(2,1)S(1)}, u32[]{:S(2)}, u32[]{:S(2)}) collective-permute-start(bf16[128,384]{1,0:T(8,128)(2,1)S(1)} %get-tuple-element.136), channel_id=1, source_target_pairs={{0,8},{8,0},{16,24},{24,16},{1,9},{9,1},{17,25},{25,17},{2,10},{10... | collective-permute-start | bytes 294920 | tf_op jit(solution)/shard_map/ppermute | solution.py:649
  23.1 51.0 %collective-permute-start = (f32[2,2]{1,0:T(2,128)}, f32[2,2]{1,0:T(2,128)S(1)}, u32[]{:S(2)}, u32[]{:S(2)}) collective-permute-start(f32[2,2]{1,0:T(2,128)} %add_convert_fusion.4), channel_id=1, source_target_pairs={{0,1},{1,0},{2,3},{3,2},{4,5},{5,4},{6,7},{7,6},{8,9},{9,8},{10,11... | collective-permute-start | bytes 56 | tf_op jit(solution)/shard_map/ppermute | solution.py:649
  25.1 40.7 %collective-permute-start.1 = (bf16[256,768]{1,0:T(8,128)(2,1)}, bf16[256,768]{1,0:T(8,128)(2,1)}, u32[]{:S(2)}, u32[]{:S(2)}) collective-permute-start(bf16[256,768]{1,0:T(8,128)(2,1)} %get-tuple-element.88), channel_id=1, source_target_pairs={{0,0},{1,8},{2,2},{3,10},{4,4},{5,12},{6,6},{7,14},{8,16},{9,24},{... | collective-permute-start | bytes 1179656 | tf_op jit(solution)/shard_map/ppermute | solution.py:693
  32.9 14.7 %collective-permute-start.9 = (bf16[512,384]{1,0:T(8,128)(2,1)S(1)}, bf16[512,384]{1,0:T(8,128)(2,1)S(1)}, u32[]{:S(2)}, u32[]{:S(2)}) collective-permute-start(bf16[512,384]{1,0:T(8,128)(2,1)S(1)} %constant_dynamic-update-slice_fusion.11), channel_id=1, source_target_pairs={{0,6},{1,7},{2,4},{3,5},{4,2},{5,3},{6,0},{7,1},{8,14},{9,15},{10,... | collective-permute-start | bytes 1179656 | tf_op jit(solution)/shard_map/ppermute | solution.py:649
  35.3 18.6 %collective-permute-start.8 = (bf16[512,384]{1,0:T(8,128)(2,1)S(1)}, bf16[512,384]{1,0:T(8,128)(2,1)S(1)}, u32[]{:S(2)}, u32[]{:S(2)}) collective-permute-start(bf16[512,384]{1,0:T(8,128)(2,1)S(1)} %constant_dynamic-update-slice_fusion.11), channel_id=1, source_target_pairs={{0,4},{1,5},{2,6},{3,7},{4,0},{5,1},{6,2},{7,3},{8,12},{9,13},{10,... | collective-permute-start | bytes 1179656 | tf_op jit(solution)/shard_map/ppermute | solution.py:649
  35.8 22.6 %collective-permute-start.7 = (bf16[512,384]{1,0:T(8,128)(2,1)S(1)}, bf16[512,384]{1,0:T(8,128)(2,1)S(1)}, u32[]{:S(2)}, u32[]{:S(2)}) collective-permute-start(bf16[512,384]{1,0:T(8,128)(2,1)S(1)} %constant_dynamic-update-slice_fusion.11), channel_id=1, source_target_pairs={{0,2},{1,3},{2,0},{3,1},{4,6},{5,7},{6,4},{7,5},{8,10},{9,11},{10,... | collective-permute-start | bytes 1179656 | tf_op jit(solution)/shard_map/ppermute | solution.py:649
  47.6 19.6 %collective-permute-start.2 = (bf16[256,768]{1,0:T(8,128)(2,1)}, bf16[256,768]{1,0:T(8,128)(2,1)S(1)}, u32[]{:S(2)}, u32[]{:S(2)}) collective-permute-start(bf16[256,768]{1,0:T(8,128)(2,1)} %get-tuple-element.89), channel_id=1, source_target_pairs={{0,16},{1,24},{2,18},{3,26},{4,20},{5,28},{6,22},{7,30},{8,0},{9,8... | collective-permute-start | bytes 1179656 | tf_op jit(solution)/shard_map/ppermute | solution.py:694
  53.9 4.8 %copy-start.6 = (bf16[512,384]{1,0:T(8,128)(2,1)}, bf16[512,384]{1,0:T(8,128)(2,1)S(1)}, u32[]{:S(2)}) copy-start(bf16[512,384]{1,0:T(8,128)(2,1)S(1)} %collective-permute-done.8) | copy-start | bytes 1179652
  53.9 21.0 %collective-permute-start.11 = (bf16[256,768]{1,0:T(8,128)(2,1)}, bf16[256,768]{1,0:T(8,128)(2,1)}, u32[]{:S(2)}, u32[]{:S(2)}) collective-permute-start(bf16[256,768]{1,0:T(8,128)(2,1)} %get-tuple-element.86), channel_id=1, source_target_pairs={{0,0},{1,8},{2,2},{3,10},{4,4},{5,12},{6,6},{7,14},{8,16},{9,24},{... | collective-permute-start | bytes 1179656 | tf_op jit(solution)/shard_map/ppermute | solution.py:693
  59.2 6.7 %copy-start.17 = (s32[32]{0:T(128)S(1)}, s32[32]{0:T(128)}, u32[]{:S(2)}) copy-start(s32[32]{0:T(128)} %constant.50.clone) | copy-start | bytes 388
  59.3 14.8 %copy-start.15 = (s32[2,1]{0,1:T(1,128)S(1)}, s32[2,1]{0,1:T(1,128)}, u32[]{:S(2)}) copy-start(s32[2,1]{0,1:T(1,128)} %param.22) | copy-start | bytes 28
  59.3 14.8 %copy-start.16 = (s32[2,1]{0,1:T(1,128)S(1)}, s32[2,1]{0,1:T(1,128)}, u32[]{:S(2)}) copy-start(s32[2,1]{0,1:T(1,128)} %param.21) | copy-start | bytes 28
  65.8 23.8 %copy-start.2 = (bf16[2048,384]{1,0:T(8,128)(2,1)}, bf16[2048,384]{1,0:T(8,128)(2,1)S(1)}, u32[]{:S(2)}) copy-start(bf16[2048,384]{1,0:T(8,128)(2,1)S(1)} %get-tuple-element.97.own) | copy-start | bytes 4718596
  65.8 31.2 %collective-permute-start.10 = (bf16[2048,384]{1,0:T(8,128)(2,1)S(1)}, bf16[2048,384]{1,0:T(8,128)(2,1)}, u32[]{:S(2)}, u32[]{:S(2)}) collective-permute-start(bf16[2048,384]{1,0:T(8,128)(2,1)S(1)} %get-tuple-element.97.own), channel_id=1, source_target_pairs={{0,1},{1,0},{2,3},{3,2},{4,5},{5,4},{6,7},{7,6},{8,9},{9,8},{10,11... | collective-permute-start | bytes 4718600 | tf_op jit(solution)/shard_map/ppermute | solution.py:649
  65.8 33.7 %copy-start.13 = (s32[32]{0:T(128)}, s32[32]{0:T(128)S(1)}, u32[]{:S(2)}) copy-start(s32[32]{0:T(128)S(1)} %get-tuple-element.138.order) | copy-start | bytes 388
  65.8 21.5 %collective-permute-start.12 = (bf16[256,768]{1,0:T(8,128)(2,1)}, bf16[256,768]{1,0:T(8,128)(2,1)S(1)}, u32[]{:S(2)}, u32[]{:S(2)}) collective-permute-start(bf16[256,768]{1,0:T(8,128)(2,1)} %get-tuple-element.87), channel_id=1, source_target_pairs={{0,16},{1,24},{2,18},{3,26},{4,20},{5,28},{6,22},{7,30},{8,0},{9,8... | collective-permute-start | bytes 1179656 | tf_op jit(solution)/shard_map/ppermute | solution.py:694
  68.5 24.2 %copy-start = (bf16[512,768]{1,0:T(8,128)(2,1)}, bf16[512,768]{1,0:T(8,128)(2,1)S(1)}, u32[]{:S(2)}) copy-start(bf16[512,768]{1,0:T(8,128)(2,1)S(1)} %maximum_select_fusion.1.tokens) | copy-start | bytes 2359300
  68.6 21.1 %collective-permute-start.3 = (bf16[512,768]{1,0:T(8,128)(2,1)S(1)}, bf16[512,768]{1,0:T(8,128)(2,1)}, u32[]{:S(2)}, u32[]{:S(2)}) collective-permute-start(bf16[512,768]{1,0:T(8,128)(2,1)S(1)} %maximum_select_fusion.1.tokens), channel_id=1, source_target_pairs={{0,1},{1,0},{2,3},{3,2},{4,5},{5,4},{6,7},{7,6},{8,9},{9,8},{10,11... | collective-permute-start | bytes 2359304 | tf_op jit(solution)/shard_map/ppermute | solution.py:649
  92.7 4.3 %copy-start.8 = (bf16[256,384]{1,0:T(8,128)(2,1)S(1)}, bf16[256,384]{1,0:T(8,128)(2,1)}, u32[]{:S(2)}) copy-start(bf16[256,384]{1,0:T(8,128)(2,1)} %get-tuple-element.96) | copy-start | bytes 589828
  167.0 13.9 %copy-start.11 = (f32[384,128]{1,0:T(8,128)S(1)}, f32[384,128]{1,0:T(8,128)}, u32[]{:S(2)}) copy-start(f32[384,128]{1,0:T(8,128)} %get-tuple-element.67) | copy-start | bytes 589828
  167.0 14.1 %copy-start.14 = (s32[32]{0:T(128)S(1)}, s32[32]{0:T(128)}, u32[]{:S(2)}) copy-start(s32[32]{0:T(128)} %copy-done.13) | copy-start | bytes 388
  167.0 14.3 %copy-start.12 = (f32[16,768]{1,0:T(8,128)S(1)}, f32[16,768]{1,0:T(8,128)}, u32[]{:S(2)}) copy-start(f32[16,768]{1,0:T(8,128)} %get-tuple-element.69) | copy-start | bytes 147460
  180.0 2.6 collective-permute-start.15
  195.8 5.3 %collective-permute-start.18 = (bf16[16,128,384]{2,1,0:T(8,128)(2,1)}, bf16[16,128,384]{2,1,0:T(8,128)(2,1)S(1)}, u32[]{:S(2)}, u32[]{:S(2)}) collective-permute-start(bf16[16,128,384]{2,1,0:T(8,128)(2,1)} %get-tuple-element.73), channel_id=1, source_target_pairs={{0,1},{1,0},{2,3},{3,2},{4,5},{5,4},{6,7},{7,6},{8,9},{9,8},{10,11... | collective-permute-start | bytes 4718600 | tf_op jit(solution)/shard_map/ppermute | solution.py:649
  196.3 34.5 %collective-permute-start.25 = (bf16[16,240,384]{2,1,0:T(8,128)(2,1)}, bf16[16,240,384]{2,1,0:T(8,128)(2,1)}, u32[]{:S(2)}, u32[]{:S(2)}) collective-permute-start(bf16[16,240,384]{2,1,0:T(8,128)(2,1)} %get-tuple-element.75), channel_id=1, source_target_pairs={{0,1},{1,0},{2,3},{3,2},{4,5},{5,4},{6,7},{7,6},{8,9},{9,8},{10,11... | collective-permute-start | bytes 8847368 | tf_op jit(solution)/shard_map/ppermute | solution.py:649
  202.9 5.1 %copy-start.4 = (bf16[512,768]{1,0:T(8,128)(2,1)S(1)}, bf16[512,768]{1,0:T(8,128)(2,1)}, u32[]{:S(2)}) copy-start(bf16[512,768]{1,0:T(8,128)(2,1)} %get-tuple-element.49) | copy-start | bytes 2359300
  202.9 5.9 %copy-start.5 = (bf16[512,768]{1,0:T(8,128)(2,1)S(1)}, bf16[512,768]{1,0:T(8,128)(2,1)}, u32[]{:S(2)}) copy-start(bf16[512,768]{1,0:T(8,128)(2,1)} %get-tuple-element.71) | copy-start | bytes 2359300
  204.0 12.3 %collective-permute-start.19 = (bf16[4,128,384]{2,1,0:T(8,128)(2,1)}, bf16[4,128,384]{2,1,0:T(8,128)(2,1)}, u32[]{:S(2)}, u32[]{:S(2)}) collective-permute-start(bf16[4,128,384]{2,1,0:T(8,128)(2,1)} %get-tuple-element.79), channel_id=1, source_target_pairs={{0,2},{1,3},{2,0},{3,1},{4,6},{5,7},{6,4},{7,5},{8,10},{9,11},{10,... | collective-permute-start | bytes 1179656 | tf_op jit(solution)/shard_map/ppermute | solution.py:649
  205.5 20.5 %collective-permute-start.21 = (bf16[4,128,384]{2,1,0:T(8,128)(2,1)}, bf16[4,128,384]{2,1,0:T(8,128)(2,1)}, u32[]{:S(2)}, u32[]{:S(2)}) collective-permute-start(bf16[4,128,384]{2,1,0:T(8,128)(2,1)} %get-tuple-element.80), channel_id=1, source_target_pairs={{0,6},{1,7},{2,4},{3,5},{4,2},{5,3},{6,0},{7,1},{8,14},{9,15},{10,... | collective-permute-start | bytes 1179656 | tf_op jit(solution)/shard_map/ppermute | solution.py:649
  207.5 19.6 %collective-permute-start.20 = (bf16[4,128,384]{2,1,0:T(8,128)(2,1)S(1)}, bf16[4,128,384]{2,1,0:T(8,128)(2,1)}, u32[]{:S(2)}, u32[]{:S(2)}) collective-permute-start(bf16[4,128,384]{2,1,0:T(8,128)(2,1)S(1)} %get-tuple-element.81), channel_id=1, source_target_pairs={{0,4},{1,5},{2,6},{3,7},{4,0},{5,1},{6,2},{7,3},{8,12},{9,13},{10,... | collective-permute-start | bytes 1179656 | tf_op jit(solution)/shard_map/ppermute | solution.py:649
  208.1 28.9 %collective-permute-start.13 = (bf16[256,768]{1,0:T(8,128)(2,1)S(1)}, bf16[256,768]{1,0:T(8,128)(2,1)S(1)}, u32[]{:S(2)}, u32[]{:S(2)}) collective-permute-start(bf16[256,768]{1,0:T(8,128)(2,1)S(1)} %get-tuple-element.84), channel_id=1, source_target_pairs={{0,0},{8,1},{2,2},{10,3},{4,4},{12,5},{6,6},{14,7},{16,8},{24,9},{... | collective-permute-start | bytes 1179656 | tf_op jit(solution)/shard_map/ppermute | solution.py:703
  208.8 24.0 %copy-start.1 = (bf16[16,240,384]{2,1,0:T(8,128)(2,1)S(1)}, bf16[16,240,384]{2,1,0:T(8,128)(2,1)}, u32[]{:S(2)}) copy-start(bf16[16,240,384]{2,1,0:T(8,128)(2,1)} %get-tuple-element.74) | copy-start | bytes 8847364
  216.3 21.4 %collective-permute-start.14 = (bf16[256,768]{1,0:T(8,128)(2,1)S(1)}, bf16[256,768]{1,0:T(8,128)(2,1)S(1)}, u32[]{:S(2)}, u32[]{:S(2)}) collective-permute-start(bf16[256,768]{1,0:T(8,128)(2,1)S(1)} %get-tuple-element.85), channel_id=1, source_target_pairs={{16,0},{24,1},{18,2},{26,3},{20,4},{28,5},{22,6},{30,7},{0,8},{8,9... | collective-permute-start | bytes 1179656 | tf_op jit(solution)/shard_map/ppermute | solution.py:706
  226.0 12.5 %collective-permute-start.16 = (bf16[256,768]{1,0:T(8,128)(2,1)S(1)}, bf16[256,768]{1,0:T(8,128)(2,1)S(1)}, u32[]{:S(2)}, u32[]{:S(2)}) collective-permute-start(bf16[256,768]{1,0:T(8,128)(2,1)S(1)} %get-tuple-element.82), channel_id=1, source_target_pairs={{0,0},{8,1},{2,2},{10,3},{4,4},{12,5},{6,6},{14,7},{16,8},{24,9},{... | collective-permute-start | bytes 1179656 | tf_op jit(solution)/shard_map/ppermute | solution.py:703
  227.1 23.0 %collective-permute-start.17 = (bf16[256,768]{1,0:T(8,128)(2,1)S(1)}, bf16[256,768]{1,0:T(8,128)(2,1)S(1)}, u32[]{:S(2)}, u32[]{:S(2)}) collective-permute-start(bf16[256,768]{1,0:T(8,128)(2,1)S(1)} %get-tuple-element.83), channel_id=1, source_target_pairs={{16,0},{24,1},{18,2},{26,3},{20,4},{28,5},{22,6},{30,7},{0,8},{8,9... | collective-permute-start | bytes 1179656 | tf_op jit(solution)/shard_map/ppermute | solution.py:706
  230.8 19.3 %collective-permute-start.22 = (bf16[128,384]{1,0:T(8,128)(2,1)S(1)}, bf16[128,384]{1,0:T(8,128)(2,1)S(1)}, u32[]{:S(2)}, u32[]{:S(2)}) collective-permute-start(bf16[128,384]{1,0:T(8,128)(2,1)S(1)} %get-tuple-element.93), channel_id=1, source_target_pairs={{0,8},{8,0},{16,24},{24,16},{1,9},{9,1},{17,25},{25,17},{2,10},{10... | collective-permute-start | bytes 294920 | tf_op jit(solution)/shard_map/ppermute | solution.py:649
  237.0 25.3 %collective-permute-start.26 = (bf16[4,240,384]{2,1,0:T(8,128)(2,1)}, bf16[4,240,384]{2,1,0:T(8,128)(2,1)}, u32[]{:S(2)}, u32[]{:S(2)}) collective-permute-start(bf16[4,240,384]{2,1,0:T(8,128)(2,1)} %get-tuple-element.76), channel_id=1, source_target_pairs={{0,2},{1,3},{2,0},{3,1},{4,6},{5,7},{6,4},{7,5},{8,10},{9,11},{10,... | collective-permute-start | bytes 2211848 | tf_op jit(solution)/shard_map/ppermute | solution.py:649
  237.7 31.9 %collective-permute-start.28 = (bf16[4,240,384]{2,1,0:T(8,128)(2,1)}, bf16[4,240,384]{2,1,0:T(8,128)(2,1)}, u32[]{:S(2)}, u32[]{:S(2)}) collective-permute-start(bf16[4,240,384]{2,1,0:T(8,128)(2,1)} %get-tuple-element.77), channel_id=1, source_target_pairs={{0,6},{1,7},{2,4},{3,5},{4,2},{5,3},{6,0},{7,1},{8,14},{9,15},{10,... | collective-permute-start | bytes 2211848 | tf_op jit(solution)/shard_map/ppermute | solution.py:649
  238.4 31.2 %collective-permute-start.27 = (bf16[4,240,384]{2,1,0:T(8,128)(2,1)}, bf16[4,240,384]{2,1,0:T(8,128)(2,1)}, u32[]{:S(2)}, u32[]{:S(2)}) collective-permute-start(bf16[4,240,384]{2,1,0:T(8,128)(2,1)} %get-tuple-element.78), channel_id=1, source_target_pairs={{0,4},{1,5},{2,6},{3,7},{4,0},{5,1},{6,2},{7,3},{8,12},{9,13},{10,... | collective-permute-start | bytes 2211848 | tf_op jit(solution)/shard_map/ppermute | solution.py:649
  250.1 7.1 %collective-permute-start.24 = (bf16[128,384]{1,0:T(8,128)(2,1)S(1)}, bf16[128,384]{1,0:T(8,128)(2,1)S(1)}, u32[]{:S(2)}, u32[]{:S(2)}) collective-permute-start(bf16[128,384]{1,0:T(8,128)(2,1)S(1)} %get-tuple-element.94), channel_id=1, source_target_pairs={{0,24},{8,16},{16,8},{24,0},{1,25},{9,17},{17,9},{25,1},{2,26},{10... | collective-permute-start | bytes 294920 | tf_op jit(solution)/shard_map/ppermute | solution.py:649
  250.1 10.2 %collective-permute-start.23 = (bf16[128,384]{1,0:T(8,128)(2,1)S(1)}, bf16[128,384]{1,0:T(8,128)(2,1)S(1)}, u32[]{:S(2)}, u32[]{:S(2)}) collective-permute-start(bf16[128,384]{1,0:T(8,128)(2,1)S(1)} %get-tuple-element.95), channel_id=1, source_target_pairs={{0,16},{8,24},{16,0},{24,8},{1,17},{9,25},{17,1},{25,9},{2,18},{10... | collective-permute-start | bytes 294920 | tf_op jit(solution)/shard_map/ppermute | solution.py:649
  271.6 9.7 %collective-permute-start.29 = (bf16[240,384]{1,0:T(8,128)(2,1)S(1)}, bf16[240,384]{1,0:T(8,128)(2,1)S(1)}, u32[]{:S(2)}, u32[]{:S(2)}) collective-permute-start(bf16[240,384]{1,0:T(8,128)(2,1)S(1)} %get-tuple-element.90), channel_id=1, source_target_pairs={{0,8},{8,0},{16,24},{24,16},{1,9},{9,1},{17,25},{25,17},{2,10},{10... | collective-permute-start | bytes 552968 | tf_op jit(solution)/shard_map/ppermute | solution.py:649
  276.6 12.9 %collective-permute-start.31 = (bf16[240,384]{1,0:T(8,128)(2,1)S(1)}, bf16[240,384]{1,0:T(8,128)(2,1)S(1)}, u32[]{:S(2)}, u32[]{:S(2)}) collective-permute-start(bf16[240,384]{1,0:T(8,128)(2,1)S(1)} %get-tuple-element.91), channel_id=1, source_target_pairs={{0,24},{8,16},{16,8},{24,0},{1,25},{9,17},{17,9},{25,1},{2,26},{10... | collective-permute-start | bytes 552968 | tf_op jit(solution)/shard_map/ppermute | solution.py:649
  280.6 16.9 %collective-permute-start.30 = (bf16[240,384]{1,0:T(8,128)(2,1)S(1)}, bf16[240,384]{1,0:T(8,128)(2,1)S(1)}, u32[]{:S(2)}, u32[]{:S(2)}) collective-permute-start(bf16[240,384]{1,0:T(8,128)(2,1)S(1)} %get-tuple-element.92), channel_id=1, source_target_pairs={{0,16},{8,24},{16,0},{24,8},{1,17},{9,25},{17,1},{25,9},{2,18},{10... | collective-permute-start | bytes 552968 | tf_op jit(solution)/shard_map/ppermute | solution.py:649
  (4 other events, 2.9 us)
Sparse Core Ops, SparseCore 0:
  10.9 86.6 all-gather.2
